TPU v7x, 128 devices: a whole 4x4x4 slice. The times are simulated.
128 devices in a mesh: dp: 4 (over x), dict: 32 (over y, z, core).
Axes of the slice: x: 4, y: 4, z: 4, core: 2. Of those that a mesh axis runs over, the one named last changes fastest.
Arguments:
- resid: bfloat16 [32768, 4096], P(('dp', 'dict')), may hold values from -6 to 6
- block_ids: int32 [32768, 2], P(('dp', 'dict')), may hold values from 0 to 127, all different within a row; in each aligned block of 256 rows (0 to 255, 256 to 511, ...) at most 8 rows name the same one
- enc_w: bfloat16 [8192, 4096], P('dict'), may hold values from -0.09375 to 0.09375
- enc_b: float32 [8192], P('dict'), may hold values from -3 to 3
- dec_w: bfloat16 [8192, 4096], P('dict'), may hold values from -0.5 to 0.5
- dec_b: float32 [4096], replicated, may hold values from -3 to 3
Outputs:
- recon: bfloat16 [32768, 4096], P(('dp', 'dict'))
- enc_grad: float32 [8192, 4096], P('dict', 'dp')
- dec_grad: float32 [8192, 4096], P('dict', 'dp')
Inputs may be any that keep to these rules, and one draw needn't show every extreme that they name: `block_ids`: each row names 2 different blocks. Within the rows of one device no block is named by more than 8 rows, and some block is named by exactly 8 of them.
All inputs are finite; a program needn't handle non-finite values.
Results may differ from a plain program's by a relative error of at most 0.012.
Values may be sent and summed in bfloat16 or wider, within the bound.
No kernel may reach another device: no remote copies, remote signals or barrier semaphores. Data moves between devices by JAX's collectives and lax.ppermute only.
A program may use at most 128 MiB of HBM per device.

v0:
```python
import jax
import jax.numpy as jnp
from jax import lax
from jax.sharding import PartitionSpec as P

LAT = 64


def body(resid, block_ids, enc_w, enc_b, dec_w, dec_b):
    tok_rows, width = resid.shape
    active = block_ids.shape[1]
    shards = lax.axis_size("dict")
    local_latents = enc_w.shape[0]
    blocks_here = local_latents // LAT
    all_blocks = blocks_here * shards
    capacity = 2 * tok_rows * active // all_blocks
    total_rows = tok_rows * lax.axis_size("dp") * shards
    scale = (all_blocks / (total_rows * active)) ** 0.5
    centered = (resid.astype(jnp.float32) - dec_b).astype(jnp.bfloat16)
    flat = block_ids.reshape(-1)
    onehot = (flat[:, None] == jnp.arange(all_blocks, dtype=jnp.int32)[None, :]).astype(jnp.int32)
    rank = jnp.sum(jnp.cumsum(onehot, axis=0) * onehot, axis=1) - 1
    slot = flat * capacity + rank
    source_row = jnp.arange(tok_rows * active, dtype=jnp.int32) // active
    outgoing = (
        jnp.zeros((all_blocks * capacity, width), jnp.bfloat16).at[slot].set(centered[source_row])
    )
    filled = jnp.zeros((all_blocks * capacity,), jnp.bfloat16).at[slot].set(1.0)
    arrived, present = (
        lax.all_to_all(
            outgoing.reshape(shards, blocks_here * capacity, width),
            "dict",
            split_axis=0,
            concat_axis=0,
            tiled=True,
        ),
        lax.all_to_all(
            filled.reshape(shards, blocks_here * capacity),
            "dict",
            split_axis=0,
            concat_axis=0,
            tiled=True,
        ),
    )
    arrived = arrived.reshape(shards, blocks_here, capacity, width)
    present = present.reshape(shards, blocks_here, capacity).astype(jnp.float32)
    enc_blocks = enc_w.reshape(blocks_here, LAT, width)
    dec_blocks = dec_w.reshape(blocks_here, LAT, width)
    bias_blocks = enc_b.reshape(blocks_here, LAT)
    pre = jnp.einsum("sjcd,jed->sjce", arrived, enc_blocks, preferred_element_type=jnp.float32)
    pre = pre + bias_blocks[None, :, None, :]
    acts = jnp.maximum(pre, 0.0).astype(jnp.bfloat16)
    parts = jnp.einsum(
        "sjce,jed->sjcd", acts, dec_blocks, preferred_element_type=jnp.float32
    ).astype(jnp.bfloat16)
    returned = lax.all_to_all(
        parts.reshape(shards, blocks_here * capacity, width),
        "dict",
        split_axis=0,
        concat_axis=0,
        tiled=True,
    )
    picked = returned.reshape(all_blocks * capacity, width)[slot].astype(jnp.float32)
    recon = (dec_b + jnp.sum(picked.reshape(tok_rows, active, width), axis=1)).astype(jnp.bfloat16)
    error = recon.astype(jnp.float32) - dec_b - centered.astype(jnp.float32)
    error_slots = (
        jnp.zeros((all_blocks * capacity, width), jnp.float32).at[slot].set(error[source_row])
    )
    received = lax.all_to_all(
        error_slots.reshape(shards, blocks_here * capacity, width).astype(jnp.bfloat16),
        "dict",
        split_axis=0,
        concat_axis=0,
        tiled=True,
    ).astype(jnp.float32)
    error_here = received.reshape(shards, blocks_here, capacity, width)
    scaled = error_here * (present[..., None] * scale)
    high = lax.Precision.HIGHEST
    rows_wide = arrived.astype(jnp.float32)
    dec_grad = jnp.einsum("sjce,sjcd->jed", acts.astype(jnp.float32), scaled, precision=high)
    gate = (pre > 0).astype(jnp.float32)
    grad_pre = (
        jnp.einsum("sjcd,jed->sjce", scaled, dec_blocks.astype(jnp.float32), precision=high) * gate
    )
    enc_grad = jnp.einsum("sjce,sjcd->jed", grad_pre, rows_wide, precision=high)
    enc_share, dec_share = (
        lax.psum_scatter(
            enc_grad.reshape(local_latents, width).astype(jnp.bfloat16),
            "dp",
            scatter_dimension=1,
            tiled=True,
        ).astype(jnp.float32),
        lax.psum_scatter(
            dec_grad.reshape(local_latents, width).astype(jnp.bfloat16),
            "dp",
            scatter_dimension=1,
            tiled=True,
        ).astype(jnp.float32),
    )
    return (recon, enc_share, dec_share)


def solution(mesh):
    placed = (
        P(("dp", "dict"), None),
        P(("dp", "dict"), None),
        P("dict", None),
        P("dict"),
        P("dict", None),
        P(),
    )
    return jax.shard_map(
        body,
        mesh=mesh,
        in_specs=placed,
        out_specs=(P(("dp", "dict"), None), P("dict", "dp"), P("dict", "dp")),
        check_vma=False,
    )
```

profile of v0, /device:TPU:1, one launch (start us, length us, event | category | flops | bytes accessed | tf_op | source)
XLA Modules:
  0.0 649.5 jit_solution(5916947025469275839)
XLA Ops:
  7.2 0.0 copy-start
  7.2 0.8 broadcast_multiply_fusion
  8.0 0.8 copy.37
  8.8 0.1 eq.29
  9.0 0.1 eq.25
  9.1 0.1 copy.36
  9.3 0.1 mul.48
  9.4 0.1 copy.39
  9.5 0.2 fusion.29
  9.9 0.2 fusion.26
  10.1 3.4 subtract_convert_fusion
  13.5 10.4 %gather_fusion = bf16[512,4096]{1,0:T(8,128)(2,1)} fusion(bf16[256,4096]{1,0:T(8,128)(2,1)} %subtract_convert_fusion, s32[1024]{0:T(1024)S(1)} %pad_clamp_fusion.1), kind=kCustom, calls=%fused_computation | custom fusion | bytes 8390656 | tf_op jit(solution)/shard_map/gather | solution.py:26
  23.9 12.9 %scatter_custom_fusion = bf16[1024,4096]{1,0:T(8,128)(2,1)} fusion(s32[512]{0:T(512)S(1)} %bitcast.75, bf16[512,4096]{1,0:T(8,128)(2,1)} %gather_fusion, bf16[]{:T(256)} %constant.16.clone.1), kind=kCustom, calls=%fused_computation.27 | custom fusion | bytes 8389120 | tf_op jit(solution)/shard_map/scatter | solution.py:26
  36.8 0.0 copy-start.2
  36.8 9.7 %all-to-all-start = ((bf16[32,32,4096]{2,1,0:T(8,128)(2,1)}), bf16[32,32,4096]{2,1,0:T(8,128)(2,1)}, u32[]{:S(2)}, u32[]{:S(2)}) async-start(bf16[32,32,4096]{2,1,0:T(8,128)(2,1)} %bitcast.69), calls=%async_computation | async-start | bytes 16777216 | tf_op jit(solution)/shard_map/all_to_all | solution.py:30
  46.5 0.1 add.80
  46.6 108.4 %all-to-all-done = bf16[32,32,4096]{2,1,0:T(8,128)(2,1)} async-done(((bf16[32,32,4096]{2,1,0:T(8,128)(2,1)}), bf16[32,32,4096]{2,1,0:T(8,128)(2,1)}, u32[]{:S(2)}, u32[]{:S(2)}) %all-to-all-start) | async-done | bytes 8388640 | tf_op jit(solution)/shard_map/all_to_all | solution.py:30
  155.0 6.3 fusion.20
  161.4 5.5 convert_bitcast_fusion
  166.9 7.7 %copy.77 = bf16[32,4,8,4096]{3,2,1,0:T(8,128)(2,1)} copy(bf16[32,4,8,4096]{3,2,0,1:T(8,128)(2,1)} %convert_bitcast_fusion) | data formatting | bytes 16777216 | tf_op jit(solution)/shard_map/convert_element_type | solution.py:55
  174.6 21.5 %all-to-all-start.1 = ((bf16[32,32,4096]{2,1,0:T(8,128)(2,1)}), bf16[32,32,4096]{2,1,0:T(8,128)(2,1)}, u32[]{:S(2)}, u32[]{:S(2)}) async-start(bf16[32,32,4096]{2,1,0:T(8,128)(2,1)} %bitcast.68), calls=%async_computation.1 | async-start | bytes 16777216 | tf_op jit(solution)/shard_map/all_to_all | solution.py:56
  196.1 3.8 scatter_custom_fusion.2
  199.9 0.7 all_to_all.20
  200.6 104.1 %all-to-all-done.1 = bf16[32,32,4096]{2,1,0:T(8,128)(2,1)} async-done(((bf16[32,32,4096]{2,1,0:T(8,128)(2,1)}), bf16[32,32,4096]{2,1,0:T(8,128)(2,1)}, u32[]{:S(2)}, u32[]{:S(2)}) %all-to-all-start.1) | async-done | bytes 8388640 | tf_op jit(solution)/shard_map/all_to_all | solution.py:56
  304.7 21.7 %all-to-all-start.3 = ((bf16[32,1,32]{2,1,0:T(2,128)(2,1)}), bf16[32,1,32]{2,1,0:T(2,128)(2,1)S(1)}, u32[]{:S(2)}, u32[]{:S(2)}) async-start(bf16[32,1,32]{2,1,0:T(2,128)(2,1)} %all_to_all.20), calls=%async_computation.3 | async-start | bytes 32768 | tf_op jit(solution)/shard_map/all_to_all | solution.py:37
  326.4 13.0 %gather_fusion.1 = bf16[512,4096]{1,0:T(8,128)(2,1)} fusion(bf16[1024,4096]{1,0:T(8,128)(2,1)} %bitcast.17, s32[1024]{0:T(1024)S(1)} %pad_clamp_fusion), kind=kCustom, calls=%fused_computation.1 | custom fusion | bytes 8390656 | tf_op jit(solution)/shard_map/gather | solution.py:63
  339.4 9.6 %reshape.161 = f32[256,2,4096]{2,1,0:T(2,128)} reshape(bf16[512,4096]{1,0:T(8,128)(2,1)} %gather_fusion.1) | data formatting | bytes 12582912 | tf_op jit(solution)/shard_map/convert_element_type | solution.py:63
  349.1 13.5 %reduce_sum.19 = f32[256,4096]{1,0:T(8,128)} reduce(f32[256,2,4096]{2,1,0:T(2,128)} %reshape.161, f32[]{:T(128)} %constant.39.clone.1), dimensions={1}, to_apply=%region_4.5 | reduce | flops 1048576 | bytes 12582916 | tf_op jit(solution)/shard_map/reduce_sum | solution.py:64
  362.6 6.4 convert_subtract_fusion
  369.0 11.2 %gather_fusion.2 = f32[512,4096]{1,0:T(8,128)} fusion(f32[256,4096]{1,0:T(8,128)} %get-tuple-element.3, s32[1024]{0:T(1024)S(1)} %pad_clamp_fusion.1), kind=kCustom, calls=%fused_computation.2 | custom fusion | bytes 16779264 | tf_op jit(solution)/shard_map/gather | solution.py:67
  380.2 14.8 %scatter_custom_fusion.1 = f32[1024,4096]{1,0:T(8,128)} fusion(s32[512]{0:T(512)S(1)} %bitcast.78, f32[512,4096]{1,0:T(8,128)} %gather_fusion.2, f32[]{:T(128)} %constant.39.clone.1), kind=kCustom, calls=%fused_computation.13 | custom fusion | bytes 16777728 | tf_op jit(solution)/shard_map/scatter | solution.py:67
  395.0 9.0 %convert_element_type.88 = bf16[1024,4096]{1,0:T(8,128)(2,1)} convert(f32[1024,4096]{1,0:T(8,128)} %scatter_custom_fusion.1) | non-fusion elementwise | flops 4194304 | bytes 25165824 | tf_op jit(solution)/shard_map/convert_element_type | solution.py:70
  404.0 0.0 all-to-all-done.3
  404.0 7.4 %all-to-all-start.2 = ((bf16[32,32,4096]{2,1,0:T(8,128)(2,1)}), bf16[32,32,4096]{2,1,0:T(8,128)(2,1)}, u32[]{:S(2)}, u32[]{:S(2)}) async-start(bf16[32,32,4096]{2,1,0:T(8,128)(2,1)} %bitcast.67), calls=%async_computation.2 | async-start | bytes 16777216 | tf_op jit(solution)/shard_map/all_to_all | solution.py:69
  411.4 0.0 reduce-scatter.3.cloned.1.call-start
  411.4 0.1 copy.44
  411.5 108.4 %all-to-all-done.2 = bf16[32,32,4096]{2,1,0:T(8,128)(2,1)} async-done(((bf16[32,32,4096]{2,1,0:T(8,128)(2,1)}), bf16[32,32,4096]{2,1,0:T(8,128)(2,1)}, u32[]{:S(2)}, u32[]{:S(2)}) %all-to-all-start.2) | async-done | bytes 8388640 | tf_op jit(solution)/shard_map/all_to_all | solution.py:69
  519.9 11.4 %bitcast_convert_fusion = f32[32,4,8,4096]{3,2,1,0:T(8,128)} fusion(bf16[32,32,4096]{2,1,0:T(8,128)(2,1)} %all-to-all-done.2), kind=kLoop, calls=%fused_computation.9 | loop fusion | flops 4194304 | bytes 25165824 | tf_op jit(solution)/shard_map/reshape | solution.py:76
  531.3 22.6 %fusion.1 = f32[4,32,8,64]{3,1,2,0:T(8,128)S(1)} fusion(bf16[4,64,4096,1]{2,1,3,0:T(8,128)(2,1)S(1)} %bitcast.66, f32[32,4,8,4096]{3,2,1,0:T(8,128)} %bitcast_convert_fusion, f32[32,4,8]{0,2,1:T(8,128)S(1)} %multiply_bitcast_fusion), kind=kOutput, calls=%fused_computation.8 | convolution fusion | flops 3225419776 | bytes 19140608 | tf_op jit(solution)/shard_map/sjcd,jed->sjce/dot_general | solution.py:83
  553.9 9.7 %fusion.15 = bf16[4,64,4096]{2,1,0:T(8,128)(2,1)} fusion(f32[4,32,8,64]{3,1,2,0:T(8,128)S(1)} %fusion.1, f32[4,32,8,64]{3,2,1,0:T(8,128)S(1)} %fusion.20, bf16[32,32,4096]{2,1,0:T(8,128)(2,1)} %all-to-all-done), kind=kOutput, calls=%fused_computation.23 | convolution fusion | flops 3222405120 | bytes 11010048 | tf_op jit(solution)/shard_map/sjce,sjcd->jed/dot_general | solution.py:85
  563.5 0.0 reduce-scatter.3.cloned.1.call-update
  563.5 0.0 reduce-scatter.5.cloned.1.call-start
  563.6 20.8 %fusion.14 = bf16[4,64,4096]{2,1,0:T(8,128)(2,1)} fusion(f32[32,4,8,4096]{3,2,1,0:T(8,128)} %bitcast_convert_fusion, f32[32,4,8]{0,2,1:T(8,128)S(1)} %multiply_bitcast_fusion, bf16[32,4,8,64]{3,2,0,1:T(8,128)(2,1)S(1)} %fusion.25), kind=kOutput, calls=%fused_computation.22 | convolution fusion | flops 3226468352 | bytes 19009536 | tf_op jit(solution)/shard_map/sjce,sjcd->jed/dot_general | solution.py:80
  584.4 0.0 reduce-scatter.5.cloned.1.call-update
  584.4 24.0 %reduce-scatter.3.cloned.1.call-done = bf16[256,1024]{1,0:T(8,128)(2,1)} async-done(((bf16[256,4096]{1,0:T(8,128)(2,1)}), bf16[256,1024]{1,0:T(8,128)(2,1)}) %reduce-scatter.3.cloned.1.call-update) | async-done | bytes 524304 | tf_op jit(solution)/shard_map/reduce_scatter | solution.py:87
  608.4 2.1 convert_element_type.93
  610.5 29.8 %reduce-scatter.5.cloned.1.call-done = bf16[256,1024]{1,0:T(8,128)(2,1)} async-done(((bf16[256,4096]{1,0:T(8,128)(2,1)}), bf16[256,1024]{1,0:T(8,128)(2,1)}) %reduce-scatter.5.cloned.1.call-update) | async-done | bytes 524304 | tf_op jit(solution)/shard_map/reduce_scatter | solution.py:93
  640.4 2.1 convert_element_type.96
  (18 shorter events, 0.2 us)
Async XLA Ops:
  7.2 154.2 %copy-start = (bf16[256,4096]{1,0:T(8,128)(2,1)S(1)}, bf16[256,4096]{1,0:T(8,128)(2,1)}, u32[]{:S(2)}) copy-start(bf16[256,4096]{1,0:T(8,128)(2,1)} %param.10) | copy-start | bytes 6291460
  36.8 9.7 %copy-start.2 = (f32[256]{0:T(256)S(1)}, f32[256]{0:T(256)}, u32[]{:S(2)}) copy-start(f32[256]{0:T(256)} %param.9) | copy-start | bytes 3076
  36.8 118.2 %all-to-all-start = ((bf16[32,32,4096]{2,1,0:T(8,128)(2,1)}), bf16[32,32,4096]{2,1,0:T(8,128)(2,1)}, u32[]{:S(2)}, u32[]{:S(2)}) async-start(bf16[32,32,4096]{2,1,0:T(8,128)(2,1)} %bitcast.69), calls=%async_computation | async-start | bytes 16777216 | tf_op jit(solution)/shard_map/all_to_all | solution.py:30
  174.6 130.0 %all-to-all-start.1 = ((bf16[32,32,4096]{2,1,0:T(8,128)(2,1)}), bf16[32,32,4096]{2,1,0:T(8,128)(2,1)}, u32[]{:S(2)}, u32[]{:S(2)}) async-start(bf16[32,32,4096]{2,1,0:T(8,128)(2,1)} %bitcast.68), calls=%async_computation.1 | async-start | bytes 16777216 | tf_op jit(solution)/shard_map/all_to_all | solution.py:56
  304.7 99.3 %all-to-all-start.3 = ((bf16[32,1,32]{2,1,0:T(2,128)(2,1)}), bf16[32,1,32]{2,1,0:T(2,128)(2,1)S(1)}, u32[]{:S(2)}, u32[]{:S(2)}) async-start(bf16[32,1,32]{2,1,0:T(2,128)(2,1)} %all_to_all.20), calls=%async_computation.3 | async-start | bytes 32768 | tf_op jit(solution)/shard_map/all_to_all | solution.py:37
  349.1 13.5 %copy-start.1 = (f32[4096]{0:T(1024)S(1)}, f32[4096]{0:T(1024)}, u32[]{:S(2)}) copy-start(f32[4096]{0:T(1024)} %param.11) | copy-start | bytes 49156
  404.0 116.0 %all-to-all-start.2 = ((bf16[32,32,4096]{2,1,0:T(8,128)(2,1)}), bf16[32,32,4096]{2,1,0:T(8,128)(2,1)}, u32[]{:S(2)}, u32[]{:S(2)}) async-start(bf16[32,32,4096]{2,1,0:T(8,128)(2,1)} %bitcast.67), calls=%async_computation.2 | async-start | bytes 16777216 | tf_op jit(solution)/shard_map/all_to_all | solution.py:69
  411.4 197.0 %reduce-scatter.3.cloned.1.call-start = ((), (), s32[]{:S(2)}) async-start(), calls=%async_computation.6 | async-start | bytes 2621440 | tf_op jit(solution)/shard_map/reduce_scatter | solution.py:87
  563.5 76.8 %reduce-scatter.5.cloned.1.call-start = ((), (), s32[]{:S(2)}) async-start(), calls=%async_computation.7 | async-start | bytes 2621440 | tf_op jit(solution)/shard_map/reduce_scatter | solution.py:93
Sparse Core Ops, SparseCore 0:
  563.7 44.7 reduce-scatter.2
  611.0 29.3 reduce-scatter.4
where the time goes:
time: 661 us; the launch traced here: 650 us
  waiting for transfers between devices  375 us (57%)
  local copies, waits for them, and re-layouts  85.8 us (13%)
  matrix products  64.9 us (10%)
  starting transfers between devices  60.4 us (9%)
  other arithmetic  49.3 us (7%)
  between operations  14.4 us (2%)
    all_to_all x1, waiting for transfers between devices, body(): lax.all_to_all(outgoing.reshape(shards, blocks_here * capacity, width), '...  108 us
    all_to_all x1, waiting for transfers between devices, body(): lax.all_to_all(error_slots.reshape(shards, blocks_here * capacity, width)...  108 us
    all_to_all x1, waiting for transfers between devices, body(): lax.all_to_all(parts.reshape(shards, blocks_here * capacity, width), 'dic...  104 us
    reduce_scatter x1, waiting for transfers between devices, body(): lax.psum_scatter(dec_grad.reshape(local_latents, width).astype(jnp.bfloat...  29.8 us
    reduce_scatter x1, waiting for transfers between devices, body(): lax.psum_scatter(enc_grad.reshape(local_latents, width).astype(jnp.bfloat...  24 us
    dot_general x1, matrix products, body(): jnp.einsum('sjcd,jed->sjce', scaled, dec_blocks.astype(jnp.float32), prec...  22.6 us
    all_to_all x1, starting transfers between devices, body(): lax.all_to_all(filled.reshape(shards, blocks_here * capacity), 'dict', sp...  21.7 us
    all_to_all x1, starting transfers between devices, body(): lax.all_to_all(parts.reshape(shards, blocks_here * capacity, width), 'dic...  21.5 us
  transfers between devices with their start and end apart: 6, of which 5 were waited for; matrix products, arithmetic and copies ran while one was open for 16% of the time, Pallas kernels for 0%

commit v1 on v0

v1 whole, which is shorter than its diff:
```python
import jax
import jax.numpy as jnp
from jax import lax
from jax.experimental import pallas as pl
from jax.experimental.pallas import tpu as pltpu
from jax.sharding import PartitionSpec as P

LAT = 64
CAP = 8
BF = jnp.bfloat16
F32 = jnp.float32
VMEM_LIMIT = 56 * 1024 * 1024


def params(**more):
    return pltpu.CompilerParams(vmem_limit_bytes=VMEM_LIMIT, **more)


def dot(a, b):
    return jnp.dot(a, b, preferred_element_type=F32)


def dot_tn(a, b):
    return lax.dot_general(a, b, (((0,), (0,)), ((), ())), preferred_element_type=F32)


def dot_nt(a, b):
    return lax.dot_general(a, b, (((1,), (1,)), ((), ())), preferred_element_type=F32)


def iota(shape, axis):
    return lax.broadcasted_iota(jnp.int32, shape, axis)


def ranks(ids, blocks):
    rows = ids.shape[1]
    block = iota((blocks, rows), 0)
    one0 = (block == ids[0:1, :]).astype(F32)
    one1 = (block == ids[1:2, :]).astype(F32)
    before = (iota((rows, rows), 0) < iota((rows, rows), 1)).astype(BF)
    pre0 = dot(one0.astype(BF), before)
    pre1 = dot(one1.astype(BF), before) + jnp.sum(one0, axis=1, keepdims=True)
    rank0 = jnp.sum(one0 * pre0, axis=0, keepdims=True).astype(jnp.int32)
    rank1 = jnp.sum(one1 * pre1, axis=0, keepdims=True).astype(jnp.int32)
    return rank0, rank1


def route_kernel(ids_ref, resid_ref, bias_ref, out_ref, table_ref, pick_ref):
    slots, rows = pick_ref.shape

    @pl.when(pl.program_id(0) == 0)
    def _():
        ids = ids_ref[...]
        rank0, rank1 = ranks(ids, slots // CAP)
        slot = iota((slots, rows), 0)
        is0 = slot == ids[0:1, :] * CAP + rank0
        is1 = slot == ids[1:2, :] * CAP + rank1
        pick_ref[...] = jnp.where(is0 | is1, 1.0, 0.0).astype(BF)
        other = jnp.where(is0, ids[1:2, :] + 1, 0) + jnp.where(is1, ids[0:1, :] + 1, 0)
        table_ref[...] = jnp.sum(other.astype(F32), axis=1, keepdims=True).astype(jnp.int32) - 1

    centered = (resid_ref[...].astype(F32) - bias_ref[...]).astype(BF)
    step = 256
    for at in range(0, slots, step):
        out_ref[0, at : at + step, :] = dot(pick_ref[at : at + step, :], centered).astype(BF)


def route(ids, resid, dec_b, parts, slots):
    rows, width = resid.shape
    cols = width // parts
    return pl.pallas_call(
        route_kernel,
        grid=(parts,),
        in_specs=[
            pl.BlockSpec(ids.shape, lambda i: (0, 0)),
            pl.BlockSpec((rows, cols), lambda i: (0, i)),
            pl.BlockSpec((1, cols), lambda i: (0, i)),
        ],
        out_specs=[
            pl.BlockSpec((1, slots, cols), lambda i: (i, 0, 0)),
            pl.BlockSpec((slots, 1), lambda i: (0, 0)),
        ],
        out_shape=[
            jax.ShapeDtypeStruct((parts, slots, cols), BF),
            jax.ShapeDtypeStruct((slots, 1), jnp.int32),
        ],
        scratch_shapes=[pltpu.VMEM((slots, rows), BF)],
        compiler_params=params(),
        name="route_rows",
    )(ids, resid, dec_b.reshape(1, width))


def encode_kernel(rows_ref, weight_ref, bias_ref, pre_ref, proj_ref):
    count, _, cols = rows_ref.shape
    low = iota((1, 1, 128), 2) < LAT
    for p in range(2):
        rows = rows_ref[:, p * 16 : (p + 1) * 16, :].reshape(count * 16, cols)
        both = dot_nt(rows, weight_ref[p]).reshape(count, 2, CAP, 256)
        pre = jnp.where(low, both[:, 0, :, :128], both[:, 1, :, :128])
        pre_ref[:, p * CAP : (p + 1) * CAP, :] = pre + bias_ref[p : p + 1, :][None]
        proj = jnp.where(low, both[:, 0, :, 128:], both[:, 1, :, 128:])
        proj_ref[:, p * CAP : (p + 1) * CAP, :] = proj


def encode(arrived, weights, bias):
    sources, here, cols = arrived.shape
    step = 32
    shape = jax.ShapeDtypeStruct((sources, 2 * CAP, 128), F32)
    return pl.pallas_call(
        encode_kernel,
        grid=(sources // step,),
        in_specs=[
            pl.BlockSpec((step, here, cols), lambda i: (i, 0, 0)),
            pl.BlockSpec(weights.shape, lambda i: (0, 0, 0)),
            pl.BlockSpec(bias.shape, lambda i: (0, 0)),
        ],
        out_specs=[pl.BlockSpec((step, 2 * CAP, 128), lambda i: (i, 0, 0))] * 2,
        out_shape=[shape, shape],
        compiler_params=params(),
        name="encode_rows",
    )(arrived, weights, bias)


def activate_kernel(ids_ref, pre_ref, rows_ref, msg_ref):
    packed = pre_ref.shape[1]
    rows = ids_ref.shape[1]
    slots = 2 * packed
    ids = ids_ref[...]
    rank0, rank1 = ranks(ids, slots // CAP)
    total = pre_ref[0] + pre_ref[1] + pre_ref[2] + pre_ref[3]
    acts = jnp.maximum(total, 0.0).astype(BF)
    slot = iota((slots, rows), 0)
    found = []
    for k, rank in ((0, rank0), (1, rank1)):
        block = ids[k : k + 1, :]
        half = block % 2
        at = (block // 2) * CAP + rank
        here = jnp.where(slot == half * packed + at, 1.0, 0.0).astype(BF)
        found.append(dot_tn(here[:packed], acts)[:, :LAT] + dot_tn(here[packed:], acts)[:, LAT:])
    first, second = found
    straight = jnp.concatenate([first, second], axis=1).astype(BF)
    crossed = jnp.concatenate([second, first], axis=1).astype(BF)
    rows_ref[...] = straight
    pick0 = jnp.where(slot == ids[0:1, :] * CAP + rank0, 1.0, 0.0).astype(BF)
    pick1 = jnp.where(slot == ids[1:2, :] * CAP + rank1, 1.0, 0.0).astype(BF)
    msg = (dot(pick0, straight) + dot(pick1, crossed)).astype(BF)
    for copy in range(msg_ref.shape[0]):
        msg_ref[copy] = msg


def activate(ids, partial):
    parts, packed, lanes = partial.shape
    rows = ids.shape[1]
    return pl.pallas_call(
        activate_kernel,
        out_shape=[
            jax.ShapeDtypeStruct((rows, lanes), BF),
            jax.ShapeDtypeStruct((parts, 2 * packed, lanes), BF),
        ],
        compiler_params=params(),
        name="activate_rows",
    )(ids, partial)


def doubled(pair):
    source, target = iota((128, 256), 0), iota((128, 256), 1)
    copy = source == (target // 128) * LAT + target % LAT
    return dot(pair, jnp.where(copy, 1.0, 0.0).astype(BF)).astype(BF)


def lane_block(group):
    return (iota((1, 128), 1) // LAT + group * 2).astype(F32).astype(BF)


def own_expanded(own):
    count = own.shape[0]
    twice = jnp.concatenate([own, own], axis=1)
    mine = (iota((count, 256), 0) // CAP) % 4 == iota((count, 256), 1) // LAT
    return jnp.where(mine, twice.astype(F32), 0.0).astype(BF)


def recon_kernel(acts_ref, ids_ref, dec_ref, bias_ref, out_ref, twice_ref, name0_ref, name1_ref, acc_ref):
    at = pl.program_id(0)
    rows = acts_ref.shape[0]
    chunk = dec_ref.shape[0]

    @pl.when(at == 0)
    def _():
        twice_ref[...] = doubled(acts_ref[...])
        ids = ids_ref[...].astype(F32)
        name0_ref[...] = jnp.broadcast_to(ids[:, 0:1], (rows, 128)).astype(BF)
        name1_ref[...] = jnp.broadcast_to(ids[:, 1:2], (rows, 128)).astype(BF)
        acc_ref[...] = jnp.broadcast_to(bias_ref[...], acc_ref.shape)

    spread = []
    zero = jnp.zeros((rows, 128), BF)
    for q in range(chunk // 128):
        block = lane_block(at * (chunk // 128) + q)
        one = jnp.where(name0_ref[...] == block, twice_ref[:, :128], zero)
        spread.append(jnp.where(name1_ref[...] == block, twice_ref[:, 128:], one))
    acc_ref[...] += dot(jnp.concatenate(spread, axis=1), dec_ref[...])

    @pl.when(at == pl.num_programs(0) - 1)
    def _():
        out_ref[...] = acc_ref[...].astype(BF)


def reconstruct(acts, ids, dec_all, bias):
    rows = acts.shape[0]
    latents, cols = dec_all.shape
    chunk = 1024
    return pl.pallas_call(
        recon_kernel,
        grid=(latents // chunk,),
        in_specs=[
            pl.BlockSpec(acts.shape, lambda i: (0, 0)),
            pl.BlockSpec(ids.shape, lambda i: (0, 0)),
            pl.BlockSpec((chunk, cols), lambda i: (i, 0)),
            pl.BlockSpec((1, cols), lambda i: (0, 0)),
        ],
        out_specs=pl.BlockSpec((rows, cols), lambda i: (0, 0)),
        out_shape=jax.ShapeDtypeStruct((rows, cols), BF),
        scratch_shapes=[
            pltpu.VMEM((rows, 256), BF),
            pltpu.VMEM((rows, 128), BF),
            pltpu.VMEM((rows, 128), BF),
            pltpu.VMEM((rows, cols), F32),
        ],
        compiler_params=params(),
        name="reconstruct_rows",
    )(acts, ids, dec_all, bias)


def gate_kernel(scale, msg_ref, other_ref, gram_ref, own_gram_ref, proj_ref, out_ref):
    count = msg_ref.shape[0]
    twice = doubled(msg_ref[...])
    names = jnp.broadcast_to(other_ref[...].astype(F32), (count, 128)).astype(BF)
    zero = jnp.zeros((count, 128), BF)
    total = dot(own_expanded(twice[:, :128]), own_gram_ref[...])
    chunk = 1024
    for at in range(0, gram_ref.shape[0], chunk):
        spread = [
            jnp.where(names == lane_block(group), twice[:, 128:], zero)
            for group in range(at // 128, (at + chunk) // 128)
        ]
        total = total + dot(jnp.concatenate(spread, axis=1), gram_ref[at : at + chunk, :])
    total = total.reshape(count // 32, 4, CAP, 256)
    low = iota((1, 1, 128), 2) < LAT
    packed = []
    for p in range(2):
        lanes = slice(p * 128, (p + 1) * 128)
        packed.append(jnp.where(low, total[:, 2 * p, :, lanes], total[:, 2 * p + 1, :, lanes]))
    out_ref[...] = ((jnp.concatenate(packed, axis=1) - proj_ref[...]) * scale).astype(BF)


def gate_partial(scale, msg, other, gram, own_gram, proj):
    count, lanes = msg.shape
    step = 512
    return pl.pallas_call(
        lambda *refs: gate_kernel(scale, *refs),
        grid=(count // step,),
        in_specs=[
            pl.BlockSpec((step, lanes), lambda i: (i, 0)),
            pl.BlockSpec((step, 1), lambda i: (i, 0)),
            pl.BlockSpec(gram.shape, lambda i: (0, 0)),
            pl.BlockSpec(own_gram.shape, lambda i: (0, 0)),
            pl.BlockSpec((step // 32, 2 * CAP, 128), lambda i: (i, 0, 0)),
        ],
        out_specs=pl.BlockSpec((step // 32, 2 * CAP, 128), lambda i: (i, 0, 0)),
        out_shape=jax.ShapeDtypeStruct(proj.shape, BF),
        compiler_params=params(),
        name="gate_partial",
    )(msg, other, gram, own_gram, proj)


def mix_kernel(msg_ref, other_ref, dec_ref, own_dec_ref, out_ref, own_ref, twice_ref, name_ref):
    at = pl.program_id(0)
    count = msg_ref.shape[0]
    chunk = dec_ref.shape[0]

    @pl.when(at == 0)
    def _():
        twice = doubled(msg_ref[...])
        twice_ref[...] = twice[:, 128:]
        name_ref[...] = jnp.broadcast_to(other_ref[...].astype(F32), (count, 128)).astype(BF)
        own = own_expanded(twice[:, :128])
        own_ref[...] = own.T
        out_ref[...] = dot(dot(own_ref[...], own).astype(BF), own_dec_ref[...])

    zero = jnp.zeros((count, 128), BF)
    spread = []
    for q in range(chunk // 128):
        block = lane_block(at * (chunk // 128) + q)
        spread.append(jnp.where(name_ref[...] == block, twice_ref[...], zero))
    mixed = dot(own_ref[...], jnp.concatenate(spread, axis=1)).astype(BF)
    out_ref[...] += dot(mixed, dec_ref[...])


def mix(msg, other, dec_all, own_dec):
    count, lanes = msg.shape
    latents, cols = dec_all.shape
    chunk = 512
    return pl.pallas_call(
        mix_kernel,
        grid=(latents // chunk,),
        in_specs=[
            pl.BlockSpec(msg.shape, lambda i: (0, 0)),
            pl.BlockSpec(other.shape, lambda i: (0, 0)),
            pl.BlockSpec((chunk, cols), lambda i: (i, 0)),
            pl.BlockSpec(own_dec.shape, lambda i: (0, 0)),
        ],
        out_specs=pl.BlockSpec(own_dec.shape, lambda i: (0, 0)),
        out_shape=jax.ShapeDtypeStruct(own_dec.shape, F32),
        scratch_shapes=[
            pltpu.VMEM((256, count), BF),
            pltpu.VMEM((count, 128), BF),
            pltpu.VMEM((count, 128), BF),
        ],
        compiler_params=params(),
        name="mix_decoder",
    )(msg, other, dec_all, own_dec)


def grads_kernel(scale, gate_ref, msg_ref, rows_ref, mixed_ref, enc_ref, dec_ref, acc_ref):
    at = pl.program_id(0)
    count = msg_ref.shape[0]
    sources = count // 32
    own = own_expanded(doubled(msg_ref[...])[:, :128])
    total = gate_ref[0].astype(F32)
    for part in range(1, gate_ref.shape[0]):
        total = total + gate_ref[part].astype(F32)
    low = iota((1, 1, 128), 2) < LAT
    zero = jnp.zeros((sources, CAP, 128), F32)
    spread = []
    for p in range(2):
        piece = total[:, p * CAP : (p + 1) * CAP, :]
        for even in (True, False):
            kept = jnp.where(low if even else ~low, piece, 0.0)
            pair = [kept, zero] if p == 0 else [zero, kept]
            spread.append(jnp.concatenate(pair, axis=2))
    wide = jnp.concatenate(spread, axis=1).reshape(count, 256)
    wide = jnp.where(own.astype(F32) > 0, wide, 0.0).astype(BF)

    @pl.when(at == 0)
    def _():
        acc_ref[...] = jnp.zeros_like(acc_ref)

    acc_ref[...] += dot_tn(jnp.concatenate([wide, own], axis=1), rows_ref[...])

    @pl.when(at == pl.num_programs(0) - 1)
    def _():
        enc_ref[...] = acc_ref[:256, :]
        dec_ref[...] = (mixed_ref[...] - acc_ref[256:, :]) * scale


def grads(scale, gates, msg, rows, mixed):
    count, lanes = msg.shape
    cols = rows.shape[1]
    step = 512
    shape = jax.ShapeDtypeStruct(mixed.shape, F32)
    return pl.pallas_call(
        lambda *refs: grads_kernel(scale, *refs),
        grid=(count // step,),
        in_specs=[
            pl.BlockSpec((gates.shape[0], step // 32, 2 * CAP, 128), lambda i: (0, i, 0, 0)),
            pl.BlockSpec((step, lanes), lambda i: (i, 0)),
            pl.BlockSpec((step, cols), lambda i: (i, 0)),
            pl.BlockSpec(mixed.shape, lambda i: (0, 0)),
        ],
        out_specs=[pl.BlockSpec(mixed.shape, lambda i: (0, 0))] * 2,
        out_shape=[shape, shape],
        scratch_shapes=[pltpu.VMEM((512, cols), F32)],
        compiler_params=params(),
        name="dictionary_grads",
    )(gates, msg, rows, mixed)


def body(resid, block_ids, enc_w, enc_b, dec_w, dec_b):
    tok_rows, width = resid.shape
    parts = lax.axis_size("dp")
    shards = lax.axis_size("dict")
    local = enc_w.shape[0]
    here = local // LAT
    slots = here * shards * CAP
    cols = width // parts
    everyone = ("dp", "dict")
    devices = parts * shards
    blocks = here * shards
    scale = (blocks / (tok_rows * devices * block_ids.shape[1])) ** 0.5
    at_x = lax.axis_index("dp")
    at_dict = lax.axis_index("dict")

    ids = block_ids.T
    outgoing, table = route(ids, resid, dec_b, parts, slots)
    arrived = lax.all_to_all(
        outgoing.reshape(devices, here * CAP, cols), everyone, 0, 0, tiled=True
    )

    enc_x = lax.dynamic_slice(enc_w, (0, at_x * cols), (local, cols))
    dec_x = lax.dynamic_slice(dec_w, (0, at_x * cols), (local, cols))
    bias_x = lax.dynamic_slice(dec_b, (at_x * cols,), (cols,)).reshape(1, cols)
    dec_all = lax.all_gather(dec_x, "dict", axis=0, tiled=True)
    gram = dot_nt(dec_all, dec_x).astype(BF)
    own_gram = lax.dynamic_slice(gram, (at_dict * local, 0), (local, local))
    group_ids = lax.all_gather(block_ids, "dp", axis=0, tiled=True)
    tables = lax.all_gather(table.reshape(shards, here * CAP), everyone, axis=0, tiled=False)
    other = lax.dynamic_slice(tables, (0, at_dict, 0), (devices, 1, here * CAP))
    other = other.reshape(devices * here * CAP, 1)

    weights = jnp.concatenate(
        [enc_x.reshape(2, 2 * LAT, cols), dec_x.reshape(2, 2 * LAT, cols)], axis=1
    )
    bias = jnp.where(at_x == 0, enc_b, 0.0).reshape(2, 2 * LAT)
    pre, proj = encode(arrived, weights, bias)
    partial = lax.all_to_all(pre, everyone, 0, 0, tiled=True)
    acts, msg = activate(ids, partial.reshape(parts, shards * 2 * CAP, 128))
    message = lax.all_to_all(
        msg.reshape(devices, here * CAP, 128), everyone, 0, 0, tiled=True
    ).reshape(devices * here * CAP, 128)
    group_acts = lax.all_gather(acts, "dp", axis=0, tiled=True)

    recon_x = reconstruct(group_acts, group_ids, dec_all, bias_x)
    recon = lax.all_to_all(recon_x, "dp", 0, 1, tiled=True)

    gate = gate_partial(scale, message, other, gram, own_gram, proj)
    gates = lax.all_gather(gate, "dp", axis=0, tiled=False)
    mixed = mix(message, other, dec_all, dec_x)
    enc_grad, dec_grad = grads(
        scale, gates, message, arrived.reshape(devices * here * CAP, cols), mixed
    )
    return (recon, enc_grad, dec_grad)


def solution(mesh):
    placed = (
        P(("dp", "dict"), None),
        P(("dp", "dict"), None),
        P("dict", None),
        P("dict"),
        P("dict", None),
        P(),
    )
    return jax.shard_map(
        body,
        mesh=mesh,
        in_specs=placed,
        out_specs=(P(("dp", "dict"), None), P("dict", "dp"), P("dict", "dp")),
        check_vma=False,
    )
```

time: 661 us -> 369 us (0.56)
  waiting for transfers between devices: 375 us -> 110 us
  Pallas kernels: 0 us -> 109 us
  blocking collectives: 0 us -> 72.7 us
  local copies, waits for them, and re-layouts: 85.8 us -> 14.8 us
  matrix products: 64.9 us -> 10.3 us
  other arithmetic: 49.3 us -> 1.82 us
  starting transfers between devices: 60.4 us -> 30.4 us
    all_to_all x4, waiting for transfers between devices: 321 us -> 110 us  [the longest x1 104 us: body(): lax.all_to_all(outgoing.reshape(devices, here * CAP, cols), everyone, 0,...]
    pallas_call x0 -> x7, Pallas kernels: none -> 109 us  [the longest x1 31.5 us: mix(): pl.pallas_call(mix_kernel, grid=(latents // chunk,), in_specs=[pl.BlockSp...]
    all_gather x0 -> x3, blocking collectives: none -> 72.7 us  [the longest x1 48.3 us: body(): lax.all_gather(table.reshape(shards, here * CAP), everyone, axis=0, tiled...]
    dot_general x5 -> x1, matrix products: 64.9 us -> 10.3 us  [dot_nt(): lax.dot_general(a, b, (((1,), (1,)), ((), ())), preferred_element_type=F32)]
    reduce_scatter x2 -> x0, waiting for transfers between devices: 53.8 us -> none  [the longest x1 29.8 us: body(): lax.psum_scatter(dec_grad.reshape(local_latents, width).astype(jnp.bfloat...]
    gather x3 -> x0, local copies, waits for them, and re-layouts: 34.6 us -> none  [the longest x1 13 us: body(): returned.reshape(all_blocks * capacity, width)[slot].astype(jnp.float32)]
    scatter x3 -> x0, local copies, waits for them, and re-layouts: 31.4 us -> none  [the longest x1 14.8 us: body(): jnp.zeros((all_blocks * capacity, width), jnp.float32).at[slot]]
    all_to_all x4, starting transfers between devices: 60.3 us -> 30.1 us  [the longest x1 12 us: body(): lax.all_to_all(outgoing.reshape(devices, here * CAP, cols), everyone, 0,...]
  transfers between devices with their start and end apart: 6 -> 6, of which waited for: 5 -> 2; matrix products, arithmetic and copies ran while one was open for 16% -> 6% of each run, Pallas kernels for 0% -> 20%
where the time goes in v1:
time: 369 us; the launch traced here: 363 us
  waiting for transfers between devices  110 us (30%)
  Pallas kernels  109 us (30%)
  blocking collectives  72.7 us (20%)
  starting transfers between devices  30.4 us (8%)
  local copies, waits for them, and re-layouts  14.8 us (4%)
  between operations  14.2 us (4%)
  matrix products  10.3 us (3%)
    all_to_all x1, waiting for transfers between devices, body(): lax.all_to_all(outgoing.reshape(devices, here * CAP, cols), everyone, 0,...  104 us
    all_gather x1, blocking collectives, body(): lax.all_gather(table.reshape(shards, here * CAP), everyone, axis=0, tiled...  48.3 us
    pallas_call x1, Pallas kernels, mix(): pl.pallas_call(mix_kernel, grid=(latents // chunk,), in_specs=[pl.BlockSp...  31.5 us
    pallas_call x1, Pallas kernels, gate_partial(): pl.pallas_call(lambda *refs: gate_kernel(scale, *refs), grid=(count // st...  23.8 us
    pallas_call x1, Pallas kernels, reconstruct(): pl.pallas_call(recon_kernel, grid=(latents // chunk,), in_specs=[pl.Block...  22.7 us
    pallas_call x1, Pallas kernels, grads(): pl.pallas_call(lambda *refs: grads_kernel(scale, *refs), grid=(count // s...  12.7 us
    all_gather x1, blocking collectives, body(): group_ids = lax.all_gather(block_ids, 'dp', axis=0, tiled=True)  12.4 us
    all_gather x1, blocking collectives, body(): group_acts = lax.all_gather(acts, 'dp', axis=0, tiled=True)  12 us
  transfers between devices with their start and end apart: 6, of which 2 were waited for; matrix products, arithmetic and copies ran while one was open for 6% of the time, Pallas kernels for 20%

profile of v1, /device:TPU:1, one launch (start us, length us, event | category | flops | bytes accessed | tf_op | source)
XLA Modules:
  0.0 363.0 jit_solution(8290306913523034738)
XLA Ops:
  7.2 0.0 copy-start
  7.2 0.0 all-gather.4.cloned.1.call-start
  7.2 1.5 copy-done
  8.8 0.8 constant_dynamic-slice_fusion.1.own_dec_ref
  9.6 0.0 all-gather.4.cloned.1.call-update
  9.6 7.1 %route_rows.1 = (bf16[4,1024,1024]{2,1,0:T(8,128)(2,1)}, s32[1024,1]{1,0:T(8,128)}) custom-call(s32[2,256]{1,0:T(2,128)} %bitcast.32, bf16[256,4096]{1,0:T(8,128)(2,1)} %resid_ref.1, f32[1,4096]{1,0:T(1,128)} %bitcast.31), custom_call_target="tpu_custom_call" | custom-call | tf_op jit(solution)/shard_map/route_rows/pallas_call | solution.py:71
  16.8 12.0 %all-to-all-start = ((bf16[128,32,1024]{2,1,0:T(8,128)(2,1)}), bf16[128,32,1024]{2,1,0:T(8,128)(2,1)}, u32[]{:S(2)}, u32[]{:S(2)}) async-start(bf16[128,32,1024]{2,1,0:T(8,128)(2,1)} %bitcast.22), calls=%async_computation | async-start | bytes 16777216 | tf_op jit(solution)/shard_map/all_to_all | solution.py:395
  28.7 0.0 copy-start.9
  28.7 1.1 constant_dynamic-slice_fusion.2
  29.8 0.0 copy-done.3
  29.8 1.0 pad_maximum_fusion.weight_ref
  30.9 0.0 copy-done.9
  30.9 0.6 select_bitcast_fusion.bias_ref
  31.5 103.7 %all-to-all-done.rows_ref = bf16[128,32,1024]{2,1,0:T(8,128)(2,1)} async-done(((bf16[128,32,1024]{2,1,0:T(8,128)(2,1)}), bf16[128,32,1024]{2,1,0:T(8,128)(2,1)}, u32[]{:S(2)}, u32[]{:S(2)}) %all-to-all-start) | async-done | bytes 8388640 | tf_op jit(solution)/shard_map/all_to_all | solution.py:395
  135.2 7.5 %encode_rows.1 = (f32[128,16,128]{2,1,0:T(8,128)}, f32[128,16,128]{2,1,0:T(8,128)}) custom-call(bf16[128,32,1024]{2,1,0:T(8,128)(2,1)} %all-to-all-done.rows_ref, bf16[2,256,1024]{2,1,0:T(8,128)(2,1)} %pad_maximum_fusion.weight_ref, f32[2,128]{1,0:T(2,128)} %select_bitcast_fusion.bias_ref), custom_call_target="tpu_custom_call" | custom-call | tf_op jit(solution)/shard_map/encode_rows/pallas_call | solution.py:109
  142.6 9.1 %all-to-all-start.1 = ((f32[128,16,128]{2,1,0:T(8,128)}), f32[128,16,128]{2,1,0:T(8,128)S(1)}, u32[]{:S(2)}, u32[]{:S(2)}) async-start(f32[128,16,128]{2,1,0:T(8,128)} %get-tuple-element.12), calls=%async_computation.1 | async-start | bytes 2097152 | tf_op jit(solution)/shard_map/all_to_all | solution.py:415
  151.7 0.0 copy-done.6
  151.7 0.2 reduce
  151.9 0.1 all_gather_reshape.3
  152.0 48.3 %all_gather.21 = s32[128,32,32]{2,1,0:T(8,128)S(1)} all-gather(s32[1,32,32]{2,1,0:T(8,128)S(1)} %all_gather_reshape.3), channel_id=1, replica_groups=mesh['dp'=4,'dict'=32] {'dp','dict'}, dimensions={0}, use_global_device_ids=true | all-gather | bytes 528384 | tf_op jit(solution)/shard_map/all_gather | solution.py:406
  200.3 0.2 dynamic-slice_reduce_fusion
  200.5 3.5 reshape.54.refs_1_.other_ref
  204.0 0.0 all-to-all-done.1
  204.0 1.0 copy-done.5
  204.9 3.6 activate_rows.1
  208.5 5.3 %all-to-all-start.3 = ((bf16[128,32,128]{2,1,0:T(8,128)(2,1)}), bf16[128,32,128]{2,1,0:T(8,128)(2,1)S(1)}, u32[]{:S(2)}, u32[]{:S(2)}) async-start(bf16[128,32,128]{2,1,0:T(8,128)(2,1)} %bitcast.30), calls=%async_computation.3 | async-start | bytes 2097152 | tf_op jit(solution)/shard_map/all_to_all | solution.py:417
  213.8 0.2 all-gather.6.cloned.1.call-start
  214.1 0.0 all-gather.4.cloned.1.call-done.dec_ref
  214.1 10.3 %convolution_convert_fusion.refs_2_ = bf16[8192,256]{1,0:T(8,128)(2,1)S(1)} fusion(bf16[8192,1024]{1,0:T(8,128)(2,1)} %all-gather.4.cloned.1.call-done.dec_ref, bf16[256,1024]{1,0:T(8,128)(2,1)S(1)} %copy-done.3), kind=kOutput, calls=%fused_computation | convolution fusion | flops 4297064448 | bytes 21495808 | tf_op jit(solution)/shard_map/dot_general | solution.py:28
  224.4 0.0 copy-start.4
  224.4 2.0 copy-done.4
  226.4 0.7 constant_dynamic-slice_fusion.refs_3_
  227.1 6.0 %all-to-all-done.3 = bf16[128,32,128]{2,1,0:T(8,128)(2,1)S(1)} async-done(((bf16[128,32,128]{2,1,0:T(8,128)(2,1)}), bf16[128,32,128]{2,1,0:T(8,128)(2,1)S(1)}, u32[]{:S(2)}, u32[]{:S(2)}) %all-to-all-start.3) | async-done | bytes 1048608 | tf_op jit(solution)/shard_map/all_to_all | solution.py:417
  233.1 1.0 copy-done.2
  234.1 23.8 %gate_partial.1 = bf16[128,16,128]{2,1,0:T(8,128)(2,1)} custom-call(bf16[4096,128]{1,0:T(8,128)(2,1)} %bitcast.19, s32[4096,1]{1,0:T(8,128)} %reshape.54.refs_1_.other_ref, bf16[8192,256]{1,0:T(8,128)(2,1)} %copy-done.4, bf16[256,256]{1,0:T(8,128)(2,1)} %constant_dynamic-slice_fusion.refs_3_, f32[128,16,128]{2,1,0:T(8,128)} %get-tuple-element.16.refs_4_), custom_call_target="tpu_custom_call" | custom-call | tf_op jit(solution)/shard_map/gate_partial/pallas_call | solution.py:259
  257.9 0.0 all-gather.6.cloned.1.call-update
  257.9 1.3 dynamic_slice.17
  259.2 0.0 copy-done.8
  259.2 0.1 copy.16
  259.4 12.4 %all_gather.19.ids_ref = s32[1024,2]{1,0:T(8,128)} all-gather(s32[256,2]{1,0:T(8,128)S(1)} %copy.16), channel_id=1, replica_groups=mesh['dp'=4,'dict'=32] {'dp'}, dimensions={0}, use_global_device_ids=true | all-gather | bytes 10240 | tf_op jit(solution)/shard_map/all_gather | solution.py:405
  271.8 12.0 %all_gather.18.acts_ref = bf16[1024,128]{1,0:T(8,128)(2,1)} all-gather(bf16[256,128]{1,0:T(8,128)(2,1)S(1)} %copy-done.7), channel_id=1, replica_groups=mesh['dp'=4,'dict'=32] {'dp'}, dimensions={0}, use_global_device_ids=true | all-gather | bytes 327680 | tf_op jit(solution)/shard_map/all_gather | solution.py:420
  283.8 22.7 %reconstruct_rows.1 = bf16[1024,1024]{1,0:T(8,128)(2,1)} custom-call(bf16[1024,128]{1,0:T(8,128)(2,1)} %all_gather.18.acts_ref, s32[1024,2]{1,0:T(8,128)} %all_gather.19.ids_ref, bf16[8192,1024]{1,0:T(8,128)(2,1)} %all-gather.4.cloned.1.call-done.dec_ref, f32[1,1024]{1,0:T(1,128)} %bitcast.34), custom_call_target="tpu_custom_call" | custom-call | tf_op jit(solution)/shard_map/reconstruct_rows/pallas_call | solution.py:212
  306.5 3.8 %all-to-all-start.2 = ((bf16[4,256,1024]{2,1,0:T(8,128)(2,1)}), bf16[4,256,1024]{2,1,0:T(8,128)(2,1)S(1)}, u32[]{:S(2)}, u32[]{:S(2)}) async-start(bf16[4,256,1024]{2,1,0:T(8,128)(2,1)} %bitcast.24), calls=%async_computation.2 | async-start | bytes 4194304 | tf_op jit(solution)/shard_map/all_to_all | solution.py:423
  310.3 31.5 %mix_decoder.1.refs_3_ = f32[256,1024]{1,0:T(8,128)} custom-call(bf16[4096,128]{1,0:T(8,128)(2,1)} %bitcast.20, s32[4096,1]{1,0:T(8,128)} %reshape.54.refs_1_.other_ref, bf16[8192,1024]{1,0:T(8,128)(2,1)} %all-gather.4.cloned.1.call-done.dec_ref, bf16[256,1024]{1,0:T(8,128)(2,1)} %constant_dynamic-slice_fusion.1.own_dec_ref), custom_call_target="tpu_custom_call" | custom-call | tf_op jit(solution)/shard_map/mix_decoder/pallas_call | solution.py:303
  341.8 0.0 all-to-all-done.2
  341.8 1.6 copy.20
  343.4 12.7 %dictionary_grads.1 = (f32[256,1024]{1,0:T(8,128)}, f32[256,1024]{1,0:T(8,128)}) custom-call(bf16[4,128,16,128]{3,2,1,0:T(8,128)(2,1)} %bitcast.28, bf16[4096,128]{1,0:T(8,128)(2,1)} %bitcast.21, bf16[4096,1024]{1,0:T(8,128)(2,1)} %bitcast.13.refs_2_, f32[256,1024]{1,0:T(8,128)} %mix_decoder.1.refs_3_), custom_call_target="tpu_custom_call" | custom-call | tf_op jit(solution)/shard_map/dictionary_grads/pallas_call | solution.py:361
  356.1 0.0 copy-done.1
  (9 shorter events, 0.0 us)
Async XLA Ops:
  7.2 1.6 copy-start
  7.2 206.9 %all-gather.4.cloned.1.call-start = ((), (), s32[]{:S(2)}) async-start(), calls=%async_computation.4 | async-start | bytes 17301504 | tf_op jit(solution)/shard_map/all_gather | solution.py:402
  16.8 13.1 %copy-start.3 = (bf16[256,1024]{1,0:T(8,128)(2,1)S(1)}, bf16[256,1024]{1,0:T(8,128)(2,1)}, u32[]{:S(2)}) copy-start(bf16[256,1024]{1,0:T(8,128)(2,1)} %constant_dynamic-slice_fusion.1.own_dec_ref) | copy-start | bytes 1572868
  16.8 118.4 %all-to-all-start = ((bf16[128,32,1024]{2,1,0:T(8,128)(2,1)}), bf16[128,32,1024]{2,1,0:T(8,128)(2,1)}, u32[]{:S(2)}, u32[]{:S(2)}) async-start(bf16[128,32,1024]{2,1,0:T(8,128)(2,1)} %bitcast.22), calls=%async_computation | async-start | bytes 16777216 | tf_op jit(solution)/shard_map/all_to_all | solution.py:395
  28.7 2.2 copy-start.9
  142.6 9.1 %copy-start.6 = (s32[1024,1]{1,0:T(8,128)S(1)}, s32[1024,1]{1,0:T(8,128)}, u32[]{:S(2)}) copy-start(s32[1024,1]{1,0:T(8,128)} %get-tuple-element.15) | copy-start | bytes 12292
  142.6 61.3 %all-to-all-start.1 = ((f32[128,16,128]{2,1,0:T(8,128)}), f32[128,16,128]{2,1,0:T(8,128)S(1)}, u32[]{:S(2)}, u32[]{:S(2)}) async-start(f32[128,16,128]{2,1,0:T(8,128)} %get-tuple-element.12), calls=%async_computation.1 | async-start | bytes 2097152 | tf_op jit(solution)/shard_map/all_to_all | solution.py:415
  204.0 1.0 copy-start.5
  208.5 24.6 %all-to-all-start.3 = ((bf16[128,32,128]{2,1,0:T(8,128)(2,1)}), bf16[128,32,128]{2,1,0:T(8,128)(2,1)S(1)}, u32[]{:S(2)}, u32[]{:S(2)}) async-start(bf16[128,32,128]{2,1,0:T(8,128)(2,1)} %bitcast.30), calls=%async_computation.3 | async-start | bytes 2097152 | tf_op jit(solution)/shard_map/all_to_all | solution.py:417
  213.8 129.6 %all-gather.6.cloned.1.call-start = ((), (), s32[]{:S(2)}) async-start(), calls=%async_computation.5 | async-start | bytes 2621440 | tf_op jit(solution)/shard_map/all_gather | solution.py:426
  224.4 2.0 copy-start.4
  233.1 1.0 copy-start.2
  234.1 25.1 %copy-start.8 = (s32[256,2]{0,1:T(2,128)S(1)}, s32[256,2]{0,1:T(2,128)}, u32[]{:S(2)}) copy-start(s32[256,2]{0,1:T(2,128)} %param.7) | copy-start | bytes 6148
  234.1 37.7 %copy-start.7 = (bf16[256,128]{1,0:T(8,128)(2,1)S(1)}, bf16[256,128]{1,0:T(8,128)(2,1)}, u32[]{:S(2)}) copy-start(bf16[256,128]{1,0:T(8,128)(2,1)} %get-tuple-element.13) | copy-start | bytes 196612
  306.5 35.3 %all-to-all-start.2 = ((bf16[4,256,1024]{2,1,0:T(8,128)(2,1)}), bf16[4,256,1024]{2,1,0:T(8,128)(2,1)S(1)}, u32[]{:S(2)}, u32[]{:S(2)}) async-start(bf16[4,256,1024]{2,1,0:T(8,128)(2,1)} %bitcast.24), calls=%async_computation.2 | async-start | bytes 4194304 | tf_op jit(solution)/shard_map/all_to_all | solution.py:423
  343.4 12.7 %copy-start.1 = (bf16[256,4096]{1,0:T(8,128)(2,1)S(1)}, bf16[256,4096]{1,0:T(8,128)(2,1)}, u32[]{:S(2)}) copy-start(bf16[256,4096]{1,0:T(8,128)(2,1)} %param.10) | copy-start | bytes 6291460
Sparse Core Ops, SparseCore 0:
  10.3 181.1 all-gather.3
  258.1 30.8 all-gather.5

commit v2 on v1

--- a/solution.py
+++ b/solution.py
@@ -14,6 +14,10 @@
 
 def params(**more):
     return pltpu.CompilerParams(vmem_limit_bytes=VMEM_LIMIT, **more)
+
+
+def cost(flops, moved):
+    return pl.CostEstimate(flops=int(flops), bytes_accessed=int(moved), transcendentals=0)
 
 
 def dot(a, b):
@@ -45,7 +49,58 @@
     return rank0, rank1
 
 
-def route_kernel(ids_ref, resid_ref, bias_ref, out_ref, table_ref, pick_ref):
+def table_kernel(ids_ref, out_ref):
+    parts, shards, _, lanes = out_ref.shape
+    rows = ids_ref.shape[1]
+    ids = ids_ref[...]
+    found = jnp.zeros((shards, lanes), F32)
+    for k, rank in enumerate(ranks(ids, shards * 4)):
+        block = ids[k : k + 1, :]
+        other = (ids[1 - k : 2 - k, :] + 1).astype(F32)
+        target = jnp.where(iota((shards, rows), 0) == block // 4, other, 0.0).astype(BF)
+        place = iota((lanes, rows), 0) == (block % 4) * CAP + rank
+        found = found + dot_nt(target, jnp.where(place, 1.0, 0.0).astype(BF))
+    found = jnp.broadcast_to((found.astype(jnp.int32) - 1)[:, None, :], (shards, CAP, lanes))
+    for copy in range(parts):
+        out_ref[copy] = found
+
+
+def table(ids, parts, shards):
+    return pl.pallas_call(
+        table_kernel,
+        out_shape=jax.ShapeDtypeStruct((parts, shards, CAP, 128), jnp.int32),
+        compiler_params=params(),
+        cost_estimate=cost(2e7, 2**20),
+        name="slot_table",
+    )(ids)
+
+
+def names_kernel(table_ref, out_ref):
+    sources = table_ref.shape[0]
+    here = out_ref.shape[0] // sources
+    row = table_ref[:, 0:1, :].astype(F32)
+    shape = (sources, here, 128)
+    kept = jnp.where(iota(shape, 1) == iota(shape, 2), jnp.broadcast_to(row, shape), 0.0)
+    name = jnp.sum(kept, axis=2, keepdims=True)
+    out_ref[...] = jnp.broadcast_to(name, shape).reshape(sources * here, 128).astype(BF)
+
+
+def names(tables, here):
+    sources = tables.shape[0]
+    step = 16
+    return pl.pallas_call(
+        names_kernel,
+        grid=(sources // step,),
+        in_specs=[pl.BlockSpec((step, CAP, 128), lambda i: (i, 0, 0))],
+        out_specs=pl.BlockSpec((step * here, 128), lambda i: (i, 0)),
+        out_shape=jax.ShapeDtypeStruct((sources * here, 128), BF),
+        compiler_params=params(),
+        cost_estimate=cost(2e7, 2**21),
+        name="slot_names",
+    )(tables)
+
+
+def route_kernel(ids_ref, resid_ref, bias_ref, out_ref, pick_ref):
     slots, rows = pick_ref.shape
 
     @pl.when(pl.program_id(0) == 0)
@@ -56,8 +111,6 @@
         is0 = slot == ids[0:1, :] * CAP + rank0
         is1 = slot == ids[1:2, :] * CAP + rank1
         pick_ref[...] = jnp.where(is0 | is1, 1.0, 0.0).astype(BF)
-        other = jnp.where(is0, ids[1:2, :] + 1, 0) + jnp.where(is1, ids[0:1, :] + 1, 0)
-        table_ref[...] = jnp.sum(other.astype(F32), axis=1, keepdims=True).astype(jnp.int32) - 1
 
     centered = (resid_ref[...].astype(F32) - bias_ref[...]).astype(BF)
     step = 256
@@ -76,16 +129,11 @@
             pl.BlockSpec((rows, cols), lambda i: (0, i)),
             pl.BlockSpec((1, cols), lambda i: (0, i)),
         ],
-        out_specs=[
-            pl.BlockSpec((1, slots, cols), lambda i: (i, 0, 0)),
-            pl.BlockSpec((slots, 1), lambda i: (0, 0)),
-        ],
-        out_shape=[
-            jax.ShapeDtypeStruct((parts, slots, cols), BF),
-            jax.ShapeDtypeStruct((slots, 1), jnp.int32),
-        ],
+        out_specs=pl.BlockSpec((1, slots, cols), lambda i: (i, 0, 0)),
+        out_shape=jax.ShapeDtypeStruct((parts, slots, cols), BF),
         scratch_shapes=[pltpu.VMEM((slots, rows), BF)],
         compiler_params=params(),
+        cost_estimate=cost(2 * slots * rows * width, 10 * 2**20),
         name="route_rows",
     )(ids, resid, dec_b.reshape(1, width))
 
@@ -117,11 +165,12 @@
         out_specs=[pl.BlockSpec((step, 2 * CAP, 128), lambda i: (i, 0, 0))] * 2,
         out_shape=[shape, shape],
         compiler_params=params(),
+        cost_estimate=cost(2 * sources * here * cols * 256, 11 * 2**20),
         name="encode_rows",
     )(arrived, weights, bias)
 
 
-def activate_kernel(ids_ref, pre_ref, rows_ref, msg_ref):
+def activate_kernel(ids_ref, columns_ref, pre_ref, rows_ref, msg_ref):
     packed = pre_ref.shape[1]
     rows = ids_ref.shape[1]
     slots = 2 * packed
@@ -140,7 +189,11 @@
     first, second = found
     straight = jnp.concatenate([first, second], axis=1).astype(BF)
     crossed = jnp.concatenate([second, first], axis=1).astype(BF)
-    rows_ref[...] = straight
+    lane = iota((rows, 128), 1)
+    named = jnp.where(lane == 0, columns_ref[:, 0:1], jnp.where(lane == 1, columns_ref[:, 1:2], 0))
+    group = jnp.concatenate([straight, named.astype(F32).astype(BF)], axis=1)
+    for copy in range(rows_ref.shape[0]):
+        rows_ref[copy] = group
     pick0 = jnp.where(slot == ids[0:1, :] * CAP + rank0, 1.0, 0.0).astype(BF)
     pick1 = jnp.where(slot == ids[1:2, :] * CAP + rank1, 1.0, 0.0).astype(BF)
     msg = (dot(pick0, straight) + dot(pick1, crossed)).astype(BF)
@@ -148,18 +201,19 @@
         msg_ref[copy] = msg
 
 
-def activate(ids, partial):
+def activate(ids, columns, partial):
     parts, packed, lanes = partial.shape
     rows = ids.shape[1]
     return pl.pallas_call(
         activate_kernel,
         out_shape=[
-            jax.ShapeDtypeStruct((rows, lanes), BF),
+            jax.ShapeDtypeStruct((parts, rows, 2 * lanes), BF),
             jax.ShapeDtypeStruct((parts, 2 * packed, lanes), BF),
         ],
         compiler_params=params(),
+        cost_estimate=cost(8 * packed * rows * lanes, 3 * 2**20),
         name="activate_rows",
-    )(ids, partial)
+    )(ids, columns, partial)
 
 
 def doubled(pair):
@@ -179,15 +233,17 @@
     return jnp.where(mine, twice.astype(F32), 0.0).astype(BF)
 
 
-def recon_kernel(acts_ref, ids_ref, dec_ref, bias_ref, out_ref, twice_ref, name0_ref, name1_ref, acc_ref):
+def recon_kernel(
+    acts_ref, dec_ref, own_dec_ref, bias_ref, out_ref, gram_ref, twice_ref, name0_ref, name1_ref, acc_ref
+):
     at = pl.program_id(0)
     rows = acts_ref.shape[0]
     chunk = dec_ref.shape[0]
 
     @pl.when(at == 0)
     def _():
-        twice_ref[...] = doubled(acts_ref[...])
-        ids = ids_ref[...].astype(F32)
+        twice_ref[...] = doubled(acts_ref[:, :128])
+        ids = acts_ref[:, 128:].astype(F32)
         name0_ref[...] = jnp.broadcast_to(ids[:, 0:1], (rows, 128)).astype(BF)
         name1_ref[...] = jnp.broadcast_to(ids[:, 1:2], (rows, 128)).astype(BF)
         acc_ref[...] = jnp.broadcast_to(bias_ref[...], acc_ref.shape)
@@ -199,13 +255,14 @@
         one = jnp.where(name0_ref[...] == block, twice_ref[:, :128], zero)
         spread.append(jnp.where(name1_ref[...] == block, twice_ref[:, 128:], one))
     acc_ref[...] += dot(jnp.concatenate(spread, axis=1), dec_ref[...])
+    gram_ref[...] = dot_nt(dec_ref[...], own_dec_ref[...]).astype(BF)
 
     @pl.when(at == pl.num_programs(0) - 1)
     def _():
         out_ref[...] = acc_ref[...].astype(BF)
 
 
-def reconstruct(acts, ids, dec_all, bias):
+def reconstruct(acts, dec_all, own_dec, bias):
     rows = acts.shape[0]
     latents, cols = dec_all.shape
     chunk = 1024
@@ -214,12 +271,18 @@
         grid=(latents // chunk,),
         in_specs=[
             pl.BlockSpec(acts.shape, lambda i: (0, 0)),
-            pl.BlockSpec(ids.shape, lambda i: (0, 0)),
             pl.BlockSpec((chunk, cols), lambda i: (i, 0)),
+            pl.BlockSpec(own_dec.shape, lambda i: (0, 0)),
             pl.BlockSpec((1, cols), lambda i: (0, 0)),
         ],
-        out_specs=pl.BlockSpec((rows, cols), lambda i: (0, 0)),
-        out_shape=jax.ShapeDtypeStruct((rows, cols), BF),
+        out_specs=[
+            pl.BlockSpec((rows, cols), lambda i: (0, 0)),
+            pl.BlockSpec((chunk, own_dec.shape[0]), lambda i: (i, 0)),
+        ],
+        out_shape=[
+            jax.ShapeDtypeStruct((rows, cols), BF),
+            jax.ShapeDtypeStruct((latents, own_dec.shape[0]), BF),
+        ],
         scratch_shapes=[
             pltpu.VMEM((rows, 256), BF),
             pltpu.VMEM((rows, 128), BF),
@@ -227,14 +290,15 @@
             pltpu.VMEM((rows, cols), F32),
         ],
         compiler_params=params(),
+        cost_estimate=cost(2 * latents * cols * (rows + own_dec.shape[0]), 24 * 2**20),
         name="reconstruct_rows",
-    )(acts, ids, dec_all, bias)
+    )(acts, dec_all, own_dec, bias)
 
 
 def gate_kernel(scale, msg_ref, other_ref, gram_ref, own_gram_ref, proj_ref, out_ref):
     count = msg_ref.shape[0]
     twice = doubled(msg_ref[...])
-    names = jnp.broadcast_to(other_ref[...].astype(F32), (count, 128)).astype(BF)
+    names = other_ref[...]
     zero = jnp.zeros((count, 128), BF)
     total = dot(own_expanded(twice[:, :128]), own_gram_ref[...])
     chunk = 1024
@@ -261,7 +325,7 @@
         grid=(count // step,),
         in_specs=[
             pl.BlockSpec((step, lanes), lambda i: (i, 0)),
-            pl.BlockSpec((step, 1), lambda i: (i, 0)),
+            pl.BlockSpec((step, lanes), lambda i: (i, 0)),
             pl.BlockSpec(gram.shape, lambda i: (0, 0)),
             pl.BlockSpec(own_gram.shape, lambda i: (0, 0)),
             pl.BlockSpec((step // 32, 2 * CAP, 128), lambda i: (i, 0, 0)),
@@ -269,11 +333,12 @@
         out_specs=pl.BlockSpec((step // 32, 2 * CAP, 128), lambda i: (i, 0, 0)),
         out_shape=jax.ShapeDtypeStruct(proj.shape, BF),
         compiler_params=params(),
+        cost_estimate=cost(2 * count * gram.shape[0] * gram.shape[1], 10 * 2**20),
         name="gate_partial",
     )(msg, other, gram, own_gram, proj)
 
 
-def mix_kernel(msg_ref, other_ref, dec_ref, own_dec_ref, out_ref, own_ref, twice_ref, name_ref):
+def mix_kernel(msg_ref, name_ref, dec_ref, own_dec_ref, out_ref, own_ref, twice_ref):
     at = pl.program_id(0)
     count = msg_ref.shape[0]
     chunk = dec_ref.shape[0]
@@ -282,7 +347,6 @@
     def _():
         twice = doubled(msg_ref[...])
         twice_ref[...] = twice[:, 128:]
-        name_ref[...] = jnp.broadcast_to(other_ref[...].astype(F32), (count, 128)).astype(BF)
         own = own_expanded(twice[:, :128])
         own_ref[...] = own.T
         out_ref[...] = dot(dot(own_ref[...], own).astype(BF), own_dec_ref[...])
@@ -314,9 +378,9 @@
         scratch_shapes=[
             pltpu.VMEM((256, count), BF),
             pltpu.VMEM((count, 128), BF),
-            pltpu.VMEM((count, 128), BF),
-        ],
-        compiler_params=params(),
+        ],
+        compiler_params=params(),
+        cost_estimate=cost(2 * latents * 256 * (count + cols), 20 * 2**20),
         name="mix_decoder",
     )(msg, other, dec_all, own_dec)
 
@@ -371,6 +435,7 @@
         out_shape=[shape, shape],
         scratch_shapes=[pltpu.VMEM((512, cols), F32)],
         compiler_params=params(),
+        cost_estimate=cost(4 * count * cols * 256, 16 * 2**20),
         name="dictionary_grads",
     )(gates, msg, rows, mixed)
 
@@ -391,7 +456,10 @@
     at_dict = lax.axis_index("dict")
 
     ids = block_ids.T
-    outgoing, table = route(ids, resid, dec_b, parts, slots)
+    tables = lax.all_to_all(
+        table(ids, parts, shards).reshape(devices, CAP, 128), everyone, 0, 0, tiled=True
+    )
+    outgoing = route(ids, resid, dec_b, parts, slots)
     arrived = lax.all_to_all(
         outgoing.reshape(devices, here * CAP, cols), everyone, 0, 0, tiled=True
     )
@@ -400,12 +468,7 @@
     dec_x = lax.dynamic_slice(dec_w, (0, at_x * cols), (local, cols))
     bias_x = lax.dynamic_slice(dec_b, (at_x * cols,), (cols,)).reshape(1, cols)
     dec_all = lax.all_gather(dec_x, "dict", axis=0, tiled=True)
-    gram = dot_nt(dec_all, dec_x).astype(BF)
-    own_gram = lax.dynamic_slice(gram, (at_dict * local, 0), (local, local))
-    group_ids = lax.all_gather(block_ids, "dp", axis=0, tiled=True)
-    tables = lax.all_gather(table.reshape(shards, here * CAP), everyone, axis=0, tiled=False)
-    other = lax.dynamic_slice(tables, (0, at_dict, 0), (devices, 1, here * CAP))
-    other = other.reshape(devices * here * CAP, 1)
+    other = names(tables, here * CAP)
 
     weights = jnp.concatenate(
         [enc_x.reshape(2, 2 * LAT, cols), dec_x.reshape(2, 2 * LAT, cols)], axis=1
@@ -413,15 +476,16 @@
     bias = jnp.where(at_x == 0, enc_b, 0.0).reshape(2, 2 * LAT)
     pre, proj = encode(arrived, weights, bias)
     partial = lax.all_to_all(pre, everyone, 0, 0, tiled=True)
-    acts, msg = activate(ids, partial.reshape(parts, shards * 2 * CAP, 128))
+    acts, msg = activate(ids, block_ids, partial.reshape(parts, shards * 2 * CAP, 128))
+    group_acts = lax.all_to_all(acts, "dp", 0, 0, tiled=True)
     message = lax.all_to_all(
         msg.reshape(devices, here * CAP, 128), everyone, 0, 0, tiled=True
     ).reshape(devices * here * CAP, 128)
-    group_acts = lax.all_gather(acts, "dp", axis=0, tiled=True)
-
-    recon_x = reconstruct(group_acts, group_ids, dec_all, bias_x)
+
+    recon_x, gram = reconstruct(group_acts.reshape(parts * tok_rows, 256), dec_all, dec_x, bias_x)
     recon = lax.all_to_all(recon_x, "dp", 0, 1, tiled=True)
 
+    own_gram = lax.dynamic_slice(gram, (at_dict * local, 0), (local, local))
     gate = gate_partial(scale, message, other, gram, own_gram, proj)
     gates = lax.all_gather(gate, "dp", axis=0, tiled=False)
     mixed = mix(message, other, dec_all, dec_x)

time: 369 us -> 336 us (0.911)
  blocking collectives: 72.7 us -> 0 us
  waiting for transfers between devices: 110 us -> 140 us
  starting transfers between devices: 30.4 us -> 44 us
  Pallas kernels: 109 us -> 121 us
  matrix products: 10.3 us -> 0 us
    all_gather x3 -> x0, blocking collectives: 72.7 us -> none  [the longest x1 48.3 us: body(): lax.all_gather(table.reshape(shards, here * CAP), everyone, axis=0, tiled...]
    all_to_all x1, waiting for transfers between devices: 0.01 us -> 17.4 us  [body(): partial = lax.all_to_all(pre, everyone, 0, 0, tiled=True)]
    all_to_all x0 -> x2, starting transfers between devices: none -> 11 us  [the longest x1 7.46 us: body(): lax.all_to_all(table(ids, parts, shards).reshape(devices, CAP, 128), ever...]
    dot_general x1 -> x0, matrix products: 10.3 us -> none  [dot_nt(): lax.dot_general(a, b, (((1,), (1,)), ((), ())), preferred_element_type=F32)]
    all_to_all x0 -> x2, waiting for transfers between devices: none -> 10.1 us  [the longest x1 8.71 us: body(): lax.all_to_all(table(ids, parts, shards).reshape(devices, CAP, 128), ever...]
    all_to_all x1, waiting for transfers between devices: 0.01 us -> 8.17 us  [body(): recon = lax.all_to_all(recon_x, 'dp', 0, 1, tiled=True)]
    pallas_call x1 -> x3, Pallas kernels: 3.59 us -> 11.1 us  [the longest x1 5.4 us: names(): pl.pallas_call(names_kernel, grid=(sources // step,), in_specs=[pl.BlockS...]
    all_to_all x1, waiting for transfers between devices: 6.04 us -> 0.01 us  [body(): lax.all_to_all(msg.reshape(devices, here * CAP, 128), everyone, 0, 0, til...]
  transfers between devices with their start and end apart: 6 -> 8, of which waited for: 2 -> 6; matrix products, arithmetic and copies ran while one was open for 6% -> 3% of each run, Pallas kernels for 20% -> 25%
where the time goes in v2:
time: 336 us; the launch traced here: 333 us
  waiting for transfers between devices  140 us (42%)
  Pallas kernels  121 us (36%)
  starting transfers between devices  44 us (13%)
  between operations  14.2 us (4%)
  local copies, waits for them, and re-layouts  12 us (4%)
    all_to_all x1, waiting for transfers between devices, body(): lax.all_to_all(outgoing.reshape(devices, here * CAP, cols), everyone, 0,...  103 us
    pallas_call x1, Pallas kernels, mix(): pl.pallas_call(mix_kernel, grid=(latents // chunk,), in_specs=[pl.BlockSp...  31 us
    pallas_call x1, Pallas kernels, reconstruct(): pl.pallas_call(recon_kernel, grid=(latents // chunk,), in_specs=[pl.Block...  28.7 us
    pallas_call x1, Pallas kernels, gate_partial(): pl.pallas_call(lambda *refs: gate_kernel(scale, *refs), grid=(count // st...  23.8 us
    all_to_all x1, waiting for transfers between devices, body(): partial = lax.all_to_all(pre, everyone, 0, 0, tiled=True)  17.4 us
    pallas_call x1, Pallas kernels, grads(): pl.pallas_call(lambda *refs: grads_kernel(scale, *refs), grid=(count // s...  12.6 us
    all_to_all x1, starting transfers between devices, body(): lax.all_to_all(outgoing.reshape(devices, here * CAP, cols), everyone, 0,...  12 us
    all_to_all x1, starting transfers between devices, body(): partial = lax.all_to_all(pre, everyone, 0, 0, tiled=True)  10.4 us
  transfers between devices with their start and end apart: 8, of which 6 were waited for; matrix products, arithmetic and copies ran while one was open for 3% of the time, Pallas kernels for 25%

profile of v2, /device:TPU:1, one launch (start us, length us, event | category | flops | bytes accessed | tf_op | source)
XLA Modules:
  0.0 332.6 jit_solution(14985014705127590996)
XLA Ops:
  7.2 0.0 copy-start
  7.2 0.0 all-gather.4.cloned.1.call-start
  7.2 1.5 copy-done
  8.8 0.8 constant_dynamic-slice_fusion.1.own_dec_ref
  9.6 0.0 all-gather.4.cloned.1.call-update
  9.6 7.1 %route_rows.1 = bf16[4,1024,1024]{2,1,0:T(8,128)(2,1)} custom-call(s32[2,256]{1,0:T(2,128)} %bitcast.31, bf16[256,4096]{1,0:T(8,128)(2,1)} %resid_ref.1, f32[1,4096]{1,0:T(1,128)} %bitcast.34), custom_call_target="tpu_custom_call" | custom-call | flops 2147483648 | bytes 10485760 | tf_op jit(solution)/shard_map/route_rows/pallas_call | solution.py:124
  16.7 0.0 copy-start.1
  16.7 12.0 %all-to-all-start = ((bf16[128,32,1024]{2,1,0:T(8,128)(2,1)}), bf16[128,32,1024]{2,1,0:T(8,128)(2,1)}, u32[]{:S(2)}, u32[]{:S(2)}) async-start(bf16[128,32,1024]{2,1,0:T(8,128)(2,1)} %bitcast.19), calls=%async_computation | async-start | bytes 16777216 | tf_op jit(solution)/shard_map/all_to_all | solution.py:463
  28.7 0.0 copy-start.6
  28.7 1.1 constant_dynamic-slice_fusion.2
  29.8 0.0 copy-done.1
  29.8 1.0 pad_maximum_fusion.weight_ref
  30.8 0.0 copy-done.6
  30.8 0.6 select_bitcast_fusion.bias_ref
  31.4 102.9 %all-to-all-done.rows_ref = bf16[128,32,1024]{2,1,0:T(8,128)(2,1)} async-done(((bf16[128,32,1024]{2,1,0:T(8,128)(2,1)}), bf16[128,32,1024]{2,1,0:T(8,128)(2,1)}, u32[]{:S(2)}, u32[]{:S(2)}) %all-to-all-start) | async-done | bytes 8388640 | tf_op jit(solution)/shard_map/all_to_all | solution.py:463
  134.3 6.9 %encode_rows.1 = (f32[128,16,128]{2,1,0:T(8,128)}, f32[128,16,128]{2,1,0:T(8,128)}) custom-call(bf16[128,32,1024]{2,1,0:T(8,128)(2,1)} %all-to-all-done.rows_ref, bf16[2,256,1024]{2,1,0:T(8,128)(2,1)} %pad_maximum_fusion.weight_ref, f32[2,128]{1,0:T(2,128)} %select_bitcast_fusion.bias_ref), custom_call_target="tpu_custom_call" | custom-call | flops 2147483648 | bytes 11534336 | tf_op jit(solution)/shard_map/encode_rows/pallas_call | solution.py:157
  141.1 0.0 copy-start.5
  141.1 10.4 %all-to-all-start.1 = ((f32[128,16,128]{2,1,0:T(8,128)}), f32[128,16,128]{2,1,0:T(8,128)S(1)}, u32[]{:S(2)}, u32[]{:S(2)}) async-start(f32[128,16,128]{2,1,0:T(8,128)} %get-tuple-element.11), calls=%async_computation.1 | async-start | bytes 2097152 | tf_op jit(solution)/shard_map/all_to_all | solution.py:478
  151.5 1.9 slot_table.1
  153.4 17.4 %all-to-all-done.1 = f32[128,16,128]{2,1,0:T(8,128)S(1)} async-done(((f32[128,16,128]{2,1,0:T(8,128)}), f32[128,16,128]{2,1,0:T(8,128)S(1)}, u32[]{:S(2)}, u32[]{:S(2)}) %all-to-all-start.1) | async-done | bytes 1048608 | tf_op jit(solution)/shard_map/all_to_all | solution.py:478
  170.8 0.0 copy-start.2
  170.8 7.5 %all-to-all-start.5 = ((s32[128,8,128]{2,1,0:T(8,128)}), s32[128,8,128]{2,1,0:T(8,128)}, u32[]{:S(2)}, u32[]{:S(2)}) async-start(s32[128,8,128]{2,1,0:T(8,128)} %bitcast.24), calls=%async_computation.5 | async-start | bytes 1048576 | tf_op jit(solution)/shard_map/all_to_all | solution.py:459
  178.3 0.0 copy-done.5
  178.3 0.8 copy.11.columns_ref
  179.1 0.0 copy-done.2
  179.1 3.8 %activate_rows.1 = (bf16[4,256,256]{2,1,0:T(8,128)(2,1)}, bf16[4,1024,128]{2,1,0:T(8,128)(2,1)}) custom-call(s32[2,256]{1,0:T(2,128)} %bitcast.33, s32[256,2]{1,0:T(8,128)} %copy.11.columns_ref, f32[4,512,128]{2,1,0:T(8,128)} %bitcast.21), custom_call_target="tpu_custom_call" | custom-call | flops 134217728 | bytes 3145728 | tf_op jit(solution)/shard_map/activate_rows/pallas_call | solution.py:207
  182.9 8.7 %all-to-all-done.5.table_ref = s32[128,8,128]{2,1,0:T(8,128)} async-done(((s32[128,8,128]{2,1,0:T(8,128)}), s32[128,8,128]{2,1,0:T(8,128)}, u32[]{:S(2)}, u32[]{:S(2)}) %all-to-all-start.5) | async-done | bytes 524320 | tf_op jit(solution)/shard_map/all_to_all | solution.py:459
  191.6 3.5 %all-to-all-start.2 = ((bf16[4,256,256]{2,1,0:T(8,128)(2,1)}), bf16[4,256,256]{2,1,0:T(8,128)(2,1)S(1)}, u32[]{:S(2)}, u32[]{:S(2)}) async-start(bf16[4,256,256]{2,1,0:T(8,128)(2,1)} %get-tuple-element.12), calls=%async_computation.2 | async-start | bytes 1048576 | tf_op jit(solution)/shard_map/all_to_all | solution.py:480
  195.2 1.3 dynamic_slice.14
  196.4 5.4 %slot_names.1.refs_1_.name_ref = bf16[4096,128]{1,0:T(8,128)(2,1)} custom-call(s32[128,8,128]{2,1,0:T(8,128)} %all-to-all-done.5.table_ref), custom_call_target="tpu_custom_call" | custom-call | flops 20000000 | bytes 2097152 | tf_op jit(solution)/shard_map/slot_names/pallas_call | solution.py:91
  201.8 1.4 all-to-all-done.2
  203.3 0.0 copy-start.4
  203.3 0.8 copy-done.4
  204.1 6.0 %all-to-all-start.4 = ((bf16[128,32,128]{2,1,0:T(8,128)(2,1)}), bf16[128,32,128]{2,1,0:T(8,128)(2,1)S(1)}, u32[]{:S(2)}, u32[]{:S(2)}) async-start(bf16[128,32,128]{2,1,0:T(8,128)(2,1)} %bitcast.29), calls=%async_computation.4 | async-start | bytes 2097152 | tf_op jit(solution)/shard_map/all_to_all | solution.py:481
  210.0 0.2 all-gather.6.cloned.1.call-start
  210.3 0.0 all-gather.4.cloned.1.call-done.dec_ref
  210.3 28.7 %reconstruct_rows.1 = (bf16[1024,1024]{1,0:T(8,128)(2,1)}, bf16[8192,256]{1,0:T(8,128)(2,1)}) custom-call(bf16[1024,256]{1,0:T(8,128)(2,1)} %bitcast.30, bf16[8192,1024]{1,0:T(8,128)(2,1)} %all-gather.4.cloned.1.call-done.dec_ref, bf16[256,1024]{1,0:T(8,128)(2,1)} %constant_dynamic-slice_fusion.1.own_dec_ref, f32[1,1024]{1,0:T(1,128)} %bitcast.35), custom_call_target="tpu_custom_call" | custom-call | flops 21474836480 | bytes 25165824 | tf_op jit(solution)/shard_map/reconstruct_rows/pallas_call | solution.py:269
  239.0 1.6 constant_dynamic-slice_fusion.refs_3_
  240.5 0.0 all-to-all-done.4
  240.5 1.0 copy-done.3
  241.5 23.8 %gate_partial.1 = bf16[128,16,128]{2,1,0:T(8,128)(2,1)} custom-call(bf16[4096,128]{1,0:T(8,128)(2,1)} %bitcast.26, bf16[4096,128]{1,0:T(8,128)(2,1)} %slot_names.1.refs_1_.name_ref, bf16[8192,256]{1,0:T(8,128)(2,1)} %get-tuple-element.15.refs_2_, bf16[256,256]{1,0:T(8,128)(2,1)} %constant_dynamic-slice_fusion.refs_3_, f32[128,16,128]{2,1,0:T(8,128)} %get-tuple-element.16.refs_4_), custom_call_target="tpu_custom_call" | custom-call | flops 17179869184 | bytes 10485760 | tf_op jit(solution)/shard_map/gate_partial/pallas_call | solution.py:323
  265.2 0.0 all-gather.6.cloned.1.call-update
  265.3 4.5 %all-to-all-start.3 = ((bf16[4,256,1024]{2,1,0:T(8,128)(2,1)}), bf16[4,256,1024]{2,1,0:T(8,128)(2,1)}, u32[]{:S(2)}, u32[]{:S(2)}) async-start(bf16[4,256,1024]{2,1,0:T(8,128)(2,1)} %bitcast.22), calls=%async_computation.3 | async-start | bytes 4194304 | tf_op jit(solution)/shard_map/all_to_all | solution.py:486
  269.7 31.0 %mix_decoder.1.refs_3_ = f32[256,1024]{1,0:T(8,128)} custom-call(bf16[4096,128]{1,0:T(8,128)(2,1)} %bitcast.27, bf16[4096,128]{1,0:T(8,128)(2,1)} %slot_names.1.refs_1_.name_ref, bf16[8192,1024]{1,0:T(8,128)(2,1)} %all-gather.4.cloned.1.call-done.dec_ref, bf16[256,1024]{1,0:T(8,128)(2,1)} %constant_dynamic-slice_fusion.1.own_dec_ref), custom_call_target="tpu_custom_call" | custom-call | flops 21474836480 | bytes 20971520 | tf_op jit(solution)/shard_map/mix_decoder/pallas_call | solution.py:367
  300.8 8.2 %all-to-all-done.3 = bf16[4,256,1024]{2,1,0:T(8,128)(2,1)} async-done(((bf16[4,256,1024]{2,1,0:T(8,128)(2,1)}), bf16[4,256,1024]{2,1,0:T(8,128)(2,1)}, u32[]{:S(2)}, u32[]{:S(2)}) %all-to-all-start.3) | async-done | bytes 2097184 | tf_op jit(solution)/shard_map/all_to_all | solution.py:486
  308.9 3.2 copy.13
  312.1 1.1 all-gather.6.cloned.1.call-done
  313.2 12.6 %dictionary_grads.1 = (f32[256,1024]{1,0:T(8,128)}, f32[256,1024]{1,0:T(8,128)}) custom-call(bf16[4,128,16,128]{3,2,1,0:T(8,128)(2,1)} %bitcast.36, bf16[4096,128]{1,0:T(8,128)(2,1)} %bitcast.28, bf16[4096,1024]{1,0:T(8,128)(2,1)} %bitcast.15.refs_2_, f32[256,1024]{1,0:T(8,128)} %mix_decoder.1.refs_3_), custom_call_target="tpu_custom_call" | custom-call | flops 4294967296 | bytes 16777216 | tf_op jit(solution)/shard_map/dictionary_grads/pallas_call | solution.py:425
  (1 shorter events, 0.0 us)
Async XLA Ops:
  7.2 1.6 copy-start
  7.2 203.1 %all-gather.4.cloned.1.call-start = ((), (), s32[]{:S(2)}) async-start(), calls=%async_computation.6 | async-start | bytes 17301504 | tf_op jit(solution)/shard_map/all_gather | solution.py:470
  16.7 13.1 %copy-start.1 = (bf16[256,1024]{1,0:T(8,128)(2,1)S(1)}, bf16[256,1024]{1,0:T(8,128)(2,1)}, u32[]{:S(2)}) copy-start(bf16[256,1024]{1,0:T(8,128)(2,1)} %constant_dynamic-slice_fusion.1.own_dec_ref) | copy-start | bytes 1572868
  16.7 117.5 %all-to-all-start = ((bf16[128,32,1024]{2,1,0:T(8,128)(2,1)}), bf16[128,32,1024]{2,1,0:T(8,128)(2,1)}, u32[]{:S(2)}, u32[]{:S(2)}) async-start(bf16[128,32,1024]{2,1,0:T(8,128)(2,1)} %bitcast.19), calls=%async_computation | async-start | bytes 16777216 | tf_op jit(solution)/shard_map/all_to_all | solution.py:463
  28.7 2.2 copy-start.6
  141.1 37.2 %copy-start.5 = (s32[256,2]{0,1:T(2,128)S(1)}, s32[256,2]{0,1:T(2,128)}, u32[]{:S(2)}) copy-start(s32[256,2]{0,1:T(2,128)} %param.7) | copy-start | bytes 6148
  141.1 29.7 %all-to-all-start.1 = ((f32[128,16,128]{2,1,0:T(8,128)}), f32[128,16,128]{2,1,0:T(8,128)S(1)}, u32[]{:S(2)}, u32[]{:S(2)}) async-start(f32[128,16,128]{2,1,0:T(8,128)} %get-tuple-element.11), calls=%async_computation.1 | async-start | bytes 2097152 | tf_op jit(solution)/shard_map/all_to_all | solution.py:478
  170.8 8.3 %copy-start.2 = (f32[128,16,128]{2,1,0:T(8,128)}, f32[128,16,128]{2,1,0:T(8,128)S(1)}, u32[]{:S(2)}) copy-start(f32[128,16,128]{2,1,0:T(8,128)S(1)} %all-to-all-done.1) | copy-start | bytes 3145732
  170.8 20.8 %all-to-all-start.5 = ((s32[128,8,128]{2,1,0:T(8,128)}), s32[128,8,128]{2,1,0:T(8,128)}, u32[]{:S(2)}, u32[]{:S(2)}) async-start(s32[128,8,128]{2,1,0:T(8,128)} %bitcast.24), calls=%async_computation.5 | async-start | bytes 1048576 | tf_op jit(solution)/shard_map/all_to_all | solution.py:459
  191.6 11.6 %all-to-all-start.2 = ((bf16[4,256,256]{2,1,0:T(8,128)(2,1)}), bf16[4,256,256]{2,1,0:T(8,128)(2,1)S(1)}, u32[]{:S(2)}, u32[]{:S(2)}) async-start(bf16[4,256,256]{2,1,0:T(8,128)(2,1)} %get-tuple-element.12), calls=%async_computation.2 | async-start | bytes 1048576 | tf_op jit(solution)/shard_map/all_to_all | solution.py:480
  203.3 0.8 copy-start.4
  204.1 36.4 %all-to-all-start.4 = ((bf16[128,32,128]{2,1,0:T(8,128)(2,1)}), bf16[128,32,128]{2,1,0:T(8,128)(2,1)S(1)}, u32[]{:S(2)}, u32[]{:S(2)}) async-start(bf16[128,32,128]{2,1,0:T(8,128)(2,1)} %bitcast.29), calls=%async_computation.4 | async-start | bytes 2097152 | tf_op jit(solution)/shard_map/all_to_all | solution.py:481
  210.0 103.2 %all-gather.6.cloned.1.call-start = ((), (), s32[]{:S(2)}) async-start(), calls=%async_computation.7 | async-start | bytes 2621440 | tf_op jit(solution)/shard_map/all_gather | solution.py:490
  240.5 1.0 copy-start.3
  265.3 43.7 %all-to-all-start.3 = ((bf16[4,256,1024]{2,1,0:T(8,128)(2,1)}), bf16[4,256,1024]{2,1,0:T(8,128)(2,1)}, u32[]{:S(2)}, u32[]{:S(2)}) async-start(bf16[4,256,1024]{2,1,0:T(8,128)(2,1)} %bitcast.22), calls=%async_computation.3 | async-start | bytes 4194304 | tf_op jit(solution)/shard_map/all_to_all | solution.py:486
Sparse Core Ops, SparseCore 0:
  10.3 185.2 all-gather.3
  265.4 47.7 all-gather.5

commit v3 on v2

--- a/solution.py
+++ b/solution.py
@@ -49,10 +49,8 @@
     return rank0, rank1
 
 
-def table_kernel(ids_ref, out_ref):
-    parts, shards, _, lanes = out_ref.shape
-    rows = ids_ref.shape[1]
-    ids = ids_ref[...]
+def slot_table(ids, shards, lanes=128):
+    rows = ids.shape[1]
     found = jnp.zeros((shards, lanes), F32)
     for k, rank in enumerate(ranks(ids, shards * 4)):
         block = ids[k : k + 1, :]
@@ -60,44 +58,15 @@
         target = jnp.where(iota((shards, rows), 0) == block // 4, other, 0.0).astype(BF)
         place = iota((lanes, rows), 0) == (block % 4) * CAP + rank
         found = found + dot_nt(target, jnp.where(place, 1.0, 0.0).astype(BF))
-    found = jnp.broadcast_to((found.astype(jnp.int32) - 1)[:, None, :], (shards, CAP, lanes))
-    for copy in range(parts):
-        out_ref[copy] = found
-
-
-def table(ids, parts, shards):
-    return pl.pallas_call(
-        table_kernel,
-        out_shape=jax.ShapeDtypeStruct((parts, shards, CAP, 128), jnp.int32),
-        compiler_params=params(),
-        cost_estimate=cost(2e7, 2**20),
-        name="slot_table",
-    )(ids)
-
-
-def names_kernel(table_ref, out_ref):
-    sources = table_ref.shape[0]
-    here = out_ref.shape[0] // sources
-    row = table_ref[:, 0:1, :].astype(F32)
-    shape = (sources, here, 128)
-    kept = jnp.where(iota(shape, 1) == iota(shape, 2), jnp.broadcast_to(row, shape), 0.0)
-    name = jnp.sum(kept, axis=2, keepdims=True)
-    out_ref[...] = jnp.broadcast_to(name, shape).reshape(sources * here, 128).astype(BF)
-
-
-def names(tables, here):
-    sources = tables.shape[0]
-    step = 16
-    return pl.pallas_call(
-        names_kernel,
-        grid=(sources // step,),
-        in_specs=[pl.BlockSpec((step, CAP, 128), lambda i: (i, 0, 0))],
-        out_specs=pl.BlockSpec((step * here, 128), lambda i: (i, 0)),
-        out_shape=jax.ShapeDtypeStruct((sources * here, 128), BF),
-        compiler_params=params(),
-        cost_estimate=cost(2e7, 2**21),
-        name="slot_names",
-    )(tables)
+    return found - 1.0
+
+
+def slot_names(table):
+    sources = table.shape[0]
+    shape = (sources, 32, 128)
+    row = jnp.concatenate([table, table], axis=1).astype(F32)
+    kept = jnp.where(iota(shape, 1) == iota(shape, 2), row, 0.0).astype(BF)
+    return dot(kept.reshape(sources * 32, 128), jnp.ones((128, 128), BF)).astype(BF)
 
 
 def route_kernel(ids_ref, resid_ref, bias_ref, out_ref, pick_ref):
@@ -171,6 +140,7 @@
 
 
 def activate_kernel(ids_ref, columns_ref, pre_ref, rows_ref, msg_ref):
+    shards = msg_ref.shape[1]
     packed = pre_ref.shape[1]
     rows = ids_ref.shape[1]
     slots = 2 * packed
@@ -197,18 +167,22 @@
     pick0 = jnp.where(slot == ids[0:1, :] * CAP + rank0, 1.0, 0.0).astype(BF)
     pick1 = jnp.where(slot == ids[1:2, :] * CAP + rank1, 1.0, 0.0).astype(BF)
     msg = (dot(pick0, straight) + dot(pick1, crossed)).astype(BF)
+    msg = msg.reshape(shards, slots // shards, 128)
+    table = slot_table(ids, shards)
+    table = jnp.broadcast_to(table[:, None, :], (shards, 16, 128)).astype(BF)
     for copy in range(msg_ref.shape[0]):
-        msg_ref[copy] = msg
-
-
-def activate(ids, columns, partial):
+        msg_ref[copy, :, : slots // shards, :] = msg
+        msg_ref[copy, :, slots // shards :, :] = table
+
+
+def activate(ids, columns, partial, shards):
     parts, packed, lanes = partial.shape
     rows = ids.shape[1]
     return pl.pallas_call(
         activate_kernel,
         out_shape=[
             jax.ShapeDtypeStruct((parts, rows, 2 * lanes), BF),
-            jax.ShapeDtypeStruct((parts, 2 * packed, lanes), BF),
+            jax.ShapeDtypeStruct((parts, shards, 2 * packed // shards + 16, lanes), BF),
         ],
         compiler_params=params(),
         cost_estimate=cost(8 * packed * rows * lanes, 3 * 2**20),
@@ -295,10 +269,10 @@
     )(acts, dec_all, own_dec, bias)
 
 
-def gate_kernel(scale, msg_ref, other_ref, gram_ref, own_gram_ref, proj_ref, out_ref):
-    count = msg_ref.shape[0]
-    twice = doubled(msg_ref[...])
-    names = other_ref[...]
+def gate_kernel(scale, msg_ref, gram_ref, own_gram_ref, proj_ref, out_ref):
+    count = msg_ref.shape[0] * 32
+    twice = doubled(msg_ref[:, :32, :].reshape(count, 128))
+    names = slot_names(msg_ref[:, 32:, :])
     zero = jnp.zeros((count, 128), BF)
     total = dot(own_expanded(twice[:, :128]), own_gram_ref[...])
     chunk = 1024
@@ -317,15 +291,15 @@
     out_ref[...] = ((jnp.concatenate(packed, axis=1) - proj_ref[...]) * scale).astype(BF)
 
 
-def gate_partial(scale, msg, other, gram, own_gram, proj):
-    count, lanes = msg.shape
+def gate_partial(scale, msg, gram, own_gram, proj):
+    sources, tall, lanes = msg.shape
+    count = sources * 32
     step = 512
     return pl.pallas_call(
         lambda *refs: gate_kernel(scale, *refs),
         grid=(count // step,),
         in_specs=[
-            pl.BlockSpec((step, lanes), lambda i: (i, 0)),
-            pl.BlockSpec((step, lanes), lambda i: (i, 0)),
+            pl.BlockSpec((step // 32, tall, lanes), lambda i: (i, 0, 0)),
             pl.BlockSpec(gram.shape, lambda i: (0, 0)),
             pl.BlockSpec(own_gram.shape, lambda i: (0, 0)),
             pl.BlockSpec((step // 32, 2 * CAP, 128), lambda i: (i, 0, 0)),
@@ -335,18 +309,19 @@
         compiler_params=params(),
         cost_estimate=cost(2 * count * gram.shape[0] * gram.shape[1], 10 * 2**20),
         name="gate_partial",
-    )(msg, other, gram, own_gram, proj)
-
-
-def mix_kernel(msg_ref, name_ref, dec_ref, own_dec_ref, out_ref, own_ref, twice_ref):
+    )(msg, gram, own_gram, proj)
+
+
+def mix_kernel(msg_ref, dec_ref, own_dec_ref, out_ref, own_ref, twice_ref, name_ref):
     at = pl.program_id(0)
-    count = msg_ref.shape[0]
+    count = msg_ref.shape[0] * 32
     chunk = dec_ref.shape[0]
 
     @pl.when(at == 0)
     def _():
-        twice = doubled(msg_ref[...])
+        twice = doubled(msg_ref[:, :32, :].reshape(count, 128))
         twice_ref[...] = twice[:, 128:]
+        name_ref[...] = slot_names(msg_ref[:, 32:, :])
         own = own_expanded(twice[:, :128])
         own_ref[...] = own.T
         out_ref[...] = dot(dot(own_ref[...], own).astype(BF), own_dec_ref[...])
@@ -360,16 +335,15 @@
     out_ref[...] += dot(mixed, dec_ref[...])
 
 
-def mix(msg, other, dec_all, own_dec):
-    count, lanes = msg.shape
+def mix(msg, dec_all, own_dec):
+    count = msg.shape[0] * 32
     latents, cols = dec_all.shape
     chunk = 512
     return pl.pallas_call(
         mix_kernel,
         grid=(latents // chunk,),
         in_specs=[
-            pl.BlockSpec(msg.shape, lambda i: (0, 0)),
-            pl.BlockSpec(other.shape, lambda i: (0, 0)),
+            pl.BlockSpec(msg.shape, lambda i: (0, 0, 0)),
             pl.BlockSpec((chunk, cols), lambda i: (i, 0)),
             pl.BlockSpec(own_dec.shape, lambda i: (0, 0)),
         ],
@@ -378,18 +352,19 @@
         scratch_shapes=[
             pltpu.VMEM((256, count), BF),
             pltpu.VMEM((count, 128), BF),
+            pltpu.VMEM((count, 128), BF),
         ],
         compiler_params=params(),
         cost_estimate=cost(2 * latents * 256 * (count + cols), 20 * 2**20),
         name="mix_decoder",
-    )(msg, other, dec_all, own_dec)
+    )(msg, dec_all, own_dec)
 
 
 def grads_kernel(scale, gate_ref, msg_ref, rows_ref, mixed_ref, enc_ref, dec_ref, acc_ref):
     at = pl.program_id(0)
-    count = msg_ref.shape[0]
-    sources = count // 32
-    own = own_expanded(doubled(msg_ref[...])[:, :128])
+    sources = msg_ref.shape[0]
+    count = sources * 32
+    own = own_expanded(doubled(msg_ref[:, :32, :].reshape(count, 128))[:, :128])
     total = gate_ref[0].astype(F32)
     for part in range(1, gate_ref.shape[0]):
         total = total + gate_ref[part].astype(F32)
@@ -418,7 +393,8 @@
 
 
 def grads(scale, gates, msg, rows, mixed):
-    count, lanes = msg.shape
+    sources, tall, lanes = msg.shape
+    count = sources * 32
     cols = rows.shape[1]
     step = 512
     shape = jax.ShapeDtypeStruct(mixed.shape, F32)
@@ -427,7 +403,7 @@
         grid=(count // step,),
         in_specs=[
             pl.BlockSpec((gates.shape[0], step // 32, 2 * CAP, 128), lambda i: (0, i, 0, 0)),
-            pl.BlockSpec((step, lanes), lambda i: (i, 0)),
+            pl.BlockSpec((step // 32, tall, lanes), lambda i: (i, 0, 0)),
             pl.BlockSpec((step, cols), lambda i: (i, 0)),
             pl.BlockSpec(mixed.shape, lambda i: (0, 0)),
         ],
@@ -456,9 +432,6 @@
     at_dict = lax.axis_index("dict")
 
     ids = block_ids.T
-    tables = lax.all_to_all(
-        table(ids, parts, shards).reshape(devices, CAP, 128), everyone, 0, 0, tiled=True
-    )
     outgoing = route(ids, resid, dec_b, parts, slots)
     arrived = lax.all_to_all(
         outgoing.reshape(devices, here * CAP, cols), everyone, 0, 0, tiled=True
@@ -468,7 +441,6 @@
     dec_x = lax.dynamic_slice(dec_w, (0, at_x * cols), (local, cols))
     bias_x = lax.dynamic_slice(dec_b, (at_x * cols,), (cols,)).reshape(1, cols)
     dec_all = lax.all_gather(dec_x, "dict", axis=0, tiled=True)
-    other = names(tables, here * CAP)
 
     weights = jnp.concatenate(
         [enc_x.reshape(2, 2 * LAT, cols), dec_x.reshape(2, 2 * LAT, cols)], axis=1
@@ -476,19 +448,21 @@
     bias = jnp.where(at_x == 0, enc_b, 0.0).reshape(2, 2 * LAT)
     pre, proj = encode(arrived, weights, bias)
     partial = lax.all_to_all(pre, everyone, 0, 0, tiled=True)
-    acts, msg = activate(ids, block_ids, partial.reshape(parts, shards * 2 * CAP, 128))
+    acts, msg = activate(ids, block_ids, partial.reshape(parts, shards * 2 * CAP, 128), shards)
     group_acts = lax.all_to_all(acts, "dp", 0, 0, tiled=True)
     message = lax.all_to_all(
-        msg.reshape(devices, here * CAP, 128), everyone, 0, 0, tiled=True
-    ).reshape(devices * here * CAP, 128)
+        msg.reshape(devices, here * CAP + 16, 128), everyone, 0, 0, tiled=True
+    )
 
     recon_x, gram = reconstruct(group_acts.reshape(parts * tok_rows, 256), dec_all, dec_x, bias_x)
-    recon = lax.all_to_all(recon_x, "dp", 0, 1, tiled=True)
+    recon = lax.all_to_all(recon_x, "dp", 0, 0, tiled=True)
 
     own_gram = lax.dynamic_slice(gram, (at_dict * local, 0), (local, local))
-    gate = gate_partial(scale, message, other, gram, own_gram, proj)
+    gate = gate_partial(scale, message, gram, own_gram, proj)
     gates = lax.all_gather(gate, "dp", axis=0, tiled=False)
-    mixed = mix(message, other, dec_all, dec_x)
+    later, recon, gate = lax.optimization_barrier((message, recon, gate))
+    mixed = mix(later, dec_all, dec_x)
+    recon = recon.reshape(parts, tok_rows, cols).transpose(1, 0, 2).reshape(tok_rows, width)
     enc_grad, dec_grad = grads(
         scale, gates, message, arrived.reshape(devices * here * CAP, cols), mixed
     )

time: 336 us -> 315 us (0.938)
  waiting for transfers between devices: 140 us -> 128 us
  starting transfers between devices: 44 us -> 38.3 us
  Pallas kernels: 121 us -> 116 us
  local copies, waits for them, and re-layouts: 12 us -> 15.9 us
    all_to_all x3 -> x2, waiting for transfers between devices: 16.9 us -> 0.72 us  [the longest x1 0.72 us: body(): recon = lax.all_to_all(recon_x, 'dp', 0, 0, tiled=True)]
    pallas_call x2 -> x0, Pallas kernels: 7.29 us -> none  [the longest x1 5.4 us: names(): pl.pallas_call(names_kernel, grid=(sources // step,), in_specs=[pl.BlockS...]
    all_to_all x3 -> x2, starting transfers between devices: 17.9 us -> 12.4 us  [the longest x1 8.26 us: body(): lax.all_to_all(msg.reshape(devices, here * CAP + 16, 128), everyone, 0, 0...]
    all_to_all x1, waiting for transfers between devices: 1.42 us -> 6.09 us  [body(): group_acts = lax.all_to_all(acts, 'dp', 0, 0, tiled=True)]
    unnamed x15 -> x18, local copies, waits for them, and re-layouts: 4.11 us -> 8.57 us
  transfers between devices with their start and end apart: 8 -> 7, of which waited for: 6 -> 4; matrix products, arithmetic and copies ran while one was open for 3% -> 4% of each run, Pallas kernels for 25% -> 33%
where the time goes in v3:
time: 315 us; the launch traced here: 314 us
  waiting for transfers between devices  128 us (41%)
  Pallas kernels  116 us (37%)
  starting transfers between devices  38.3 us (12%)
  local copies, waits for them, and re-layouts  15.9 us (5%)
  between operations  14.1 us (4%)
    all_to_all x1, waiting for transfers between devices, body(): lax.all_to_all(outgoing.reshape(devices, here * CAP, cols), everyone, 0,...  103 us
    pallas_call x1, Pallas kernels, mix(): pl.pallas_call(mix_kernel, grid=(latents // chunk,), in_specs=[pl.BlockSp...  31.3 us
    pallas_call x1, Pallas kernels, reconstruct(): pl.pallas_call(recon_kernel, grid=(latents // chunk,), in_specs=[pl.Block...  28.7 us
    pallas_call x1, Pallas kernels, gate_partial(): pl.pallas_call(lambda *refs: gate_kernel(scale, *refs), grid=(count // st...  25 us
    all_to_all x1, waiting for transfers between devices, body(): partial = lax.all_to_all(pre, everyone, 0, 0, tiled=True)  18.5 us
    pallas_call x1, Pallas kernels, grads(): pl.pallas_call(lambda *refs: grads_kernel(scale, *refs), grid=(count // s...  12.8 us
    all_to_all x1, starting transfers between devices, body(): lax.all_to_all(outgoing.reshape(devices, here * CAP, cols), everyone, 0,...  12 us
    all_to_all x1, starting transfers between devices, body(): partial = lax.all_to_all(pre, everyone, 0, 0, tiled=True)  10.4 us
  transfers between devices with their start and end apart: 7, of which 4 were waited for; matrix products, arithmetic and copies ran while one was open for 4% of the time, Pallas kernels for 33%

profile of v3, /device:TPU:1, one launch (start us, length us, event | category | flops | bytes accessed | tf_op | source)
XLA Modules:
  0.0 314.1 jit_solution(17520152004442145802)
XLA Ops:
  7.2 0.0 copy-start
  7.2 0.0 all-gather.4.cloned.1.call-start
  7.2 1.5 copy-done
  8.8 0.8 constant_dynamic-slice_fusion.1.own_dec_ref
  9.6 0.0 all-gather.4.cloned.1.call-update
  9.6 7.1 %route_rows.1 = bf16[4,1024,1024]{2,1,0:T(8,128)(2,1)} custom-call(s32[2,256]{1,0:T(2,128)} %bitcast.29, bf16[256,4096]{1,0:T(8,128)(2,1)} %resid_ref.1, f32[1,4096]{1,0:T(1,128)} %bitcast.28), custom_call_target="tpu_custom_call" | custom-call | flops 2147483648 | bytes 10485760 | tf_op jit(solution)/shard_map/route_rows/pallas_call | solution.py:93
  16.7 0.0 copy-start.2
  16.7 12.0 %all-to-all-start = ((bf16[128,32,1024]{2,1,0:T(8,128)(2,1)}), bf16[128,32,1024]{2,1,0:T(8,128)(2,1)}, u32[]{:S(2)}, u32[]{:S(2)}) async-start(bf16[128,32,1024]{2,1,0:T(8,128)(2,1)} %bitcast.19), calls=%async_computation | async-start | bytes 16777216 | tf_op jit(solution)/shard_map/all_to_all | solution.py:436
  28.7 0.0 copy-start.7
  28.7 1.1 constant_dynamic-slice_fusion.2
  29.8 0.0 copy-done.2
  29.8 1.0 pad_maximum_fusion.weight_ref
  30.8 0.0 copy-done.7
  30.8 0.6 select_bitcast_fusion.bias_ref
  31.4 103.0 %all-to-all-done.rows_ref = bf16[128,32,1024]{2,1,0:T(8,128)(2,1)} async-done(((bf16[128,32,1024]{2,1,0:T(8,128)(2,1)}), bf16[128,32,1024]{2,1,0:T(8,128)(2,1)}, u32[]{:S(2)}, u32[]{:S(2)}) %all-to-all-start) | async-done | bytes 8388640 | tf_op jit(solution)/shard_map/all_to_all | solution.py:436
  134.4 6.9 %encode_rows.1 = (f32[128,16,128]{2,1,0:T(8,128)}, f32[128,16,128]{2,1,0:T(8,128)}) custom-call(bf16[128,32,1024]{2,1,0:T(8,128)(2,1)} %all-to-all-done.rows_ref, bf16[2,256,1024]{2,1,0:T(8,128)(2,1)} %pad_maximum_fusion.weight_ref, f32[2,128]{1,0:T(2,128)} %select_bitcast_fusion.bias_ref), custom_call_target="tpu_custom_call" | custom-call | flops 2147483648 | bytes 11534336 | tf_op jit(solution)/shard_map/encode_rows/pallas_call | solution.py:126
  141.3 0.0 copy-start.6
  141.3 10.4 %all-to-all-start.1 = ((f32[128,16,128]{2,1,0:T(8,128)}), f32[128,16,128]{2,1,0:T(8,128)S(1)}, u32[]{:S(2)}, u32[]{:S(2)}) async-start(f32[128,16,128]{2,1,0:T(8,128)} %get-tuple-element.13), calls=%async_computation.1 | async-start | bytes 2097152 | tf_op jit(solution)/shard_map/all_to_all | solution.py:450
  151.7 0.0 copy-done.6
  151.7 0.8 copy.14.columns_ref
  152.5 18.5 %all-to-all-done.1 = f32[128,16,128]{2,1,0:T(8,128)S(1)} async-done(((f32[128,16,128]{2,1,0:T(8,128)}), f32[128,16,128]{2,1,0:T(8,128)S(1)}, u32[]{:S(2)}, u32[]{:S(2)}) %all-to-all-start.1) | async-done | bytes 1048608 | tf_op jit(solution)/shard_map/all_to_all | solution.py:450
  171.0 0.0 copy-start.3
  171.0 1.0 copy-done.3
  172.0 4.0 %activate_rows.1 = (bf16[4,256,256]{2,1,0:T(8,128)(2,1)}, bf16[4,32,48,128]{3,2,1,0:T(8,128)(2,1)}) custom-call(s32[2,256]{1,0:T(2,128)} %bitcast.30, s32[256,2]{1,0:T(8,128)} %copy.14.columns_ref, f32[4,512,128]{2,1,0:T(8,128)} %bitcast.23), custom_call_target="tpu_custom_call" | custom-call | flops 134217728 | bytes 3145728 | tf_op jit(solution)/shard_map/activate_rows/pallas_call | solution.py:181
  175.9 3.5 %all-to-all-start.3 = ((bf16[4,256,256]{2,1,0:T(8,128)(2,1)}), bf16[4,256,256]{2,1,0:T(8,128)(2,1)S(1)}, u32[]{:S(2)}, u32[]{:S(2)}) async-start(bf16[4,256,256]{2,1,0:T(8,128)(2,1)} %get-tuple-element.15), calls=%async_computation.3 | async-start | bytes 1048576 | tf_op jit(solution)/shard_map/all_to_all | solution.py:452
  179.4 1.3 dynamic_slice.14
  180.7 6.1 %all-to-all-done.3 = bf16[4,256,256]{2,1,0:T(8,128)(2,1)S(1)} async-done(((bf16[4,256,256]{2,1,0:T(8,128)(2,1)}), bf16[4,256,256]{2,1,0:T(8,128)(2,1)S(1)}, u32[]{:S(2)}, u32[]{:S(2)}) %all-to-all-start.3) | async-done | bytes 524320 | tf_op jit(solution)/shard_map/all_to_all | solution.py:452
  186.8 0.0 copy-start.5
  186.8 8.3 %all-to-all-start.2 = ((bf16[128,48,128]{2,1,0:T(8,128)(2,1)}), bf16[128,48,128]{2,1,0:T(8,128)(2,1)S(1)}, u32[]{:S(2)}, u32[]{:S(2)}) async-start(bf16[128,48,128]{2,1,0:T(8,128)(2,1)} %bitcast.26), calls=%async_computation.2 | async-start | bytes 3145728 | tf_op jit(solution)/shard_map/all_to_all | solution.py:453
  195.1 0.0 all-gather.4.cloned.1.call-done.dec_ref
  195.1 0.0 copy-done.5
  195.1 28.7 %reconstruct_rows.1 = (bf16[1024,1024]{1,0:T(8,128)(2,1)}, bf16[8192,256]{1,0:T(8,128)(2,1)}) custom-call(bf16[1024,256]{1,0:T(8,128)(2,1)} %bitcast.27, bf16[8192,1024]{1,0:T(8,128)(2,1)} %all-gather.4.cloned.1.call-done.dec_ref, bf16[256,1024]{1,0:T(8,128)(2,1)} %constant_dynamic-slice_fusion.1.own_dec_ref, f32[1,1024]{1,0:T(1,128)} %bitcast.31), custom_call_target="tpu_custom_call" | custom-call | flops 21474836480 | bytes 25165824 | tf_op jit(solution)/shard_map/reconstruct_rows/pallas_call | solution.py:243
  223.8 1.6 constant_dynamic-slice_fusion.refs_2_
  225.4 0.0 all-to-all-done.2.refs_0_.msg_ref.refs_1_
  225.4 0.0 copy-start.4
  225.4 1.2 copy-done.4
  226.5 4.2 %all-to-all-start.4 = ((bf16[4,256,1024]{2,1,0:T(8,128)(2,1)}), bf16[4,256,1024]{2,1,0:T(8,128)(2,1)S(1)}, u32[]{:S(2)}, u32[]{:S(2)}) async-start(bf16[4,256,1024]{2,1,0:T(8,128)(2,1)} %bitcast.24), calls=%async_computation.4 | async-start | bytes 4194304 | tf_op jit(solution)/shard_map/all_to_all | solution.py:458
  230.7 0.0 all-gather.6.cloned.1.call-start
  230.7 25.0 %gate_partial.1 = bf16[128,16,128]{2,1,0:T(8,128)(2,1)} custom-call(bf16[128,48,128]{2,1,0:T(8,128)(2,1)} %copy-done.4, bf16[8192,256]{1,0:T(8,128)(2,1)} %get-tuple-element.17.refs_1_, bf16[256,256]{1,0:T(8,128)(2,1)} %constant_dynamic-slice_fusion.refs_2_, f32[128,16,128]{2,1,0:T(8,128)} %get-tuple-element.18.refs_3_), custom_call_target="tpu_custom_call" | custom-call | flops 17179869184 | bytes 10485760 | tf_op jit(solution)/shard_map/gate_partial/pallas_call | solution.py:298
  255.7 0.0 all-gather.6.cloned.1.call-update
  255.8 0.7 all-to-all-done.4
  256.5 2.6 copy.15
  259.1 4.1 %copy.16 = bf16[256,4096]{1,0:T(8,128)(2,1)} copy(bf16[256,4096]{0,1:T(8,128)(2,1)} %bitcast.21) | data formatting | bytes 4194304
  263.1 31.3 %mix_decoder.1.refs_3_ = f32[256,1024]{1,0:T(8,128)} custom-call(bf16[128,48,128]{2,1,0:T(8,128)(2,1)} %copy-done.4, bf16[8192,1024]{1,0:T(8,128)(2,1)} %all-gather.4.cloned.1.call-done.dec_ref, bf16[256,1024]{1,0:T(8,128)(2,1)} %constant_dynamic-slice_fusion.1.own_dec_ref), custom_call_target="tpu_custom_call" | custom-call | flops 21474836480 | bytes 20971520 | tf_op jit(solution)/shard_map/mix_decoder/pallas_call | solution.py:342
  294.5 0.0 all-gather.6.cloned.1.call-done
  294.5 0.0 copy-start.1
  294.5 12.8 %dictionary_grads.1 = (f32[256,1024]{1,0:T(8,128)}, f32[256,1024]{1,0:T(8,128)}) custom-call(bf16[4,128,16,128]{3,2,1,0:T(8,128)(2,1)} %bitcast.32, bf16[128,48,128]{2,1,0:T(8,128)(2,1)} %copy-done.4, bf16[4096,1024]{1,0:T(8,128)(2,1)} %bitcast.16.refs_2_, f32[256,1024]{1,0:T(8,128)} %mix_decoder.1.refs_3_), custom_call_target="tpu_custom_call" | custom-call | flops 4294967296 | bytes 16777216 | tf_op jit(solution)/shard_map/dictionary_grads/pallas_call | solution.py:401
  307.3 0.0 copy-done.1
Async XLA Ops:
  7.2 1.6 copy-start
  7.2 187.9 %all-gather.4.cloned.1.call-start = ((), (), s32[]{:S(2)}) async-start(), calls=%async_computation.5 | async-start | bytes 17301504 | tf_op jit(solution)/shard_map/all_gather | solution.py:443
  16.7 13.1 %copy-start.2 = (bf16[256,1024]{1,0:T(8,128)(2,1)S(1)}, bf16[256,1024]{1,0:T(8,128)(2,1)}, u32[]{:S(2)}) copy-start(bf16[256,1024]{1,0:T(8,128)(2,1)} %constant_dynamic-slice_fusion.1.own_dec_ref) | copy-start | bytes 1572868
  16.7 117.7 %all-to-all-start = ((bf16[128,32,1024]{2,1,0:T(8,128)(2,1)}), bf16[128,32,1024]{2,1,0:T(8,128)(2,1)}, u32[]{:S(2)}, u32[]{:S(2)}) async-start(bf16[128,32,1024]{2,1,0:T(8,128)(2,1)} %bitcast.19), calls=%async_computation | async-start | bytes 16777216 | tf_op jit(solution)/shard_map/all_to_all | solution.py:436
  28.7 2.2 copy-start.7
  141.3 10.4 %copy-start.6 = (s32[256,2]{0,1:T(2,128)S(1)}, s32[256,2]{0,1:T(2,128)}, u32[]{:S(2)}) copy-start(s32[256,2]{0,1:T(2,128)} %param.7) | copy-start | bytes 6148
  141.3 29.7 %all-to-all-start.1 = ((f32[128,16,128]{2,1,0:T(8,128)}), f32[128,16,128]{2,1,0:T(8,128)S(1)}, u32[]{:S(2)}, u32[]{:S(2)}) async-start(f32[128,16,128]{2,1,0:T(8,128)} %get-tuple-element.13), calls=%async_computation.1 | async-start | bytes 2097152 | tf_op jit(solution)/shard_map/all_to_all | solution.py:450
  171.0 1.0 copy-start.3
  175.9 10.9 %all-to-all-start.3 = ((bf16[4,256,256]{2,1,0:T(8,128)(2,1)}), bf16[4,256,256]{2,1,0:T(8,128)(2,1)S(1)}, u32[]{:S(2)}, u32[]{:S(2)}) async-start(bf16[4,256,256]{2,1,0:T(8,128)(2,1)} %get-tuple-element.15), calls=%async_computation.3 | async-start | bytes 1048576 | tf_op jit(solution)/shard_map/all_to_all | solution.py:452
  186.8 8.3 %copy-start.5 = (bf16[4,256,256]{2,1,0:T(8,128)(2,1)}, bf16[4,256,256]{2,1,0:T(8,128)(2,1)S(1)}, u32[]{:S(2)}) copy-start(bf16[4,256,256]{2,1,0:T(8,128)(2,1)S(1)} %all-to-all-done.3) | copy-start | bytes 1572868
  186.8 38.6 %all-to-all-start.2 = ((bf16[128,48,128]{2,1,0:T(8,128)(2,1)}), bf16[128,48,128]{2,1,0:T(8,128)(2,1)S(1)}, u32[]{:S(2)}, u32[]{:S(2)}) async-start(bf16[128,48,128]{2,1,0:T(8,128)(2,1)} %bitcast.26), calls=%async_computation.2 | async-start | bytes 3145728 | tf_op jit(solution)/shard_map/all_to_all | solution.py:453
  225.4 1.2 copy-start.4
  226.5 29.9 %all-to-all-start.4 = ((bf16[4,256,1024]{2,1,0:T(8,128)(2,1)}), bf16[4,256,1024]{2,1,0:T(8,128)(2,1)S(1)}, u32[]{:S(2)}, u32[]{:S(2)}) async-start(bf16[4,256,1024]{2,1,0:T(8,128)(2,1)} %bitcast.24), calls=%async_computation.4 | async-start | bytes 4194304 | tf_op jit(solution)/shard_map/all_to_all | solution.py:458
  230.7 63.7 %all-gather.6.cloned.1.call-start = ((), (), s32[]{:S(2)}) async-start(), calls=%async_computation.6 | async-start | bytes 2621440 | tf_op jit(solution)/shard_map/all_gather | solution.py:462
  294.5 12.8 %copy-start.1 = (bf16[256,4096]{1,0:T(8,128)(2,1)S(1)}, bf16[256,4096]{1,0:T(8,128)(2,1)}, u32[]{:S(2)}) copy-start(bf16[256,4096]{1,0:T(8,128)(2,1)} %param.10) | copy-start | bytes 6291460
Sparse Core Ops, SparseCore 0:
  10.3 179.8 all-gather.3
  255.9 32.9 all-gather.5

commit v4 on v3

--- a/solution.py
+++ b/solution.py
@@ -1,3 +1,5 @@
+import functools
+
 import jax
 import jax.numpy as jnp
 from jax import lax
@@ -107,24 +109,25 @@
     )(ids, resid, dec_b.reshape(1, width))
 
 
-def encode_kernel(rows_ref, weight_ref, bias_ref, pre_ref, proj_ref):
+def encode_kernel(scale, rows_ref, weight_ref, bias_ref, pre_ref, proj_ref):
     count, _, cols = rows_ref.shape
+    projected = []
     low = iota((1, 1, 128), 2) < LAT
     for p in range(2):
         rows = rows_ref[:, p * 16 : (p + 1) * 16, :].reshape(count * 16, cols)
         both = dot_nt(rows, weight_ref[p]).reshape(count, 2, CAP, 256)
         pre = jnp.where(low, both[:, 0, :, :128], both[:, 1, :, :128])
         pre_ref[:, p * CAP : (p + 1) * CAP, :] = pre + bias_ref[p : p + 1, :][None]
-        proj = jnp.where(low, both[:, 0, :, 128:], both[:, 1, :, 128:])
-        proj_ref[:, p * CAP : (p + 1) * CAP, :] = proj
-
-
-def encode(arrived, weights, bias):
+        projected.append(jnp.where(low, both[:, 0, :, 128:], both[:, 1, :, 128:]) * scale)
+    proj_ref[...] = jnp.concatenate(projected, axis=1).astype(BF)
+
+
+def encode(scale, arrived, weights, bias):
     sources, here, cols = arrived.shape
     step = 32
-    shape = jax.ShapeDtypeStruct((sources, 2 * CAP, 128), F32)
-    return pl.pallas_call(
-        encode_kernel,
+    shape = (sources, 2 * CAP, 128)
+    return pl.pallas_call(
+        functools.partial(encode_kernel, scale),
         grid=(sources // step,),
         in_specs=[
             pl.BlockSpec((step, here, cols), lambda i: (i, 0, 0)),
@@ -132,14 +135,14 @@
             pl.BlockSpec(bias.shape, lambda i: (0, 0)),
         ],
         out_specs=[pl.BlockSpec((step, 2 * CAP, 128), lambda i: (i, 0, 0))] * 2,
-        out_shape=[shape, shape],
+        out_shape=[jax.ShapeDtypeStruct(shape, F32), jax.ShapeDtypeStruct(shape, BF)],
         compiler_params=params(),
         cost_estimate=cost(2 * sources * here * cols * 256, 11 * 2**20),
         name="encode_rows",
     )(arrived, weights, bias)
 
 
-def activate_kernel(ids_ref, columns_ref, pre_ref, rows_ref, msg_ref):
+def activate_kernel(ids_ref, pre_ref, group_ref, msg_ref):
     shards = msg_ref.shape[1]
     packed = pre_ref.shape[1]
     rows = ids_ref.shape[1]
@@ -159,11 +162,9 @@
     first, second = found
     straight = jnp.concatenate([first, second], axis=1).astype(BF)
     crossed = jnp.concatenate([second, first], axis=1).astype(BF)
-    lane = iota((rows, 128), 1)
-    named = jnp.where(lane == 0, columns_ref[:, 0:1], jnp.where(lane == 1, columns_ref[:, 1:2], 0))
-    group = jnp.concatenate([straight, named.astype(F32).astype(BF)], axis=1)
-    for copy in range(rows_ref.shape[0]):
-        rows_ref[copy] = group
+    group_ref[:packed, :] = acts
+    halves = [ids[:, :128], ids[:, 128:], jnp.zeros((12, 128), jnp.int32)]
+    group_ref[packed:, :] = jnp.concatenate(halves, axis=0).astype(F32).astype(BF)
     pick0 = jnp.where(slot == ids[0:1, :] * CAP + rank0, 1.0, 0.0).astype(BF)
     pick1 = jnp.where(slot == ids[1:2, :] * CAP + rank1, 1.0, 0.0).astype(BF)
     msg = (dot(pick0, straight) + dot(pick1, crossed)).astype(BF)
@@ -175,19 +176,19 @@
         msg_ref[copy, :, slots // shards :, :] = table
 
 
-def activate(ids, columns, partial, shards):
+def activate(ids, partial, shards):
     parts, packed, lanes = partial.shape
     rows = ids.shape[1]
     return pl.pallas_call(
         activate_kernel,
         out_shape=[
-            jax.ShapeDtypeStruct((parts, rows, 2 * lanes), BF),
+            jax.ShapeDtypeStruct((packed + 16, lanes), BF),
             jax.ShapeDtypeStruct((parts, shards, 2 * packed // shards + 16, lanes), BF),
         ],
         compiler_params=params(),
         cost_estimate=cost(8 * packed * rows * lanes, 3 * 2**20),
         name="activate_rows",
-    )(ids, columns, partial)
+    )(ids, partial)
 
 
 def doubled(pair):
@@ -207,109 +208,106 @@
     return jnp.where(mine, twice.astype(F32), 0.0).astype(BF)
 
 
-def recon_kernel(
-    acts_ref, dec_ref, own_dec_ref, bias_ref, out_ref, gram_ref, twice_ref, name0_ref, name1_ref, acc_ref
-):
-    at = pl.program_id(0)
-    rows = acts_ref.shape[0]
-    chunk = dec_ref.shape[0]
-
-    @pl.when(at == 0)
-    def _():
-        twice_ref[...] = doubled(acts_ref[:, :128])
-        ids = acts_ref[:, 128:].astype(F32)
-        name0_ref[...] = jnp.broadcast_to(ids[:, 0:1], (rows, 128)).astype(BF)
-        name1_ref[...] = jnp.broadcast_to(ids[:, 1:2], (rows, 128)).astype(BF)
-        acc_ref[...] = jnp.broadcast_to(bias_ref[...], acc_ref.shape)
-
-    spread = []
-    zero = jnp.zeros((rows, 128), BF)
-    for q in range(chunk // 128):
-        block = lane_block(at * (chunk // 128) + q)
-        one = jnp.where(name0_ref[...] == block, twice_ref[:, :128], zero)
-        spread.append(jnp.where(name1_ref[...] == block, twice_ref[:, 128:], one))
-    acc_ref[...] += dot(jnp.concatenate(spread, axis=1), dec_ref[...])
-    gram_ref[...] = dot_nt(dec_ref[...], own_dec_ref[...]).astype(BF)
-
-    @pl.when(at == pl.num_programs(0) - 1)
-    def _():
-        out_ref[...] = acc_ref[...].astype(BF)
-
-
-def reconstruct(acts, dec_all, own_dec, bias):
-    rows = acts.shape[0]
-    latents, cols = dec_all.shape
-    chunk = 1024
-    return pl.pallas_call(
-        recon_kernel,
-        grid=(latents // chunk,),
-        in_specs=[
-            pl.BlockSpec(acts.shape, lambda i: (0, 0)),
-            pl.BlockSpec((chunk, cols), lambda i: (i, 0)),
-            pl.BlockSpec(own_dec.shape, lambda i: (0, 0)),
-            pl.BlockSpec((1, cols), lambda i: (0, 0)),
-        ],
-        out_specs=[
-            pl.BlockSpec((rows, cols), lambda i: (0, 0)),
-            pl.BlockSpec((chunk, own_dec.shape[0]), lambda i: (i, 0)),
-        ],
-        out_shape=[
-            jax.ShapeDtypeStruct((rows, cols), BF),
-            jax.ShapeDtypeStruct((latents, own_dec.shape[0]), BF),
-        ],
-        scratch_shapes=[
-            pltpu.VMEM((rows, 256), BF),
-            pltpu.VMEM((rows, 128), BF),
-            pltpu.VMEM((rows, 128), BF),
-            pltpu.VMEM((rows, cols), F32),
-        ],
-        compiler_params=params(),
-        cost_estimate=cost(2 * latents * cols * (rows + own_dec.shape[0]), 24 * 2**20),
-        name="reconstruct_rows",
-    )(acts, dec_all, own_dec, bias)
-
-
-def gate_kernel(scale, msg_ref, gram_ref, own_gram_ref, proj_ref, out_ref):
-    count = msg_ref.shape[0] * 32
-    twice = doubled(msg_ref[:, :32, :].reshape(count, 128))
-    names = slot_names(msg_ref[:, 32:, :])
-    zero = jnp.zeros((count, 128), BF)
-    total = dot(own_expanded(twice[:, :128]), own_gram_ref[...])
-    chunk = 1024
-    for at in range(0, gram_ref.shape[0], chunk):
-        spread = [
-            jnp.where(names == lane_block(group), twice[:, 128:], zero)
-            for group in range(at // 128, (at + chunk) // 128)
-        ]
-        total = total + dot(jnp.concatenate(spread, axis=1), gram_ref[at : at + chunk, :])
-    total = total.reshape(count // 32, 4, CAP, 256)
+def spread(packed):
+    low = iota((1, 1, 128), 2) < LAT
+    zero = jnp.zeros((packed.shape[0], CAP, 128), F32)
+    rows = []
+    for p in range(2):
+        piece = packed[:, p * CAP : (p + 1) * CAP, :]
+        for q in range(2):
+            kept = jnp.where(low if q == 0 else ~low, piece, 0.0)
+            rows.append(jnp.concatenate([kept, zero] if p == 0 else [zero, kept], axis=2))
+    return jnp.concatenate(rows, axis=1).reshape(packed.shape[0] * 32, 256)
+
+
+def gathered(wide):
+    wide = wide.reshape(wide.shape[0] // 32, 4, CAP, 256)
     low = iota((1, 1, 128), 2) < LAT
     packed = []
     for p in range(2):
         lanes = slice(p * 128, (p + 1) * 128)
-        packed.append(jnp.where(low, total[:, 2 * p, :, lanes], total[:, 2 * p + 1, :, lanes]))
-    out_ref[...] = ((jnp.concatenate(packed, axis=1) - proj_ref[...]) * scale).astype(BF)
-
-
-def gate_partial(scale, msg, gram, own_gram, proj):
-    sources, tall, lanes = msg.shape
-    count = sources * 32
-    step = 512
-    return pl.pallas_call(
-        lambda *refs: gate_kernel(scale, *refs),
-        grid=(count // step,),
-        in_specs=[
-            pl.BlockSpec((step // 32, tall, lanes), lambda i: (i, 0, 0)),
-            pl.BlockSpec(gram.shape, lambda i: (0, 0)),
-            pl.BlockSpec(own_gram.shape, lambda i: (0, 0)),
-            pl.BlockSpec((step // 32, 2 * CAP, 128), lambda i: (i, 0, 0)),
-        ],
-        out_specs=pl.BlockSpec((step // 32, 2 * CAP, 128), lambda i: (i, 0, 0)),
-        out_shape=jax.ShapeDtypeStruct(proj.shape, BF),
-        compiler_params=params(),
-        cost_estimate=cost(2 * count * gram.shape[0] * gram.shape[1], 10 * 2**20),
-        name="gate_partial",
-    )(msg, gram, own_gram, proj)
+        packed.append(jnp.where(low, wide[:, 2 * p, :, lanes], wide[:, 2 * p + 1, :, lanes]))
+    return jnp.concatenate(packed, axis=1)
+
+
+def home_kernel(scale, *refs):
+    group, (dec_ref, bias_ref, recon_ref, gate_ref, pick_ref, part_ref) = refs[:4], refs[4:]
+    at = pl.program_id(0)
+    steps = pl.num_programs(0) // 2
+    slots, rows = pick_ref.shape[1:]
+    packed = slots // 2
+    per = dec_ref.shape[0] // 256
+
+    @pl.when(at == 0)
+    def _():
+        slot = iota((slots, rows), 0)
+        for d in range(4):
+            halves = group[d][packed:, :].astype(F32).astype(jnp.int32)
+            ids = jnp.concatenate([halves[0:2], halves[2:4]], axis=1)
+            rank0, rank1 = ranks(ids, slots // CAP)
+            here = (slot == ids[0:1, :] * CAP + rank0) | (slot == ids[1:2, :] * CAP + rank1)
+            pick_ref[d] = jnp.where(here, 1.0, 0.0).astype(BF)
+
+    @pl.when(at < steps)
+    def _():
+        for g in range(per):
+            shard = at * per + g
+            source = pl.ds(pl.multiple_of(shard * 16, 16), 16)
+            target = pl.ds(pl.multiple_of(shard * 32, 32), 32)
+            acts = jnp.stack([group[d][source, :].astype(F32) for d in range(4)])
+            part = dot(spread(acts).astype(BF), dec_ref[g * 256 : (g + 1) * 256, :]).astype(BF)
+            for d in range(4):
+                part_ref[d, target, :] = part[d * 32 : (d + 1) * 32]
+
+    @pl.when(at == steps)
+    def _():
+        for d in range(4):
+            total = dot_tn(pick_ref[d], part_ref[d])
+            recon_ref[d * rows : (d + 1) * rows, :] = (total + bias_ref[...]).astype(BF)
+            part_ref[d] = dot(pick_ref[d], total.astype(BF)).astype(BF)
+
+    @pl.when(at >= steps)
+    def _():
+        for g in range(per):
+            shard = (at - steps) * per + g
+            source = pl.ds(pl.multiple_of(shard * 32, 32), 32)
+            total = jnp.concatenate([part_ref[d, source, :] for d in range(4)], axis=0)
+            wide = dot_nt(total, dec_ref[g * 256 : (g + 1) * 256, :])
+            gate_ref[:, pl.ds(pl.multiple_of(g * 16, 16), 16), :] = (gathered(wide) * scale).astype(BF)
+
+
+def home(scale, group, dec_all, bias):
+    latents, cols = dec_all.shape
+    tall, lanes = group[0].shape
+    packed = tall - 16
+    rows = 256
+    chunk = 1024
+    steps = latents // chunk
+    per = chunk // 256
+    return pl.pallas_call(
+        functools.partial(home_kernel, scale),
+        grid=(2 * steps,),
+        in_specs=[pl.BlockSpec((tall, lanes), lambda i: (0, 0))] * 4
+        + [
+            pl.BlockSpec((chunk, cols), lambda i: (i % steps, 0)),
+            pl.BlockSpec((1, cols), lambda i: (0, 0)),
+        ],
+        out_specs=[
+            pl.BlockSpec((4 * rows, cols), lambda i: (0, 0)),
+            pl.BlockSpec((4, 16 * per, lanes), lambda i: (0, jnp.maximum(i - steps, 0), 0)),
+        ],
+        out_shape=[
+            jax.ShapeDtypeStruct((4 * rows, cols), BF),
+            jax.ShapeDtypeStruct((4, packed, lanes), BF),
+        ],
+        scratch_shapes=[
+            pltpu.VMEM((4, 2 * packed, rows), BF),
+            pltpu.VMEM((4, 2 * packed, cols), BF),
+        ],
+        compiler_params=params(),
+        cost_estimate=cost(8 * latents * cols * 128, 36 * 2**20),
+        name="home_rows",
+    )(*group, dec_all, bias)
 
 
 def mix_kernel(msg_ref, dec_ref, own_dec_ref, out_ref, own_ref, twice_ref, name_ref):
@@ -360,25 +358,15 @@
     )(msg, dec_all, own_dec)
 
 
-def grads_kernel(scale, gate_ref, msg_ref, rows_ref, mixed_ref, enc_ref, dec_ref, acc_ref):
+def grads_kernel(scale, gate_ref, proj_ref, msg_ref, rows_ref, mixed_ref, enc_ref, dec_ref, acc_ref):
     at = pl.program_id(0)
     sources = msg_ref.shape[0]
     count = sources * 32
     own = own_expanded(doubled(msg_ref[:, :32, :].reshape(count, 128))[:, :128])
-    total = gate_ref[0].astype(F32)
-    for part in range(1, gate_ref.shape[0]):
-        total = total + gate_ref[part].astype(F32)
-    low = iota((1, 1, 128), 2) < LAT
-    zero = jnp.zeros((sources, CAP, 128), F32)
-    spread = []
-    for p in range(2):
-        piece = total[:, p * CAP : (p + 1) * CAP, :]
-        for even in (True, False):
-            kept = jnp.where(low if even else ~low, piece, 0.0)
-            pair = [kept, zero] if p == 0 else [zero, kept]
-            spread.append(jnp.concatenate(pair, axis=2))
-    wide = jnp.concatenate(spread, axis=1).reshape(count, 256)
-    wide = jnp.where(own.astype(F32) > 0, wide, 0.0).astype(BF)
+    total = gate_ref[...].astype(F32)
+    for part in range(proj_ref.shape[0]):
+        total = total - proj_ref[part].astype(F32)
+    wide = jnp.where(own.astype(F32) > 0, spread(total), 0.0).astype(BF)
 
     @pl.when(at == 0)
     def _():
@@ -392,7 +380,7 @@
         dec_ref[...] = (mixed_ref[...] - acc_ref[256:, :]) * scale
 
 
-def grads(scale, gates, msg, rows, mixed):
+def grads(scale, gate, proj, msg, rows, mixed):
     sources, tall, lanes = msg.shape
     count = sources * 32
     cols = rows.shape[1]
@@ -402,7 +390,8 @@
         lambda *refs: grads_kernel(scale, *refs),
         grid=(count // step,),
         in_specs=[
-            pl.BlockSpec((gates.shape[0], step // 32, 2 * CAP, 128), lambda i: (0, i, 0, 0)),
+            pl.BlockSpec((step // 32, 2 * CAP, 128), lambda i: (i, 0, 0)),
+            pl.BlockSpec((proj.shape[0], step // 32, 2 * CAP, 128), lambda i: (0, i, 0, 0)),
             pl.BlockSpec((step // 32, tall, lanes), lambda i: (i, 0, 0)),
             pl.BlockSpec((step, cols), lambda i: (i, 0)),
             pl.BlockSpec(mixed.shape, lambda i: (0, 0)),
@@ -413,7 +402,13 @@
         compiler_params=params(),
         cost_estimate=cost(4 * count * cols * 256, 16 * 2**20),
         name="dictionary_grads",
-    )(gates, msg, rows, mixed)
+    )(gate, proj, msg, rows, mixed)
+
+
+def shifted(value, by, parts):
+    if by == 0:
+        return value
+    return lax.ppermute(value, "dp", [(i, (i + by) % parts) for i in range(parts)])
 
 
 def body(resid, block_ids, enc_w, enc_b, dec_w, dec_b):
@@ -429,7 +424,6 @@
     blocks = here * shards
     scale = (blocks / (tok_rows * devices * block_ids.shape[1])) ** 0.5
     at_x = lax.axis_index("dp")
-    at_dict = lax.axis_index("dict")
 
     ids = block_ids.T
     outgoing = route(ids, resid, dec_b, parts, slots)
@@ -446,25 +440,31 @@
         [enc_x.reshape(2, 2 * LAT, cols), dec_x.reshape(2, 2 * LAT, cols)], axis=1
     )
     bias = jnp.where(at_x == 0, enc_b, 0.0).reshape(2, 2 * LAT)
-    pre, proj = encode(arrived, weights, bias)
+    pre, proj = encode(scale, arrived, weights, bias)
     partial = lax.all_to_all(pre, everyone, 0, 0, tiled=True)
-    acts, msg = activate(ids, block_ids, partial.reshape(parts, shards * 2 * CAP, 128), shards)
-    group_acts = lax.all_to_all(acts, "dp", 0, 0, tiled=True)
+    projs = lax.all_gather(proj, "dp", axis=0, tiled=False)
+    acts, msg = activate(ids, partial.reshape(parts, shards * 2 * CAP, 128), shards)
+    group = [shifted(acts, d, parts) for d in range(parts)]
     message = lax.all_to_all(
         msg.reshape(devices, here * CAP + 16, 128), everyone, 0, 0, tiled=True
     )
 
-    recon_x, gram = reconstruct(group_acts.reshape(parts * tok_rows, 256), dec_all, dec_x, bias_x)
-    recon = lax.all_to_all(recon_x, "dp", 0, 0, tiled=True)
-
-    own_gram = lax.dynamic_slice(gram, (at_dict * local, 0), (local, local))
-    gate = gate_partial(scale, message, gram, own_gram, proj)
-    gates = lax.all_gather(gate, "dp", axis=0, tiled=False)
-    later, recon, gate = lax.optimization_barrier((message, recon, gate))
-    mixed = mix(later, dec_all, dec_x)
-    recon = recon.reshape(parts, tok_rows, cols).transpose(1, 0, 2).reshape(tok_rows, width)
+    recon_x, gate = home(scale, group, dec_all, bias_x)
+    total = gate[0].astype(F32)
+    for d in range(1, parts):
+        total = total + shifted(gate[d], -d, parts).astype(F32)
+    total = total.astype(BF).reshape(1, shards, 2 * CAP, 128)
+    total = jnp.broadcast_to(total, (parts, shards, 2 * CAP, 128))
+    gates = lax.all_to_all(total.reshape(devices, 2 * CAP, 128), everyone, 0, 0, tiled=True)
+
+    recon = jnp.zeros((tok_rows, width), BF)
+    for d in range(parts):
+        piece = shifted(recon_x[d * tok_rows : (d + 1) * tok_rows], -d, parts)
+        recon = lax.dynamic_update_slice(recon, piece, (0, ((at_x + d) % parts) * cols))
+
+    mixed = mix(message, dec_all, dec_x)
     enc_grad, dec_grad = grads(
-        scale, gates, message, arrived.reshape(devices * here * CAP, cols), mixed
+        scale, gates, projs, message, arrived.reshape(devices * here * CAP, cols), mixed
     )
     return (recon, enc_grad, dec_grad)
 

time: 315 us -> 298 us (0.946)
  blocking collectives: 0 us -> 31 us
  Pallas kernels: 116 us -> 89.6 us
  waiting for transfers between devices: 128 us -> 107 us
    all_to_all x0 -> x1, blocking collectives: none -> 31 us  [body(): partial = lax.all_to_all(pre, everyone, 0, 0, tiled=True)]
    pallas_call x4 -> x3, Pallas kernels: 64.5 us -> 38.3 us  [the longest x1 27.7 us: home(): pl.pallas_call(functools.partial(home_kernel, scale), grid=(2 * steps,),...]
    all_to_all x3 -> x1, waiting for transfers between devices: 25.3 us -> 0.01 us  [body(): lax.all_to_all(total.reshape(devices, 2 * CAP, 128), everyone, 0, 0, tile...]
    all_to_all x3 -> x1, starting transfers between devices: 18.1 us -> 7.4 us  [body(): lax.all_to_all(total.reshape(devices, 2 * CAP, 128), everyone, 0, 0, tile...]
    ppermute x0 -> x9, starting transfers between devices: none -> 10.3 us  [shifted(): lax.ppermute(value, 'dp', [(i, (i + by) % parts) for i in range(parts)])]
    unnamed x18 -> x14, local copies, waits for them, and re-layouts: 8.57 us -> 1.57 us
    dynamic_update_slice x0 -> x3, local copies, waits for them, and re-layouts: none -> 5.61 us  [body(): lax.dynamic_update_slice(recon, piece, (0, (at_x + d) % parts * cols))]
  transfers between devices with their start and end apart: 7 -> 14, of which waited for: 4 -> 3; matrix products, arithmetic and copies ran while one was open for 4% -> 5% of each run, Pallas kernels for 33% -> 26%
where the time goes in v4:
time: 298 us; the launch traced here: 297 us
  waiting for transfers between devices  107 us (36%)
  Pallas kernels  89.6 us (30%)
  starting transfers between devices  37.5 us (13%)
  blocking collectives  31 us (10%)
  local copies, waits for them, and re-layouts  15.3 us (5%)
  between operations  14.2 us (5%)
    all_to_all x1, waiting for transfers between devices, body(): lax.all_to_all(outgoing.reshape(devices, here * CAP, cols), everyone, 0,...  102 us
    pallas_call x1, Pallas kernels, mix(): pl.pallas_call(mix_kernel, grid=(latents // chunk,), in_specs=[pl.BlockSp...  31.3 us
    all_to_all x1, blocking collectives, body(): partial = lax.all_to_all(pre, everyone, 0, 0, tiled=True)  31 us
    pallas_call x1, Pallas kernels, home(): pl.pallas_call(functools.partial(home_kernel, scale), grid=(2 * steps,),...  27.7 us
    pallas_call x1, Pallas kernels, grads(): pl.pallas_call(lambda *refs: grads_kernel(scale, *refs), grid=(count // s...  12.8 us
    all_to_all x1, starting transfers between devices, body(): lax.all_to_all(outgoing.reshape(devices, here * CAP, cols), everyone, 0,...  12 us
    ppermute x9, starting transfers between devices, shifted(): lax.ppermute(value, 'dp', [(i, (i + by) % parts) for i in range(parts)])  10.3 us
    all_to_all x1, starting transfers between devices, body(): lax.all_to_all(msg.reshape(devices, here * CAP + 16, 128), everyone, 0, 0...  7.75 us
  transfers between devices with their start and end apart: 14, of which 3 were waited for; matrix products, arithmetic and copies ran while one was open for 5% of the time, Pallas kernels for 26%

profile of v4, /device:TPU:1, one launch (start us, length us, event | category | flops | bytes accessed | tf_op | source)
XLA Modules:
  0.0 297.2 jit_solution(9819463370764773169)
XLA Ops:
  7.2 0.0 copy-start
  7.2 0.0 all-gather.4.cloned.1.call-start
  7.2 1.5 copy-done
  8.8 0.9 constant_dynamic-slice_fusion.own_dec_ref
  9.7 0.0 all-gather.4.cloned.1.call-update
  9.7 7.1 %route_rows.1 = bf16[4,1024,1024]{2,1,0:T(8,128)(2,1)} custom-call(s32[2,256]{1,0:T(2,128)} %bitcast.30, bf16[256,4096]{1,0:T(8,128)(2,1)} %resid_ref.1, f32[1,4096]{1,0:T(1,128)} %bitcast.29), custom_call_target="tpu_custom_call" | custom-call | flops 2147483648 | bytes 10485760 | tf_op jit(solution)/shard_map/route_rows/pallas_call | solution.py:95
  16.8 12.0 %all-to-all-start = ((bf16[128,32,1024]{2,1,0:T(8,128)(2,1)}), bf16[128,32,1024]{2,1,0:T(8,128)(2,1)}, u32[]{:S(2)}, u32[]{:S(2)}) async-start(bf16[128,32,1024]{2,1,0:T(8,128)(2,1)} %bitcast.23), calls=%async_computation | async-start | bytes 16777216 | tf_op jit(solution)/shard_map/all_to_all | solution.py:430
  28.7 0.0 copy-start.3
  28.7 0.0 all-gather.6.cloned.1.call-start
  28.8 1.1 constant_dynamic-slice_fusion.1
  29.9 1.0 pad_maximum_fusion.weight_ref
  30.9 0.6 select_bitcast_fusion.bias_ref
  31.5 101.8 %all-to-all-done.rows_ref = bf16[128,32,1024]{2,1,0:T(8,128)(2,1)} async-done(((bf16[128,32,1024]{2,1,0:T(8,128)(2,1)}), bf16[128,32,1024]{2,1,0:T(8,128)(2,1)}, u32[]{:S(2)}, u32[]{:S(2)}) %all-to-all-start) | async-done | bytes 8388640 | tf_op jit(solution)/shard_map/all_to_all | solution.py:430
  133.3 6.8 %encode_rows.1 = (f32[128,16,128]{2,1,0:T(8,128)}, bf16[128,16,128]{2,1,0:T(8,128)(2,1)}) custom-call(bf16[128,32,1024]{2,1,0:T(8,128)(2,1)} %all-to-all-done.rows_ref, bf16[2,256,1024]{2,1,0:T(8,128)(2,1)} %pad_maximum_fusion.weight_ref, f32[2,128]{1,0:T(2,128)} %select_bitcast_fusion.bias_ref), custom_call_target="tpu_custom_call" | custom-call | flops 2147483648 | bytes 11534336 | tf_op jit(solution)/shard_map/encode_rows/pallas_call | solution.py:129
  140.0 31.0 %all_to_all.20 = f32[128,16,128]{2,1,0:T(8,128)} all-to-all(f32[128,16,128]{2,1,0:T(8,128)} %get-tuple-element.11), channel_id=1, replica_groups=mesh['dp'=4,'dict'=32] {'dp','dict'}, dimensions={0} | all-to-all | bytes 2097152 | tf_op jit(solution)/shard_map/all_to_all | solution.py:444
  171.1 3.9 %activate_rows.1 = (bf16[528,128]{1,0:T(8,128)(2,1)}, bf16[4,32,48,128]{3,2,1,0:T(8,128)(2,1)}) custom-call(s32[2,256]{1,0:T(2,128)} %bitcast.31, f32[4,512,128]{2,1,0:T(8,128)} %bitcast.25), custom_call_target="tpu_custom_call" | custom-call | flops 134217728 | bytes 3145728 | tf_op jit(solution)/shard_map/activate_rows/pallas_call | solution.py:182
  175.0 0.4 collective-permute-start
  175.4 2.3 collective-permute-start.1
  177.7 0.7 collective-permute-start.2
  178.4 1.3 dynamic_slice.11
  179.7 0.0 all-gather.6.cloned.1.call-update
  179.7 7.8 %all-to-all-start.3 = ((bf16[128,48,128]{2,1,0:T(8,128)(2,1)}), bf16[128,48,128]{2,1,0:T(8,128)(2,1)}, u32[]{:S(2)}, u32[]{:S(2)}) async-start(bf16[128,48,128]{2,1,0:T(8,128)(2,1)} %bitcast.27), calls=%async_computation.3 | async-start | bytes 3145728 | tf_op jit(solution)/shard_map/all_to_all | solution.py:448
  187.5 0.0 copy-start.4
  187.5 0.0 collective-permute-done.1.refs_2_
  187.5 0.0 collective-permute-done.2.refs_3_
  187.5 2.7 all-gather.4.cloned.1.call-done.refs_4_.dec_ref
  190.2 27.7 %home_rows.1 = (bf16[1024,1024]{1,0:T(8,128)(2,1)}, bf16[4,512,128]{2,1,0:T(8,128)(2,1)}) custom-call(bf16[528,128]{1,0:T(8,128)(2,1)} %get-tuple-element.12.refs_0_, bf16[528,128]{1,0:T(8,128)(2,1)} %copy-done.4, bf16[528,128]{1,0:T(8,128)(2,1)} %copy-done.5, bf16[528,128]{1,0:T(8,128)(2,1)} %copy-done.6, ...), custom_call_target="tpu_custom_call" | custom-call | flops 8589934592 | bytes 37748736 | tf_op jit(solution)/shard_map/home_rows/pallas_call | solution.py:287
  217.9 1.2 slice_bitcast_fusion.2
  219.1 2.5 collective-permute-start.6
  221.6 0.5 collective-permute-start.7
  222.1 0.6 collective-permute-start.8
  222.7 1.6 broadcast_in_dim.14
  224.3 1.2 fusion.3
  225.5 2.1 collective-permute-start.3
  227.5 1.3 collective-permute-start.4
  228.8 0.0 collective-permute-done.6
  228.8 0.0 collective-permute-start.5
  228.8 0.0 collective-permute-done.7
  228.8 2.5 collective-permute-done.8
  231.3 1.0 fusion.2
  232.3 0.0 all-to-all-done.3.msg_ref.refs_2_
  232.3 0.9 broadcast_in_dim.17
  233.2 7.4 %all-to-all-start.2 = ((bf16[128,16,128]{2,1,0:T(8,128)(2,1)}), bf16[128,16,128]{2,1,0:T(8,128)(2,1)}, u32[]{:S(2)}, u32[]{:S(2)}) async-start(bf16[128,16,128]{2,1,0:T(8,128)(2,1)} %bitcast.13), calls=%async_computation.2 | async-start | bytes 1048576 | tf_op jit(solution)/shard_map/all_to_all | solution.py:458
  240.6 31.3 %mix_decoder.1.refs_4_ = f32[256,1024]{1,0:T(8,128)} custom-call(bf16[128,48,128]{2,1,0:T(8,128)(2,1)} %all-to-all-done.3.msg_ref.refs_2_, bf16[8192,1024]{1,0:T(8,128)(2,1)} %all-gather.4.cloned.1.call-done.refs_4_.dec_ref, bf16[256,1024]{1,0:T(8,128)(2,1)} %constant_dynamic-slice_fusion.own_dec_ref), custom_call_target="tpu_custom_call" | custom-call | flops 21474836480 | bytes 20971520 | tf_op jit(solution)/shard_map/mix_decoder/pallas_call | solution.py:340
  271.9 1.9 constant_dynamic-update-slice_fusion.2
  273.8 1.9 constant_dynamic-update-slice_fusion.1
  275.7 1.9 constant_dynamic-update-slice_fusion
  277.5 12.8 %dictionary_grads.1 = (f32[256,1024]{1,0:T(8,128)}, f32[256,1024]{1,0:T(8,128)}) custom-call(bf16[128,16,128]{2,1,0:T(8,128)(2,1)} %all-to-all-done.2.refs_0_, bf16[4,128,16,128]{3,2,1,0:T(8,128)(2,1)} %bitcast.33, bf16[128,48,128]{2,1,0:T(8,128)(2,1)} %all-to-all-done.3.msg_ref.refs_2_, bf16[4096,1024]{1,0:T(8,128)(2,1)} %bitcast.16.refs_3_, ...), custom_call_target="tpu_custom_call" | custom-call | flops 4294967296 | bytes 16777216 | tf_op jit(solution)/shard_map/dictionary_grads/pallas_call | solution.py:389
  (16 shorter events, 0.0 us)
Async XLA Ops:
  7.2 1.6 copy-start
  7.2 183.1 %all-gather.4.cloned.1.call-start = ((), (), s32[]{:S(2)}) async-start(), calls=%async_computation.4 | async-start | bytes 17301504 | tf_op jit(solution)/shard_map/all_gather | solution.py:437
  16.7 13.1 %copy-start.1 = (bf16[256,1024]{1,0:T(8,128)(2,1)S(1)}, bf16[256,1024]{1,0:T(8,128)(2,1)}, u32[]{:S(2)}) copy-start(bf16[256,1024]{1,0:T(8,128)(2,1)} %constant_dynamic-slice_fusion.own_dec_ref) | copy-start | bytes 1572868
  16.8 116.5 %all-to-all-start = ((bf16[128,32,1024]{2,1,0:T(8,128)(2,1)}), bf16[128,32,1024]{2,1,0:T(8,128)(2,1)}, u32[]{:S(2)}, u32[]{:S(2)}) async-start(bf16[128,32,1024]{2,1,0:T(8,128)(2,1)} %bitcast.23), calls=%async_computation | async-start | bytes 16777216 | tf_op jit(solution)/shard_map/all_to_all | solution.py:430
  28.7 2.2 copy-start.3
  28.7 248.8 %all-gather.6.cloned.1.call-start = ((), (), s32[]{:S(2)}) async-start(), calls=%async_computation.5 | async-start | bytes 2621440 | tf_op jit(solution)/shard_map/all_gather | solution.py:445
  175.0 12.5 %collective-permute-start = (bf16[528,128]{1,0:T(8,128)(2,1)}, bf16[528,128]{1,0:T(8,128)(2,1)S(1)}, u32[]{:S(2)}, u32[]{:S(2)}) collective-permute-start(bf16[528,128]{1,0:T(8,128)(2,1)} %get-tuple-element.12.refs_0_), channel_id=1, source_target_pairs={{0,32},{32,64},{64,96},{96,0},{1,33},{33,65},{65,97},{97,1},{2,34}... | collective-permute-start | bytes 405512 | tf_op jit(solution)/shard_map/ppermute | solution.py:411
  175.4 12.1 %collective-permute-start.1 = (bf16[528,128]{1,0:T(8,128)(2,1)}, bf16[528,128]{1,0:T(8,128)(2,1)S(1)}, u32[]{:S(2)}, u32[]{:S(2)}) collective-permute-start(bf16[528,128]{1,0:T(8,128)(2,1)} %get-tuple-element.12.refs_0_), channel_id=1, source_target_pairs={{0,64},{32,96},{64,0},{96,32},{1,65},{33,97},{65,1},{97,33},{2,66}... | collective-permute-start | bytes 405512 | tf_op jit(solution)/shard_map/ppermute | solution.py:411
  177.7 9.8 %collective-permute-start.2 = (bf16[528,128]{1,0:T(8,128)(2,1)}, bf16[528,128]{1,0:T(8,128)(2,1)S(1)}, u32[]{:S(2)}, u32[]{:S(2)}) collective-permute-start(bf16[528,128]{1,0:T(8,128)(2,1)} %get-tuple-element.12.refs_0_), channel_id=1, source_target_pairs={{0,96},{32,0},{64,32},{96,64},{1,97},{33,1},{65,33},{97,65},{2,98}... | collective-permute-start | bytes 405512 | tf_op jit(solution)/shard_map/ppermute | solution.py:411
  179.7 52.6 %all-to-all-start.3 = ((bf16[128,48,128]{2,1,0:T(8,128)(2,1)}), bf16[128,48,128]{2,1,0:T(8,128)(2,1)}, u32[]{:S(2)}, u32[]{:S(2)}) async-start(bf16[128,48,128]{2,1,0:T(8,128)(2,1)} %bitcast.27), calls=%async_computation.3 | async-start | bytes 3145728 | tf_op jit(solution)/shard_map/all_to_all | solution.py:448
  187.5 2.8 copy-start.4
  187.5 2.7 copy-start.5
  187.5 2.7 copy-start.6
  217.9 6.3 %copy-start.2 = (bf16[1024,1024]{1,0:T(8,128)(2,1)S(1)}, bf16[1024,1024]{1,0:T(8,128)(2,1)}, u32[]{:S(2)}) copy-start(bf16[1024,1024]{1,0:T(8,128)(2,1)} %get-tuple-element.13) | copy-start | bytes 6291460
  219.1 9.7 %collective-permute-start.6 = (bf16[512,128]{1,0:T(8,128)(2,1)S(1)}, bf16[512,128]{1,0:T(8,128)(2,1)S(1)}, u32[]{:S(2)}, u32[]{:S(2)}) collective-permute-start(bf16[512,128]{1,0:T(8,128)(2,1)S(1)} %get-tuple-element.23), channel_id=1, source_target_pairs={{0,96},{32,0},{64,32},{96,64},{1,97},{33,1},{65,33},{97,65},{2,98}... | collective-permute-start | bytes 393224 | tf_op jit(solution)/shard_map/ppermute | solution.py:411
  221.6 7.2 %collective-permute-start.7 = (bf16[512,128]{1,0:T(8,128)(2,1)S(1)}, bf16[512,128]{1,0:T(8,128)(2,1)S(1)}, u32[]{:S(2)}, u32[]{:S(2)}) collective-permute-start(bf16[512,128]{1,0:T(8,128)(2,1)S(1)} %get-tuple-element.25), channel_id=1, source_target_pairs={{0,64},{32,96},{64,0},{96,32},{1,65},{33,97},{65,1},{97,33},{2,66}... | collective-permute-start | bytes 393224 | tf_op jit(solution)/shard_map/ppermute | solution.py:411
  222.1 9.2 %collective-permute-start.8 = (bf16[512,128]{1,0:T(8,128)(2,1)S(1)}, bf16[512,128]{1,0:T(8,128)(2,1)S(1)}, u32[]{:S(2)}, u32[]{:S(2)}) collective-permute-start(bf16[512,128]{1,0:T(8,128)(2,1)S(1)} %get-tuple-element.24), channel_id=1, source_target_pairs={{0,32},{32,64},{64,96},{96,0},{1,33},{33,65},{65,97},{97,1},{2,34}... | collective-permute-start | bytes 393224 | tf_op jit(solution)/shard_map/ppermute | solution.py:411
  225.5 46.5 %collective-permute-start.3 = (bf16[256,1024]{1,0:T(8,128)(2,1)}, bf16[256,1024]{1,0:T(8,128)(2,1)}, u32[]{:S(2)}, u32[]{:S(2)}) collective-permute-start(bf16[256,1024]{1,0:T(8,128)(2,1)} %get-tuple-element.21), channel_id=1, source_target_pairs={{0,96},{32,0},{64,32},{96,64},{1,97},{33,1},{65,33},{97,65},{2,98}... | collective-permute-start | bytes 1572872 | tf_op jit(solution)/shard_map/ppermute | solution.py:411
  227.5 46.3 %collective-permute-start.4 = (bf16[256,1024]{1,0:T(8,128)(2,1)S(1)}, bf16[256,1024]{1,0:T(8,128)(2,1)}, u32[]{:S(2)}, u32[]{:S(2)}) collective-permute-start(bf16[256,1024]{1,0:T(8,128)(2,1)S(1)} %get-tuple-element.20), channel_id=1, source_target_pairs={{0,64},{32,96},{64,0},{96,32},{1,65},{33,97},{65,1},{97,33},{2,66}... | collective-permute-start | bytes 1572872 | tf_op jit(solution)/shard_map/ppermute | solution.py:411
  228.8 46.9 %collective-permute-start.5 = (bf16[256,1024]{1,0:T(8,128)(2,1)S(1)}, bf16[256,1024]{1,0:T(8,128)(2,1)}, u32[]{:S(2)}, u32[]{:S(2)}) collective-permute-start(bf16[256,1024]{1,0:T(8,128)(2,1)S(1)} %get-tuple-element.19), channel_id=1, source_target_pairs={{0,32},{32,64},{64,96},{96,0},{1,33},{33,65},{65,97},{97,1},{2,34}... | collective-permute-start | bytes 1572872 | tf_op jit(solution)/shard_map/ppermute | solution.py:411
  233.2 44.4 %all-to-all-start.2 = ((bf16[128,16,128]{2,1,0:T(8,128)(2,1)}), bf16[128,16,128]{2,1,0:T(8,128)(2,1)}, u32[]{:S(2)}, u32[]{:S(2)}) async-start(bf16[128,16,128]{2,1,0:T(8,128)(2,1)} %bitcast.13), calls=%async_computation.2 | async-start | bytes 1048576 | tf_op jit(solution)/shard_map/all_to_all | solution.py:458
Sparse Core Ops, SparseCore 0:
  10.3 179.9 all-gather.3
  191.9 32.3 all-gather.5

commit v5 on v4

--- a/solution.py
+++ b/solution.py
@@ -11,6 +11,7 @@
 CAP = 8
 BF = jnp.bfloat16
 F32 = jnp.float32
+PIECES = 4
 VMEM_LIMIT = 56 * 1024 * 1024
 
 
@@ -109,33 +110,41 @@
     )(ids, resid, dec_b.reshape(1, width))
 
 
-def encode_kernel(scale, rows_ref, weight_ref, bias_ref, pre_ref, proj_ref):
-    count, _, cols = rows_ref.shape
-    projected = []
+def encode_kernel(scale, rows_hbm, weight_ref, bias_ref, pre_ref, proj_ref, rows_ref, sems):
+    pieces = sems.shape[0]
+    sources, _, cols = rows_ref.shape
+    count = sources // pieces
     low = iota((1, 1, 128), 2) < LAT
-    for p in range(2):
-        rows = rows_ref[:, p * 16 : (p + 1) * 16, :].reshape(count * 16, cols)
-        both = dot_nt(rows, weight_ref[p]).reshape(count, 2, CAP, 256)
-        pre = jnp.where(low, both[:, 0, :, :128], both[:, 1, :, :128])
-        pre_ref[:, p * CAP : (p + 1) * CAP, :] = pre + bias_ref[p : p + 1, :][None]
-        projected.append(jnp.where(low, both[:, 0, :, 128:], both[:, 1, :, 128:]) * scale)
-    proj_ref[...] = jnp.concatenate(projected, axis=1).astype(BF)
+
+    def fetch(piece):
+        at = pl.ds(piece * count, count)
+        return pltpu.make_async_copy(rows_hbm.at[at], rows_ref.at[at], sems.at[piece])
+
+    for piece in range(pieces):
+        fetch(piece).start()
+    for piece in range(pieces):
+        fetch(piece).wait()
+        here = slice(piece * count, (piece + 1) * count)
+        projected = []
+        for p in range(2):
+            rows = rows_ref[here, p * 16 : (p + 1) * 16, :].reshape(count * 16, cols)
+            both = dot(rows, weight_ref[p]).reshape(count, 2, CAP, 256)
+            pre = jnp.where(low, both[:, 0, :, :128], both[:, 1, :, :128])
+            pre_ref[here, p * CAP : (p + 1) * CAP, :] = pre + bias_ref[p : p + 1, :][None]
+            projected.append(jnp.where(low, both[:, 0, :, 128:], both[:, 1, :, 128:]) * scale)
+        proj_ref[here] = jnp.concatenate(projected, axis=1).astype(BF)
 
 
 def encode(scale, arrived, weights, bias):
     sources, here, cols = arrived.shape
-    step = 32
     shape = (sources, 2 * CAP, 128)
+    vmem = pl.BlockSpec(memory_space=pltpu.VMEM)
     return pl.pallas_call(
         functools.partial(encode_kernel, scale),
-        grid=(sources // step,),
-        in_specs=[
-            pl.BlockSpec((step, here, cols), lambda i: (i, 0, 0)),
-            pl.BlockSpec(weights.shape, lambda i: (0, 0, 0)),
-            pl.BlockSpec(bias.shape, lambda i: (0, 0)),
-        ],
-        out_specs=[pl.BlockSpec((step, 2 * CAP, 128), lambda i: (i, 0, 0))] * 2,
+        in_specs=[pl.BlockSpec(memory_space=pl.ANY), vmem, vmem],
+        out_specs=[vmem, vmem],
         out_shape=[jax.ShapeDtypeStruct(shape, F32), jax.ShapeDtypeStruct(shape, BF)],
+        scratch_shapes=[pltpu.VMEM(arrived.shape, BF), pltpu.SemaphoreType.DMA((PIECES,))],
         compiler_params=params(),
         cost_estimate=cost(2 * sources * here * cols * 256, 11 * 2**20),
         name="encode_rows",
@@ -230,113 +239,148 @@
     return jnp.concatenate(packed, axis=1)
 
 
-def home_kernel(scale, *refs):
-    group, (dec_ref, bias_ref, recon_ref, gate_ref, pick_ref, part_ref) = refs[:4], refs[4:]
-    at = pl.program_id(0)
-    steps = pl.num_programs(0) // 2
+def home_kernel(scale, parts, *refs):
+    group, (dec_hbm, bias_ref), refs = refs[:parts], refs[parts : parts + 2], refs[parts + 2 :]
+    recon, gates, (pick_ref, part_ref, dec_ref, sems) = refs[:parts], refs[parts : 2 * parts], refs[2 * parts :]
     slots, rows = pick_ref.shape[1:]
     packed = slots // 2
-    per = dec_ref.shape[0] // 256
-
-    @pl.when(at == 0)
-    def _():
-        slot = iota((slots, rows), 0)
-        for d in range(4):
-            halves = group[d][packed:, :].astype(F32).astype(jnp.int32)
-            ids = jnp.concatenate([halves[0:2], halves[2:4]], axis=1)
-            rank0, rank1 = ranks(ids, slots // CAP)
-            here = (slot == ids[0:1, :] * CAP + rank0) | (slot == ids[1:2, :] * CAP + rank1)
-            pick_ref[d] = jnp.where(here, 1.0, 0.0).astype(BF)
-
-    @pl.when(at < steps)
-    def _():
+    pieces = sems.shape[0]
+    tall = dec_ref.shape[0] // pieces
+    per = tall // 256
+
+    def fetch(piece):
+        at = pl.ds(pl.multiple_of(piece * tall, tall), tall)
+        return pltpu.make_async_copy(dec_hbm.at[at], dec_ref.at[at], sems.at[piece])
+
+    for piece in range(pieces):
+        fetch(piece).start()
+
+    slot = iota((slots, rows), 0)
+    for d in range(parts):
+        halves = group[d][packed:, :].astype(F32).astype(jnp.int32)
+        ids = jnp.concatenate([halves[0:2], halves[2:4]], axis=1)
+        rank0, rank1 = ranks(ids, slots // CAP)
+        here = (slot == ids[0:1, :] * CAP + rank0) | (slot == ids[1:2, :] * CAP + rank1)
+        pick_ref[d] = jnp.where(here, 1.0, 0.0).astype(BF)
+
+    def aligned(start, size):
+        return pl.ds(pl.multiple_of(start * size, size), size)
+
+    @pl.loop(0, pieces)
+    def _(piece):
+        fetch(piece).wait()
         for g in range(per):
-            shard = at * per + g
-            source = pl.ds(pl.multiple_of(shard * 16, 16), 16)
-            target = pl.ds(pl.multiple_of(shard * 32, 32), 32)
-            acts = jnp.stack([group[d][source, :].astype(F32) for d in range(4)])
-            part = dot(spread(acts).astype(BF), dec_ref[g * 256 : (g + 1) * 256, :]).astype(BF)
-            for d in range(4):
-                part_ref[d, target, :] = part[d * 32 : (d + 1) * 32]
-
-    @pl.when(at == steps)
-    def _():
-        for d in range(4):
-            total = dot_tn(pick_ref[d], part_ref[d])
-            recon_ref[d * rows : (d + 1) * rows, :] = (total + bias_ref[...]).astype(BF)
-            part_ref[d] = dot(pick_ref[d], total.astype(BF)).astype(BF)
-
-    @pl.when(at >= steps)
-    def _():
+            shard = piece * per + g
+            acts = jnp.stack([group[d][aligned(shard, 16), :].astype(F32) for d in range(parts)])
+            part = dot(spread(acts).astype(BF), dec_ref[aligned(shard, 256), :]).astype(BF)
+            for d in range(parts):
+                part_ref[d, aligned(shard, 32), :] = part[d * 32 : (d + 1) * 32]
+
+    for d in range(parts):
+        total = dot_tn(pick_ref[d], part_ref[d])
+        recon[d][...] = (total + bias_ref[...]).astype(BF)
+        part_ref[d] = dot(pick_ref[d], total.astype(BF)).astype(BF)
+
+    @pl.loop(0, pieces)
+    def _(piece):
         for g in range(per):
-            shard = (at - steps) * per + g
-            source = pl.ds(pl.multiple_of(shard * 32, 32), 32)
-            total = jnp.concatenate([part_ref[d, source, :] for d in range(4)], axis=0)
-            wide = dot_nt(total, dec_ref[g * 256 : (g + 1) * 256, :])
-            gate_ref[:, pl.ds(pl.multiple_of(g * 16, 16), 16), :] = (gathered(wide) * scale).astype(BF)
+            shard = piece * per + g
+            total = jnp.concatenate([part_ref[d, aligned(shard, 32), :] for d in range(parts)], axis=0)
+            wide = dot_nt(total, dec_ref[aligned(shard, 256), :])
+            gate = (gathered(wide) * scale).astype(BF)
+            for d in range(parts):
+                gates[d][aligned(shard, 16), :] = gate[d]
 
 
 def home(scale, group, dec_all, bias):
     latents, cols = dec_all.shape
     tall, lanes = group[0].shape
+    parts = len(group)
     packed = tall - 16
     rows = 256
-    chunk = 1024
-    steps = latents // chunk
-    per = chunk // 256
-    return pl.pallas_call(
-        functools.partial(home_kernel, scale),
-        grid=(2 * steps,),
-        in_specs=[pl.BlockSpec((tall, lanes), lambda i: (0, 0))] * 4
-        + [
-            pl.BlockSpec((chunk, cols), lambda i: (i % steps, 0)),
-            pl.BlockSpec((1, cols), lambda i: (0, 0)),
+    vmem = pl.BlockSpec(memory_space=pltpu.VMEM)
+    return pl.pallas_call(
+        functools.partial(home_kernel, scale, parts),
+        in_specs=[vmem] * parts + [pl.BlockSpec(memory_space=pl.ANY), vmem],
+        out_specs=[vmem] * (2 * parts),
+        out_shape=[jax.ShapeDtypeStruct((rows, cols), BF)] * parts
+        + [jax.ShapeDtypeStruct((packed, lanes), BF)] * parts,
+        scratch_shapes=[
+            pltpu.VMEM((parts, 2 * packed, rows), BF),
+            pltpu.VMEM((parts, 2 * packed, cols), BF),
+            pltpu.VMEM((latents, cols), BF),
+            pltpu.SemaphoreType.DMA((8,)),
         ],
-        out_specs=[
-            pl.BlockSpec((4 * rows, cols), lambda i: (0, 0)),
-            pl.BlockSpec((4, 16 * per, lanes), lambda i: (0, jnp.maximum(i - steps, 0), 0)),
-        ],
-        out_shape=[
-            jax.ShapeDtypeStruct((4 * rows, cols), BF),
-            jax.ShapeDtypeStruct((4, packed, lanes), BF),
-        ],
-        scratch_shapes=[
-            pltpu.VMEM((4, 2 * packed, rows), BF),
-            pltpu.VMEM((4, 2 * packed, cols), BF),
-        ],
-        compiler_params=params(),
-        cost_estimate=cost(8 * latents * cols * 128, 36 * 2**20),
+        compiler_params=params(),
+        cost_estimate=cost(8 * latents * cols * 128, 20 * 2**20),
         name="home_rows",
     )(*group, dec_all, bias)
 
 
+def assemble_kernel(at_ref, *refs):
+    pieces, out, sems = refs[:-2], refs[-2], refs[-1]
+    cols = pieces[0].shape[1]
+    copies = []
+    for d, piece in enumerate(pieces):
+        place = pl.multiple_of(((at_ref[0] + d) % len(pieces)) * cols, cols)
+        copies.append(pltpu.make_async_copy(piece, out.at[:, pl.ds(place, cols)], sems.at[d]))
+    for copy in copies:
+        copy.start()
+    for copy in copies:
+        copy.wait()
+
+
+def assemble(at, pieces):
+    rows, cols = pieces[0].shape
+    return pl.pallas_call(
+        assemble_kernel,
+        in_specs=[pl.BlockSpec(memory_space=pltpu.SMEM)]
+        + [pl.BlockSpec(memory_space=pltpu.VMEM)] * len(pieces),
+        out_specs=pl.BlockSpec(memory_space=pl.ANY),
+        out_shape=jax.ShapeDtypeStruct((rows, cols * len(pieces)), BF),
+        scratch_shapes=[pltpu.SemaphoreType.DMA((len(pieces),))],
+        compiler_params=params(),
+        cost_estimate=cost(0, 2**22),
+        name="assemble_recon",
+    )(at.astype(jnp.int32).reshape(1), *pieces)
+
+
 def mix_kernel(msg_ref, dec_ref, own_dec_ref, out_ref, own_ref, twice_ref, name_ref):
     at = pl.program_id(0)
-    count = msg_ref.shape[0] * 32
+    sources = msg_ref.shape[0]
+    count = sources * 32
     chunk = dec_ref.shape[0]
 
     @pl.when(at == 0)
     def _():
-        twice = doubled(msg_ref[:, :32, :].reshape(count, 128))
-        twice_ref[...] = twice[:, 128:]
-        name_ref[...] = slot_names(msg_ref[:, 32:, :])
-        own = own_expanded(twice[:, :128])
-        own_ref[...] = own.T
-        out_ref[...] = dot(dot(own_ref[...], own).astype(BF), own_dec_ref[...])
-
-    zero = jnp.zeros((count, 128), BF)
-    spread = []
-    for q in range(chunk // 128):
-        block = lane_block(at * (chunk // 128) + q)
-        spread.append(jnp.where(name_ref[...] == block, twice_ref[...], zero))
-    mixed = dot(own_ref[...], jnp.concatenate(spread, axis=1)).astype(BF)
-    out_ref[...] += dot(mixed, dec_ref[...])
+        twice = doubled(msg_ref[:, :32, :].reshape(count, 128)).astype(F32).reshape(sources, 4, CAP, 256)
+        name = slot_names(msg_ref[:, 32:, :]).astype(F32).reshape(sources, 4, CAP, 128)
+        for b in range(4):
+            rows = twice[:, b].reshape(sources * CAP, 256).astype(BF)
+            name_ref[b] = name[:, b].reshape(sources * CAP, 128).astype(BF)
+            twice_ref[b] = rows[:, 128:]
+            own = rows[:, :128].T[:LAT]
+            own_ref[b] = own
+            mixed = dot(own, rows[:, :128])[:, :LAT].astype(BF)
+            here = slice(b * LAT, (b + 1) * LAT)
+            out_ref[here, :] = dot(mixed, own_dec_ref[here, :])
+
+    zero = jnp.zeros((sources * CAP, 128), BF)
+    mixed = []
+    for b in range(4):
+        wide = []
+        for q in range(chunk // 128):
+            block = lane_block(at * (chunk // 128) + q)
+            wide.append(jnp.where(name_ref[b] == block, twice_ref[b], zero))
+        mixed.append(dot(own_ref[b], jnp.concatenate(wide, axis=1)).astype(BF))
+    out_ref[...] += dot(jnp.concatenate(mixed, axis=0), dec_ref[...])
 
 
 def mix(msg, dec_all, own_dec):
-    count = msg.shape[0] * 32
+    per = msg.shape[0] * CAP
+    count = 4 * per
     latents, cols = dec_all.shape
-    chunk = 512
+    chunk = 1024
     return pl.pallas_call(
         mix_kernel,
         grid=(latents // chunk,),
@@ -348,9 +392,9 @@
         out_specs=pl.BlockSpec(own_dec.shape, lambda i: (0, 0)),
         out_shape=jax.ShapeDtypeStruct(own_dec.shape, F32),
         scratch_shapes=[
-            pltpu.VMEM((256, count), BF),
-            pltpu.VMEM((count, 128), BF),
-            pltpu.VMEM((count, 128), BF),
+            pltpu.VMEM((4, LAT, per), BF),
+            pltpu.VMEM((4, per, 128), BF),
+            pltpu.VMEM((4, per, 128), BF),
         ],
         compiler_params=params(),
         cost_estimate=cost(2 * latents * 256 * (count + cols), 20 * 2**20),
@@ -358,51 +402,71 @@
     )(msg, dec_all, own_dec)
 
 
-def grads_kernel(scale, gate_ref, proj_ref, msg_ref, rows_ref, mixed_ref, enc_ref, dec_ref, acc_ref):
-    at = pl.program_id(0)
-    sources = msg_ref.shape[0]
+def grads_kernel(
+    scale, gate_hbm, proj_hbm, msg_hbm, rows_hbm, mixed_hbm, enc_ref, dec_ref,
+    gate_ref, proj_ref, msg_ref, rows_ref, mixed_ref, acc_ref, sems, last
+):
+    pieces = sems.shape[0]
+    sources = msg_ref.shape[0] // pieces
     count = sources * 32
-    own = own_expanded(doubled(msg_ref[:, :32, :].reshape(count, 128))[:, :128])
-    total = gate_ref[...].astype(F32)
-    for part in range(proj_ref.shape[0]):
-        total = total - proj_ref[part].astype(F32)
-    wide = jnp.where(own.astype(F32) > 0, spread(total), 0.0).astype(BF)
-
-    @pl.when(at == 0)
-    def _():
-        acc_ref[...] = jnp.zeros_like(acc_ref)
-
-    acc_ref[...] += dot_tn(jnp.concatenate([wide, own], axis=1), rows_ref[...])
-
-    @pl.when(at == pl.num_programs(0) - 1)
-    def _():
-        enc_ref[...] = acc_ref[:256, :]
-        dec_ref[...] = (mixed_ref[...] - acc_ref[256:, :]) * scale
+
+    def fetch(piece):
+        at = pl.ds(piece * sources, sources)
+        tall = pl.ds(piece * count, count)
+        return [
+            pltpu.make_async_copy(msg_hbm.at[at], msg_ref.at[at], sems.at[piece, 0]),
+            pltpu.make_async_copy(gate_hbm.at[at], gate_ref.at[at], sems.at[piece, 1]),
+            pltpu.make_async_copy(proj_hbm.at[:, at], proj_ref.at[:, at], sems.at[piece, 2]),
+            pltpu.make_async_copy(rows_hbm.at[tall], rows_ref.at[tall], sems.at[piece, 3]),
+        ]
+
+    mixed_copy = pltpu.make_async_copy(mixed_hbm, mixed_ref, last)
+    for piece in range(pieces):
+        for copy in fetch(piece):
+            copy.start()
+    mixed_copy.start()
+    for piece in range(pieces):
+        for copy in fetch(piece):
+            copy.wait()
+        here = slice(piece * sources, (piece + 1) * sources)
+        own = own_expanded(doubled(msg_ref[here, :32, :].reshape(count, 128))[:, :128])
+        total = gate_ref[here].astype(F32)
+        for part in range(proj_ref.shape[0]):
+            total = total - proj_ref[part, here].astype(F32)
+        wide = jnp.where(own.astype(F32) > 0, spread(total), 0.0).astype(BF)
+        both = jnp.concatenate([wide, own], axis=1)
+        more = dot_tn(both, rows_ref[piece * count : (piece + 1) * count, :])
+        if piece == 0:
+            acc_ref[...] = more
+        elif piece < pieces - 1:
+            acc_ref[...] += more
+        else:
+            more = acc_ref[...] + more
+            enc_ref[...] = more[:256, :]
+            mixed_copy.wait()
+            dec_ref[...] = (mixed_ref[...] - more[256:, :]) * scale
 
 
 def grads(scale, gate, proj, msg, rows, mixed):
-    sources, tall, lanes = msg.shape
-    count = sources * 32
     cols = rows.shape[1]
-    step = 512
     shape = jax.ShapeDtypeStruct(mixed.shape, F32)
-    return pl.pallas_call(
-        lambda *refs: grads_kernel(scale, *refs),
-        grid=(count // step,),
-        in_specs=[
-            pl.BlockSpec((step // 32, 2 * CAP, 128), lambda i: (i, 0, 0)),
-            pl.BlockSpec((proj.shape[0], step // 32, 2 * CAP, 128), lambda i: (0, i, 0, 0)),
-            pl.BlockSpec((step // 32, tall, lanes), lambda i: (i, 0, 0)),
-            pl.BlockSpec((step, cols), lambda i: (i, 0)),
-            pl.BlockSpec(mixed.shape, lambda i: (0, 0)),
+    vmem = pl.BlockSpec(memory_space=pltpu.VMEM)
+    arrays = (gate, proj, msg, rows, mixed)
+    return pl.pallas_call(
+        functools.partial(grads_kernel, scale),
+        in_specs=[pl.BlockSpec(memory_space=pl.ANY)] * len(arrays),
+        out_specs=[vmem, vmem],
+        out_shape=[shape, shape],
+        scratch_shapes=[pltpu.VMEM(array.shape, array.dtype) for array in arrays]
+        + [
+            pltpu.VMEM((512, cols), F32),
+            pltpu.SemaphoreType.DMA((PIECES, 4)),
+            pltpu.SemaphoreType.DMA,
         ],
-        out_specs=[pl.BlockSpec(mixed.shape, lambda i: (0, 0))] * 2,
-        out_shape=[shape, shape],
-        scratch_shapes=[pltpu.VMEM((512, cols), F32)],
-        compiler_params=params(),
-        cost_estimate=cost(4 * count * cols * 256, 16 * 2**20),
+        compiler_params=params(),
+        cost_estimate=cost(4 * msg.shape[0] * 32 * cols * 256, 16 * 2**20),
         name="dictionary_grads",
-    )(gate, proj, msg, rows, mixed)
+    )(*arrays)
 
 
 def shifted(value, by, parts):
@@ -438,7 +502,7 @@
 
     weights = jnp.concatenate(
         [enc_x.reshape(2, 2 * LAT, cols), dec_x.reshape(2, 2 * LAT, cols)], axis=1
-    )
+    ).transpose(0, 2, 1)
     bias = jnp.where(at_x == 0, enc_b, 0.0).reshape(2, 2 * LAT)
     pre, proj = encode(scale, arrived, weights, bias)
     partial = lax.all_to_all(pre, everyone, 0, 0, tiled=True)
@@ -449,18 +513,14 @@
         msg.reshape(devices, here * CAP + 16, 128), everyone, 0, 0, tiled=True
     )
 
-    recon_x, gate = home(scale, group, dec_all, bias_x)
-    total = gate[0].astype(F32)
+    made = home(scale, group, dec_all, bias_x)
+    total = made[parts].astype(F32)
     for d in range(1, parts):
-        total = total + shifted(gate[d], -d, parts).astype(F32)
+        total = total + shifted(made[parts + d], -d, parts).astype(F32)
     total = total.astype(BF).reshape(1, shards, 2 * CAP, 128)
     total = jnp.broadcast_to(total, (parts, shards, 2 * CAP, 128))
     gates = lax.all_to_all(total.reshape(devices, 2 * CAP, 128), everyone, 0, 0, tiled=True)
-
-    recon = jnp.zeros((tok_rows, width), BF)
-    for d in range(parts):
-        piece = shifted(recon_x[d * tok_rows : (d + 1) * tok_rows], -d, parts)
-        recon = lax.dynamic_update_slice(recon, piece, (0, ((at_x + d) % parts) * cols))
+    recon = assemble(at_x, [shifted(made[d], -d, parts) for d in range(parts)])
 
     mixed = mix(message, dec_all, dec_x)
     enc_grad, dec_grad = grads(

time: 298 us -> 309 us (1.037)
  waiting for transfers between devices: 107 us -> 127 us
  Pallas kernels: 89.6 us -> 74.8 us
  starting transfers between devices: 37.5 us -> 49.5 us
  local copies, waits for them, and re-layouts: 15.3 us -> 8.58 us
    ppermute x9, waiting for transfers between devices: 2.55 us -> 27.3 us  [shifted(): lax.ppermute(value, 'dp', [(i, (i + by) % parts) for i in range(parts)])]
    all_to_all x1, starting transfers between devices: 7.4 us -> 19.9 us  [body(): lax.all_to_all(total.reshape(devices, 2 * CAP, 128), everyone, 0, 0, tile...]
    pallas_call x3 -> x4, Pallas kernels: 47.2 us -> 38.9 us  [the longest x1 19.8 us: home(): pl.pallas_call(functools.partial(home_kernel, scale, parts), in_specs=[vm...]
    pallas_call x1, Pallas kernels: 31.3 us -> 25 us  [mix(): pl.pallas_call(mix_kernel, grid=(latents // chunk,), in_specs=[pl.BlockSp...]
    dynamic_update_slice x3 -> x0, local copies, waits for them, and re-layouts: 5.61 us -> none  [body(): lax.dynamic_update_slice(recon, piece, (0, (at_x + d) % parts * cols))]
  transfers between devices with their start and end apart: 14 -> 14, of which waited for: 3 -> 6; matrix products, arithmetic and copies ran while one was open for 5% -> 3% of each run, Pallas kernels for 26% -> 21%
where the time goes in v5:
time: 309 us
  waiting for transfers between devices  127 us (41%)
  Pallas kernels  74.8 us (24%)
  starting transfers between devices  49.5 us (16%)
  blocking collectives  31 us (10%)
  between operations  14.2 us (5%)
  local copies, waits for them, and re-layouts  8.58 us (3%)
  other arithmetic  3.68 us (1%)
    all_to_all x1, waiting for transfers between devices, body(): lax.all_to_all(outgoing.reshape(devices, here * CAP, cols), everyone, 0,...  99.6 us
    all_to_all x1, blocking collectives, body(): partial = lax.all_to_all(pre, everyone, 0, 0, tiled=True)  31 us
    ppermute x9, waiting for transfers between devices, shifted(): lax.ppermute(value, 'dp', [(i, (i + by) % parts) for i in range(parts)])  27.3 us
    pallas_call x1, Pallas kernels, mix(): pl.pallas_call(mix_kernel, grid=(latents // chunk,), in_specs=[pl.BlockSp...  25 us
    all_to_all x1, starting transfers between devices, body(): lax.all_to_all(total.reshape(devices, 2 * CAP, 128), everyone, 0, 0, tile...  19.9 us
    pallas_call x1, Pallas kernels, home(): pl.pallas_call(functools.partial(home_kernel, scale, parts), in_specs=[vm...  19.8 us
    all_to_all x1, starting transfers between devices, body(): lax.all_to_all(outgoing.reshape(devices, here * CAP, cols), everyone, 0,...  12 us
    ppermute x9, starting transfers between devices, shifted(): lax.ppermute(value, 'dp', [(i, (i + by) % parts) for i in range(parts)])  10.1 us
  transfers between devices with their start and end apart: 14, of which 6 were waited for; matrix products, arithmetic and copies ran while one was open for 3% of the time, Pallas kernels for 21%

profile of v5, /device:TPU:1, one launch (start us, length us, event | category | flops | bytes accessed | tf_op | source)
XLA Modules:
  0.0 308.8 jit_solution(8524437292689898011)
XLA Ops:
  7.2 0.0 copy-start
  7.2 0.0 all-gather.4.cloned.1.call-start
  7.2 1.5 copy-done
  8.8 0.9 constant_dynamic-slice_fusion.own_dec_ref
  9.6 0.0 all-gather.4.cloned.1.call-update
  9.6 7.1 %route_rows.1 = bf16[4,1024,1024]{2,1,0:T(8,128)(2,1)} custom-call(s32[2,256]{1,0:T(2,128)} %bitcast.24, bf16[256,4096]{1,0:T(8,128)(2,1)} %resid_ref.1, f32[1,4096]{1,0:T(1,128)} %bitcast.23), custom_call_target="tpu_custom_call" | custom-call | flops 2147483648 | bytes 10485760 | tf_op jit(solution)/shard_map/route_rows/pallas_call | solution.py:96
  16.7 12.0 %all-to-all-start = ((bf16[128,32,1024]{2,1,0:T(8,128)(2,1)}), bf16[128,32,1024]{2,1,0:T(8,128)(2,1)}, u32[]{:S(2)}, u32[]{:S(2)}) async-start(bf16[128,32,1024]{2,1,0:T(8,128)(2,1)} %bitcast.17), calls=%async_computation | async-start | bytes 16777216 | tf_op jit(solution)/shard_map/all_to_all | solution.py:494
  28.7 0.3 copy.12
  29.0 0.0 copy-start.4
  29.0 1.1 constant_dynamic-slice_fusion.1
  30.1 1.0 copy.11
  31.1 2.1 maximum_bitcast_fusion.weight_ref
  33.2 0.6 select_bitcast_fusion.bias_ref
  33.8 99.6 %all-to-all-done.rows_hbm = bf16[128,32,1024]{2,1,0:T(8,128)(2,1)} async-done(((bf16[128,32,1024]{2,1,0:T(8,128)(2,1)}), bf16[128,32,1024]{2,1,0:T(8,128)(2,1)}, u32[]{:S(2)}, u32[]{:S(2)}) %all-to-all-start) | async-done | bytes 8388640 | tf_op jit(solution)/shard_map/all_to_all | solution.py:494
  133.4 6.8 %encode_rows.1 = (f32[128,16,128]{2,1,0:T(8,128)}, bf16[128,16,128]{2,1,0:T(8,128)(2,1)}) custom-call(bf16[128,32,1024]{2,1,0:T(8,128)(2,1)} %all-to-all-done.rows_hbm, bf16[2,1024,256]{2,1,0:T(8,128)(2,1)} %maximum_bitcast_fusion.weight_ref, f32[2,128]{1,0:T(2,128)} %select_bitcast_fusion.bias_ref), custom_call_target="tpu_custom_call" | custom-call | flops 2147483648 | bytes 11534336 | tf_op jit(solution)/shard_map/encode_rows/pallas_call | solution.py:142
  140.2 31.0 %all_to_all.20 = f32[128,16,128]{2,1,0:T(8,128)} all-to-all(f32[128,16,128]{2,1,0:T(8,128)} %get-tuple-element.17), channel_id=1, replica_groups=mesh['dp'=4,'dict'=32] {'dp','dict'}, dimensions={0} | all-to-all | bytes 2097152 | tf_op jit(solution)/shard_map/all_to_all | solution.py:508
  171.3 3.9 %activate_rows.1 = (bf16[528,128]{1,0:T(8,128)(2,1)}, bf16[4,32,48,128]{3,2,1,0:T(8,128)(2,1)}) custom-call(s32[2,256]{1,0:T(2,128)} %bitcast.25, f32[4,512,128]{2,1,0:T(8,128)} %bitcast.19), custom_call_target="tpu_custom_call" | custom-call | flops 134217728 | bytes 3145728 | tf_op jit(solution)/shard_map/activate_rows/pallas_call | solution.py:191
  175.1 7.4 %all-to-all-start.3 = ((bf16[128,48,128]{2,1,0:T(8,128)(2,1)}), bf16[128,48,128]{2,1,0:T(8,128)(2,1)}, u32[]{:S(2)}, u32[]{:S(2)}) async-start(bf16[128,48,128]{2,1,0:T(8,128)(2,1)} %bitcast.21), calls=%async_computation.3 | async-start | bytes 3145728 | tf_op jit(solution)/shard_map/all_to_all | solution.py:512
  182.5 0.0 all-gather.6.cloned.1.call-start
  182.6 1.5 collective-permute-start
  184.0 2.4 collective-permute-start.1
  186.4 1.2 collective-permute-start.2
  187.6 1.3 dynamic_slice.11
  188.9 0.0 all-gather.6.cloned.1.call-update
  188.9 15.9 %collective-permute-done.refs_1_ = bf16[528,128]{1,0:T(8,128)(2,1)S(1)} collective-permute-done((bf16[528,128]{1,0:T(8,128)(2,1)S(1)}, bf16[528,128]{1,0:T(8,128)(2,1)S(1)}, u32[]{:S(2)}, u32[]{:S(2)}) %collective-permute-start) | collective-permute-done | bytes 135200 | tf_op jit(solution)/shard_map/ppermute | solution.py:475
  204.8 3.1 collective-permute-done.1.refs_2_
  207.9 0.0 collective-permute-done.2.refs_3_
  207.9 0.0 all-gather.4.cloned.1.call-done.refs_4_.dec_ref
  207.9 0.6 copy-done.7
  208.5 0.1 copy-done.8
  208.6 19.8 %home_rows.1 = (bf16[256,1024]{1,0:T(8,128)(2,1)}, bf16[256,1024]{1,0:T(8,128)(2,1)}, bf16[256,1024]{1,0:T(8,128)(2,1)}, bf16[256,1024]{1,0:T(8,128)(2,1)}, bf16...) custom-call(bf16[528,128]{1,0:T(8,128)(2,1)} %get-tuple-element.18.refs_0_, ...), custom_call_target="tpu_custom_call" | custom-call | flops 8589934592 | bytes 20971520 | tf_op jit(solution)/shard_map/home_rows/pallas_call | solution.py:302
  228.4 0.1 collective-permute-start.6
  228.5 1.4 collective-permute-start.7
  229.9 0.3 collective-permute-start.8
  230.2 2.4 collective-permute-start.3
  232.6 1.0 collective-permute-start.4
  233.5 3.2 %collective-permute-done.6 = bf16[512,128]{1,0:T(8,128)(2,1)S(1)} collective-permute-done((bf16[512,128]{1,0:T(8,128)(2,1)}, bf16[512,128]{1,0:T(8,128)(2,1)S(1)}, u32[]{:S(2)}, u32[]{:S(2)}) %collective-permute-start.6) | collective-permute-done | bytes 131104 | tf_op jit(solution)/shard_map/ppermute | solution.py:475
  236.7 1.5 collective-permute-done.7
  238.2 3.7 %collective-permute-done.8 = bf16[512,128]{1,0:T(8,128)(2,1)S(1)} collective-permute-done((bf16[512,128]{1,0:T(8,128)(2,1)}, bf16[512,128]{1,0:T(8,128)(2,1)S(1)}, u32[]{:S(2)}, u32[]{:S(2)}) %collective-permute-start.8) | collective-permute-done | bytes 131104 | tf_op jit(solution)/shard_map/ppermute | solution.py:475
  241.9 1.0 add_convert_fusion
  242.9 0.9 broadcast_in_dim.13
  243.7 19.9 %all-to-all-start.2 = ((bf16[128,16,128]{2,1,0:T(8,128)(2,1)}), bf16[128,16,128]{2,1,0:T(8,128)(2,1)}, u32[]{:S(2)}, u32[]{:S(2)}) async-start(bf16[128,16,128]{2,1,0:T(8,128)(2,1)} %bitcast.11), calls=%async_computation.2 | async-start | bytes 1048576 | tf_op jit(solution)/shard_map/all_to_all | solution.py:522
  263.6 25.0 %mix_decoder.1.mixed_hbm = f32[256,1024]{1,0:T(8,128)} custom-call(bf16[128,48,128]{2,1,0:T(8,128)(2,1)} %all-to-all-done.3.msg_ref.msg_hbm, bf16[8192,1024]{1,0:T(8,128)(2,1)} %all-gather.4.cloned.1.call-done.refs_4_.dec_ref, bf16[256,1024]{1,0:T(8,128)(2,1)} %constant_dynamic-slice_fusion.own_dec_ref), custom_call_target="tpu_custom_call" | custom-call | flops 21474836480 | bytes 20971520 | tf_op jit(solution)/shard_map/mix_decoder/pallas_call | solution.py:384
  288.7 0.8 copy-done.2
  289.4 0.2 copy-done.3
  289.6 2.9 assemble_recon.1
  292.5 0.0 all-gather.6.cloned.1.call-done
  292.5 9.4 %dictionary_grads.1 = (f32[256,1024]{1,0:T(8,128)}, f32[256,1024]{1,0:T(8,128)}) custom-call(bf16[128,16,128]{2,1,0:T(8,128)(2,1)} %all-to-all-done.2.gate_hbm, bf16[4,128,16,128]{3,2,1,0:T(8,128)(2,1)} %bitcast.27, bf16[128,48,128]{2,1,0:T(8,128)(2,1)} %all-to-all-done.3.msg_ref.msg_hbm, bf16[4096,1024]{1,0:T(8,128)(2,1)} %bitcast.14.rows_hbm, ...), custom_call_target="tpu_custom_call" | custom-call | flops 4294967296 | bytes 16777216 | tf_op jit(solution)/shard_map/dictionary_grads/pallas_call | solution.py:455
  (17 shorter events, 0.0 us)
Async XLA Ops:
  7.2 1.6 copy-start
  7.2 200.7 %all-gather.4.cloned.1.call-start = ((), (), s32[]{:S(2)}) async-start(), calls=%async_computation.4 | async-start | bytes 17301504 | tf_op jit(solution)/shard_map/all_gather | solution.py:501
  16.7 12.0 %copy-start.1 = (bf16[256,1024]{1,0:T(8,128)(2,1)S(1)}, bf16[256,1024]{1,0:T(8,128)(2,1)}, u32[]{:S(2)}) copy-start(bf16[256,1024]{1,0:T(8,128)(2,1)} %constant_dynamic-slice_fusion.own_dec_ref) | copy-start | bytes 1572868
  16.7 116.6 %all-to-all-start = ((bf16[128,32,1024]{2,1,0:T(8,128)(2,1)}), bf16[128,32,1024]{2,1,0:T(8,128)(2,1)}, u32[]{:S(2)}, u32[]{:S(2)}) async-start(bf16[128,32,1024]{2,1,0:T(8,128)(2,1)} %bitcast.17), calls=%async_computation | async-start | bytes 16777216 | tf_op jit(solution)/shard_map/all_to_all | solution.py:494
  29.0 4.2 %copy-start.4 = (f32[256]{0:T(256)S(1)}, f32[256]{0:T(256)}, u32[]{:S(2)}) copy-start(f32[256]{0:T(256)} %param.9) | copy-start | bytes 3076
  175.1 7.5 %copy-start.5 = (bf16[528,128]{1,0:T(8,128)(2,1)S(1)}, bf16[528,128]{1,0:T(8,128)(2,1)}, u32[]{:S(2)}) copy-start(bf16[528,128]{1,0:T(8,128)(2,1)} %get-tuple-element.18.refs_0_) | copy-start | bytes 405508
  175.1 67.7 %all-to-all-start.3 = ((bf16[128,48,128]{2,1,0:T(8,128)(2,1)}), bf16[128,48,128]{2,1,0:T(8,128)(2,1)}, u32[]{:S(2)}, u32[]{:S(2)}) async-start(bf16[128,48,128]{2,1,0:T(8,128)(2,1)} %bitcast.21), calls=%async_computation.3 | async-start | bytes 3145728 | tf_op jit(solution)/shard_map/all_to_all | solution.py:512
  182.5 110.0 %all-gather.6.cloned.1.call-start = ((), (), s32[]{:S(2)}) async-start(), calls=%async_computation.5 | async-start | bytes 2621440 | tf_op jit(solution)/shard_map/all_gather | solution.py:509
  182.6 22.2 %collective-permute-start = (bf16[528,128]{1,0:T(8,128)(2,1)S(1)}, bf16[528,128]{1,0:T(8,128)(2,1)S(1)}, u32[]{:S(2)}, u32[]{:S(2)}) collective-permute-start(bf16[528,128]{1,0:T(8,128)(2,1)S(1)} %copy-done.5), channel_id=1, source_target_pairs={{0,32},{32,64},{64,96},{96,0},{1,33},{33,65},{65,97},{97,1},{2,34}... | collective-permute-start | bytes 405512 | tf_op jit(solution)/shard_map/ppermute | solution.py:475
  184.0 23.8 %collective-permute-start.1 = (bf16[528,128]{1,0:T(8,128)(2,1)S(1)}, bf16[528,128]{1,0:T(8,128)(2,1)S(1)}, u32[]{:S(2)}, u32[]{:S(2)}) collective-permute-start(bf16[528,128]{1,0:T(8,128)(2,1)S(1)} %copy-done.5), channel_id=1, source_target_pairs={{0,64},{32,96},{64,0},{96,32},{1,65},{33,97},{65,1},{97,33},{2,66}... | collective-permute-start | bytes 405512 | tf_op jit(solution)/shard_map/ppermute | solution.py:475
  186.4 21.4 %collective-permute-start.2 = (bf16[528,128]{1,0:T(8,128)(2,1)S(1)}, bf16[528,128]{1,0:T(8,128)(2,1)S(1)}, u32[]{:S(2)}, u32[]{:S(2)}) collective-permute-start(bf16[528,128]{1,0:T(8,128)(2,1)S(1)} %copy-done.5), channel_id=1, source_target_pairs={{0,96},{32,0},{64,32},{96,64},{1,97},{33,1},{65,33},{97,65},{2,98}... | collective-permute-start | bytes 405512 | tf_op jit(solution)/shard_map/ppermute | solution.py:475
  204.8 3.1 %copy-start.6 = (bf16[528,128]{1,0:T(8,128)(2,1)}, bf16[528,128]{1,0:T(8,128)(2,1)S(1)}, u32[]{:S(2)}) copy-start(bf16[528,128]{1,0:T(8,128)(2,1)S(1)} %collective-permute-done.refs_1_) | copy-start | bytes 405508
  207.9 0.6 copy-start.7
  207.9 0.7 copy-start.8
  228.4 8.3 %collective-permute-start.6 = (bf16[512,128]{1,0:T(8,128)(2,1)}, bf16[512,128]{1,0:T(8,128)(2,1)S(1)}, u32[]{:S(2)}, u32[]{:S(2)}) collective-permute-start(bf16[512,128]{1,0:T(8,128)(2,1)} %get-tuple-element.24), channel_id=1, source_target_pairs={{0,96},{32,0},{64,32},{96,64},{1,97},{33,1},{65,33},{97,65},{2,98}... | collective-permute-start | bytes 393224 | tf_op jit(solution)/shard_map/ppermute | solution.py:475
  228.5 9.7 %collective-permute-start.7 = (bf16[512,128]{1,0:T(8,128)(2,1)}, bf16[512,128]{1,0:T(8,128)(2,1)S(1)}, u32[]{:S(2)}, u32[]{:S(2)}) collective-permute-start(bf16[512,128]{1,0:T(8,128)(2,1)} %get-tuple-element.25), channel_id=1, source_target_pairs={{0,64},{32,96},{64,0},{96,32},{1,65},{33,97},{65,1},{97,33},{2,66}... | collective-permute-start | bytes 393224 | tf_op jit(solution)/shard_map/ppermute | solution.py:475
  229.9 12.0 %collective-permute-start.8 = (bf16[512,128]{1,0:T(8,128)(2,1)}, bf16[512,128]{1,0:T(8,128)(2,1)S(1)}, u32[]{:S(2)}, u32[]{:S(2)}) collective-permute-start(bf16[512,128]{1,0:T(8,128)(2,1)} %get-tuple-element.26), channel_id=1, source_target_pairs={{0,32},{32,64},{64,96},{96,0},{1,33},{33,65},{65,97},{97,1},{2,34}... | collective-permute-start | bytes 393224 | tf_op jit(solution)/shard_map/ppermute | solution.py:475
  230.2 58.4 %collective-permute-start.3 = (bf16[256,1024]{1,0:T(8,128)(2,1)}, bf16[256,1024]{1,0:T(8,128)(2,1)S(1)}, u32[]{:S(2)}, u32[]{:S(2)}) collective-permute-start(bf16[256,1024]{1,0:T(8,128)(2,1)} %get-tuple-element.20), channel_id=1, source_target_pairs={{0,96},{32,0},{64,32},{96,64},{1,97},{33,1},{65,33},{97,65},{2,98}... | collective-permute-start | bytes 1572872 | tf_op jit(solution)/shard_map/ppermute | solution.py:475
  232.6 56.1 %collective-permute-start.4 = (bf16[256,1024]{1,0:T(8,128)(2,1)}, bf16[256,1024]{1,0:T(8,128)(2,1)S(1)}, u32[]{:S(2)}, u32[]{:S(2)}) collective-permute-start(bf16[256,1024]{1,0:T(8,128)(2,1)} %get-tuple-element.21), channel_id=1, source_target_pairs={{0,64},{32,96},{64,0},{96,32},{1,65},{33,97},{65,1},{97,33},{2,66}... | collective-permute-start | bytes 1572872 | tf_op jit(solution)/shard_map/ppermute | solution.py:475
  236.7 52.0 %collective-permute-start.5 = (bf16[256,1024]{1,0:T(8,128)(2,1)}, bf16[256,1024]{1,0:T(8,128)(2,1)}, u32[]{:S(2)}, u32[]{:S(2)}) collective-permute-start(bf16[256,1024]{1,0:T(8,128)(2,1)} %get-tuple-element.22), channel_id=1, source_target_pairs={{0,32},{32,64},{64,96},{96,0},{1,33},{33,65},{65,97},{97,1},{2,34}... | collective-permute-start | bytes 1572872 | tf_op jit(solution)/shard_map/ppermute | solution.py:475
  243.7 48.8 %all-to-all-start.2 = ((bf16[128,16,128]{2,1,0:T(8,128)(2,1)}), bf16[128,16,128]{2,1,0:T(8,128)(2,1)}, u32[]{:S(2)}, u32[]{:S(2)}) async-start(bf16[128,16,128]{2,1,0:T(8,128)(2,1)} %bitcast.11), calls=%async_computation.2 | async-start | bytes 1048576 | tf_op jit(solution)/shard_map/all_to_all | solution.py:522
  288.6 0.8 copy-start.2
  288.6 1.0 copy-start.3
Sparse Core Ops, SparseCore 0:
  10.3 194.2 all-gather.3
  206.2 49.1 all-gather.5

commit v6 on v5

--- a/solution.py
+++ b/solution.py
@@ -240,7 +240,7 @@
 
 
 def home_kernel(scale, parts, *refs):
-    group, (dec_hbm, bias_ref), refs = refs[:parts], refs[parts : parts + 2], refs[parts + 2 :]
+    group, (place_ref, dec_hbm, bias_ref), refs = refs[:parts], refs[parts : parts + 3], refs[parts + 3 :]
     recon, gates, (pick_ref, part_ref, dec_ref, sems) = refs[:parts], refs[parts : 2 * parts], refs[2 * parts :]
     slots, rows = pick_ref.shape[1:]
     packed = slots // 2
@@ -276,9 +276,10 @@
             for d in range(parts):
                 part_ref[d, aligned(shard, 32), :] = part[d * 32 : (d + 1) * 32]
 
+    bias = bias_ref[pl.ds(place_ref[0], 1), :]
     for d in range(parts):
         total = dot_tn(pick_ref[d], part_ref[d])
-        recon[d][...] = (total + bias_ref[...]).astype(BF)
+        recon[d][...] = (total + bias).astype(BF)
         part_ref[d] = dot(pick_ref[d], total.astype(BF)).astype(BF)
 
     @pl.loop(0, pieces)
@@ -292,7 +293,7 @@
                 gates[d][aligned(shard, 16), :] = gate[d]
 
 
-def home(scale, group, dec_all, bias):
+def home(scale, place, group, dec_all, bias):
     latents, cols = dec_all.shape
     tall, lanes = group[0].shape
     parts = len(group)
@@ -301,7 +302,8 @@
     vmem = pl.BlockSpec(memory_space=pltpu.VMEM)
     return pl.pallas_call(
         functools.partial(home_kernel, scale, parts),
-        in_specs=[vmem] * parts + [pl.BlockSpec(memory_space=pl.ANY), vmem],
+        in_specs=[vmem] * parts
+        + [pl.BlockSpec(memory_space=pltpu.SMEM), pl.BlockSpec(memory_space=pl.ANY), vmem],
         out_specs=[vmem] * (2 * parts),
         out_shape=[jax.ShapeDtypeStruct((rows, cols), BF)] * parts
         + [jax.ShapeDtypeStruct((packed, lanes), BF)] * parts,
@@ -314,7 +316,7 @@
         compiler_params=params(),
         cost_estimate=cost(8 * latents * cols * 128, 20 * 2**20),
         name="home_rows",
-    )(*group, dec_all, bias)
+    )(*group, place, dec_all, bias)
 
 
 def assemble_kernel(at_ref, *refs):
@@ -345,59 +347,91 @@
     )(at.astype(jnp.int32).reshape(1), *pieces)
 
 
-def mix_kernel(msg_ref, dec_ref, own_dec_ref, out_ref, own_ref, twice_ref, name_ref):
-    at = pl.program_id(0)
+def sum_kernel(*refs):
+    out_ref = refs[-1]
+    total = refs[0][...].astype(F32)
+    for ref in refs[1:-1]:
+        total = total + ref[...].astype(F32)
+    for copy in range(out_ref.shape[0]):
+        out_ref[copy] = total.astype(BF)
+
+
+def summed(pieces, copies):
+    return pl.pallas_call(
+        sum_kernel,
+        out_shape=jax.ShapeDtypeStruct((copies, *pieces[0].shape), BF),
+        compiler_params=params(),
+        cost_estimate=cost(0, 2**20),
+        name="sum_pieces",
+    )(*pieces)
+
+
+def mix_kernel(msg_ref, dec_hbm, start_ref, out_ref, own_ref, other_ref, name_ref, dec_ref, sems):
     sources = msg_ref.shape[0]
     count = sources * 32
-    chunk = dec_ref.shape[0]
-
-    @pl.when(at == 0)
-    def _():
-        twice = doubled(msg_ref[:, :32, :].reshape(count, 128)).astype(F32).reshape(sources, 4, CAP, 256)
-        name = slot_names(msg_ref[:, 32:, :]).astype(F32).reshape(sources, 4, CAP, 128)
+    steps = sems.shape[0]
+    quarter = dec_ref.shape[0] // 4
+    tall = quarter // steps
+
+    def fetch(step, q):
+        at = pl.ds(q * quarter + step * tall, tall)
+        return pltpu.make_async_copy(dec_hbm.at[at], dec_ref.at[at], sems.at[step, q])
+
+    for step in range(steps):
+        for q in range(4):
+            fetch(step, q).start()
+
+    twice = doubled(msg_ref[:, :32, :].reshape(count, 128)).astype(F32).reshape(sources, 4, CAP, 256)
+    block = slot_names(msg_ref[:, 32:, :]).astype(F32).reshape(sources, 4, CAP, 128)
+    for b in range(4):
+        rows = twice[:, b].reshape(sources * CAP, 256)
+        other_ref[b] = rows[:, 128:].astype(BF)
+        name = block[:, b].reshape(sources * CAP, 128)
+        within = jnp.floor(name * (1.0 / 32.0))
+        name_ref[b] = (name - 32.0 * within).astype(BF)
+        wide = jnp.concatenate([rows[:, :128]] * 2, axis=1)
+        lane = (iota((1, 256), 1) // LAT).astype(F32)
+        own_ref[b] = jnp.where(jnp.concatenate([within] * 2, axis=1) == lane, wide, 0.0).astype(BF).T
+        own = rows[:, :128].astype(BF)
+        here = slice(b * LAT, (b + 1) * LAT)
+        out_ref[here, :] = dot(dot_tn(own, own)[:LAT, :LAT].astype(BF), start_ref[here, :])
+
+    zero = jnp.zeros((sources * CAP, 128), BF)
+    for step in range(steps):
+        mixed = []
         for b in range(4):
-            rows = twice[:, b].reshape(sources * CAP, 256).astype(BF)
-            name_ref[b] = name[:, b].reshape(sources * CAP, 128).astype(BF)
-            twice_ref[b] = rows[:, 128:]
-            own = rows[:, :128].T[:LAT]
-            own_ref[b] = own
-            mixed = dot(own, rows[:, :128])[:, :LAT].astype(BF)
-            here = slice(b * LAT, (b + 1) * LAT)
-            out_ref[here, :] = dot(mixed, own_dec_ref[here, :])
-
-    zero = jnp.zeros((sources * CAP, 128), BF)
-    mixed = []
-    for b in range(4):
-        wide = []
-        for q in range(chunk // 128):
-            block = lane_block(at * (chunk // 128) + q)
-            wide.append(jnp.where(name_ref[b] == block, twice_ref[b], zero))
-        mixed.append(dot(own_ref[b], jnp.concatenate(wide, axis=1)).astype(BF))
-    out_ref[...] += dot(jnp.concatenate(mixed, axis=0), dec_ref[...])
+            wide = []
+            for pair in range(tall // 128):
+                name = iota((1, 128), 1) // LAT + 2 * pair + step * (tall // LAT)
+                wide.append(jnp.where(name_ref[b] == name.astype(F32).astype(BF), other_ref[b], zero))
+            mixed.append(dot(own_ref[b], jnp.concatenate(wide, axis=1)).astype(BF))
+        total = out_ref[...]
+        for q in range(4):
+            fetch(step, q).wait()
+            left = jnp.concatenate([mixed[b][q * LAT : (q + 1) * LAT] for b in range(4)], axis=0)
+            start = q * quarter + step * tall
+            total = total + dot(left, dec_ref[start : start + tall, :])
+        out_ref[...] = total
 
 
 def mix(msg, dec_all, own_dec):
+    latents, cols = dec_all.shape
     per = msg.shape[0] * CAP
-    count = 4 * per
-    latents, cols = dec_all.shape
-    chunk = 1024
+    vmem = pl.BlockSpec(memory_space=pltpu.VMEM)
     return pl.pallas_call(
         mix_kernel,
-        grid=(latents // chunk,),
-        in_specs=[
-            pl.BlockSpec(msg.shape, lambda i: (0, 0, 0)),
-            pl.BlockSpec((chunk, cols), lambda i: (i, 0)),
-            pl.BlockSpec(own_dec.shape, lambda i: (0, 0)),
-        ],
-        out_specs=pl.BlockSpec(own_dec.shape, lambda i: (0, 0)),
+        in_specs=[vmem, pl.BlockSpec(memory_space=pl.ANY), vmem],
+        out_specs=vmem,
         out_shape=jax.ShapeDtypeStruct(own_dec.shape, F32),
         scratch_shapes=[
-            pltpu.VMEM((4, LAT, per), BF),
+            pltpu.VMEM((4, 4 * LAT, per), BF),
             pltpu.VMEM((4, per, 128), BF),
             pltpu.VMEM((4, per, 128), BF),
+            pltpu.VMEM(dec_all.shape, BF),
+            pltpu.SemaphoreType.DMA((4, 4)),
         ],
         compiler_params=params(),
-        cost_estimate=cost(2 * latents * 256 * (count + cols), 20 * 2**20),
+        cost_estimate=cost(2 * latents * 256 * (per + cols), 20 * 2**20),
         name="mix_decoder",
     )(msg, dec_all, own_dec)
 
@@ -406,39 +440,40 @@
     scale, gate_hbm, proj_hbm, msg_hbm, rows_hbm, mixed_hbm, enc_ref, dec_ref,
     gate_ref, proj_ref, msg_ref, rows_ref, mixed_ref, acc_ref, sems, last
 ):
-    pieces = sems.shape[0]
-    sources = msg_ref.shape[0] // pieces
+    parts = proj_hbm.shape[0]
+    sources = msg_ref.shape[0] // parts
     count = sources * 32
-
-    def fetch(piece):
-        at = pl.ds(piece * sources, sources)
-        tall = pl.ds(piece * count, count)
+    cols = rows_ref.shape[1]
+
+    def fetch(part):
+        at = pl.ds(part * sources, sources)
+        tall = pl.ds(part * count, count)
         return [
-            pltpu.make_async_copy(msg_hbm.at[at], msg_ref.at[at], sems.at[piece, 0]),
-            pltpu.make_async_copy(gate_hbm.at[at], gate_ref.at[at], sems.at[piece, 1]),
-            pltpu.make_async_copy(proj_hbm.at[:, at], proj_ref.at[:, at], sems.at[piece, 2]),
-            pltpu.make_async_copy(rows_hbm.at[tall], rows_ref.at[tall], sems.at[piece, 3]),
+            pltpu.make_async_copy(msg_hbm.at[at], msg_ref.at[at], sems.at[part, 0]),
+            pltpu.make_async_copy(gate_hbm.at[at], gate_ref.at[at], sems.at[part, 1]),
+            pltpu.make_async_copy(proj_hbm.at[:, at], proj_ref.at[:, at], sems.at[part, 2]),
+            pltpu.make_async_copy(rows_hbm.at[tall], rows_ref.at[tall], sems.at[part, 3]),
         ]
 
     mixed_copy = pltpu.make_async_copy(mixed_hbm, mixed_ref, last)
-    for piece in range(pieces):
-        for copy in fetch(piece):
+    for part in range(parts):
+        for copy in fetch(part):
             copy.start()
     mixed_copy.start()
-    for piece in range(pieces):
-        for copy in fetch(piece):
+    for part in range(parts):
+        for copy in fetch(part):
             copy.wait()
-        here = slice(piece * sources, (piece + 1) * sources)
+        here = slice(part * sources, (part + 1) * sources)
         own = own_expanded(doubled(msg_ref[here, :32, :].reshape(count, 128))[:, :128])
         total = gate_ref[here].astype(F32)
-        for part in range(proj_ref.shape[0]):
-            total = total - proj_ref[part, here].astype(F32)
+        for other in range(parts):
+            total = total - proj_ref[other, here].astype(F32)
         wide = jnp.where(own.astype(F32) > 0, spread(total), 0.0).astype(BF)
         both = jnp.concatenate([wide, own], axis=1)
-        more = dot_tn(both, rows_ref[piece * count : (piece + 1) * count, :])
-        if piece == 0:
+        more = dot_tn(both, rows_ref[part * count : (part + 1) * count, :])
+        if part == 0:
             acc_ref[...] = more
-        elif piece < pieces - 1:
+        elif part < parts - 1:
             acc_ref[...] += more
         else:
             more = acc_ref[...] + more
@@ -460,7 +495,7 @@
         scratch_shapes=[pltpu.VMEM(array.shape, array.dtype) for array in arrays]
         + [
             pltpu.VMEM((512, cols), F32),
-            pltpu.SemaphoreType.DMA((PIECES, 4)),
+            pltpu.SemaphoreType.DMA((proj.shape[0], 4)),
             pltpu.SemaphoreType.DMA,
         ],
         compiler_params=params(),
@@ -497,7 +532,6 @@
 
     enc_x = lax.dynamic_slice(enc_w, (0, at_x * cols), (local, cols))
     dec_x = lax.dynamic_slice(dec_w, (0, at_x * cols), (local, cols))
-    bias_x = lax.dynamic_slice(dec_b, (at_x * cols,), (cols,)).reshape(1, cols)
     dec_all = lax.all_gather(dec_x, "dict", axis=0, tiled=True)
 
     weights = jnp.concatenate(
@@ -509,19 +543,16 @@
     projs = lax.all_gather(proj, "dp", axis=0, tiled=False)
     acts, msg = activate(ids, partial.reshape(parts, shards * 2 * CAP, 128), shards)
     group = [shifted(acts, d, parts) for d in range(parts)]
+    msg, *group = lax.optimization_barrier((msg, *group))
     message = lax.all_to_all(
         msg.reshape(devices, here * CAP + 16, 128), everyone, 0, 0, tiled=True
     )
 
-    made = home(scale, group, dec_all, bias_x)
-    total = made[parts].astype(F32)
-    for d in range(1, parts):
-        total = total + shifted(made[parts + d], -d, parts).astype(F32)
-    total = total.astype(BF).reshape(1, shards, 2 * CAP, 128)
-    total = jnp.broadcast_to(total, (parts, shards, 2 * CAP, 128))
+    place = at_x.astype(jnp.int32).reshape(1)
+    made = home(scale, place, group, dec_all, dec_b.reshape(parts, cols))
+    total = summed([shifted(made[parts + d], -d, parts) for d in range(parts)], parts)
     gates = lax.all_to_all(total.reshape(devices, 2 * CAP, 128), everyone, 0, 0, tiled=True)
     recon = assemble(at_x, [shifted(made[d], -d, parts) for d in range(parts)])
-
     mixed = mix(message, dec_all, dec_x)
     enc_grad, dec_grad = grads(
         scale, gates, projs, message, arrived.reshape(devices * here * CAP, cols), mixed

time: 309 us -> 286 us (0.926)
  blocking collectives: 31 us -> 0 us
  waiting for transfers between devices: 127 us -> 137 us
  Pallas kernels: 74.8 us -> 67.5 us
  starting transfers between devices: 49.5 us -> 55.6 us
    all_to_all x1 -> x0, blocking collectives: 31 us -> none  [body(): partial = lax.all_to_all(pre, everyone, 0, 0, tiled=True)]
    all_to_all x0 -> x1, waiting for transfers between devices: none -> 18.6 us  [body(): partial = lax.all_to_all(pre, everyone, 0, 0, tiled=True)]
    ppermute x9, waiting for transfers between devices: 27.3 us -> 13.4 us  [shifted(): lax.ppermute(value, 'dp', [(i, (i + by) % parts) for i in range(parts)])]
    all_to_all x0 -> x1, starting transfers between devices: none -> 10.6 us  [body(): partial = lax.all_to_all(pre, everyone, 0, 0, tiled=True)]
    pallas_call x1 -> x2, Pallas kernels: 25 us -> 17.1 us  [the longest x1 15.2 us: mix(): pl.pallas_call(mix_kernel, in_specs=[vmem, pl.BlockSpec(memory_space=pl.A...]
    all_to_all x1, starting transfers between devices: 19.9 us -> 12.9 us  [body(): lax.all_to_all(total.reshape(devices, 2 * CAP, 128), everyone, 0, 0, tile...]
    all_to_all x1, waiting for transfers between devices: 0.01 us -> 4.06 us  [body(): lax.all_to_all(total.reshape(devices, 2 * CAP, 128), everyone, 0, 0, tile...]
  transfers between devices with their start and end apart: 14 -> 15, of which waited for: 6 -> 9; matrix products, arithmetic and copies ran while one was open for 3% -> 2% of each run, Pallas kernels for 21% -> 20%
where the time goes in v6:
time: 286 us; the launch traced here: 285 us
  waiting for transfers between devices  137 us (48%)
  Pallas kernels  67.5 us (24%)
  starting transfers between devices  55.6 us (19%)
  between operations  14.2 us (5%)
  local copies, waits for them, and re-layouts  7.96 us (3%)
    all_to_all x1, waiting for transfers between devices, body(): lax.all_to_all(outgoing.reshape(devices, here * CAP, cols), everyone, 0,...  101 us
    pallas_call x1, Pallas kernels, home(): pl.pallas_call(functools.partial(home_kernel, scale, parts), in_specs=[vm...  20.2 us
    all_to_all x1, waiting for transfers between devices, body(): partial = lax.all_to_all(pre, everyone, 0, 0, tiled=True)  18.6 us
    pallas_call x1, Pallas kernels, mix(): pl.pallas_call(mix_kernel, in_specs=[vmem, pl.BlockSpec(memory_space=pl.A...  15.2 us
    ppermute x9, waiting for transfers between devices, shifted(): lax.ppermute(value, 'dp', [(i, (i + by) % parts) for i in range(parts)])  13.4 us
    all_to_all x1, starting transfers between devices, body(): lax.all_to_all(total.reshape(devices, 2 * CAP, 128), everyone, 0, 0, tile...  12.9 us
    all_to_all x1, starting transfers between devices, body(): lax.all_to_all(outgoing.reshape(devices, here * CAP, cols), everyone, 0,...  12 us
    ppermute x9, starting transfers between devices, shifted(): lax.ppermute(value, 'dp', [(i, (i + by) % parts) for i in range(parts)])  10.9 us
  transfers between devices with their start and end apart: 15, of which 9 were waited for; matrix products, arithmetic and copies ran while one was open for 2% of the time, Pallas kernels for 20%

profile of v6, /device:TPU:1, one launch (start us, length us, event | category | flops | bytes accessed | tf_op | source)
XLA Modules:
  0.0 285.4 jit_solution(13318771965771317845)
XLA Ops:
  7.2 0.0 copy-start
  7.2 0.0 all-gather.4.cloned.1.call-start
  7.2 1.5 copy-done
  8.8 0.9 constant_dynamic-slice_fusion.start_ref
  9.6 0.0 all-gather.4.cloned.1.call-update
  9.7 7.1 %route_rows.1 = bf16[4,1024,1024]{2,1,0:T(8,128)(2,1)} custom-call(s32[2,256]{1,0:T(2,128)} %bitcast.22, bf16[256,4096]{1,0:T(8,128)(2,1)} %resid_ref.1, f32[1,4096]{1,0:T(1,128)} %bitcast.21), custom_call_target="tpu_custom_call" | custom-call | flops 2147483648 | bytes 10485760 | tf_op jit(solution)/shard_map/route_rows/pallas_call | solution.py:96
  16.7 12.0 %all-to-all-start = ((bf16[128,32,1024]{2,1,0:T(8,128)(2,1)}), bf16[128,32,1024]{2,1,0:T(8,128)(2,1)}, u32[]{:S(2)}, u32[]{:S(2)}) async-start(bf16[128,32,1024]{2,1,0:T(8,128)(2,1)} %bitcast.15), calls=%async_computation | async-start | bytes 16777216 | tf_op jit(solution)/shard_map/all_to_all | solution.py:529
  28.7 0.3 copy.12
  29.0 1.1 constant_dynamic-slice_fusion.1
  30.1 1.0 copy.11
  31.1 2.1 maximum_bitcast_fusion.weight_ref
  33.2 0.6 select_bitcast_fusion.bias_ref
  33.8 100.6 %all-to-all-done.rows_hbm = bf16[128,32,1024]{2,1,0:T(8,128)(2,1)} async-done(((bf16[128,32,1024]{2,1,0:T(8,128)(2,1)}), bf16[128,32,1024]{2,1,0:T(8,128)(2,1)}, u32[]{:S(2)}, u32[]{:S(2)}) %all-to-all-start) | async-done | bytes 8388640 | tf_op jit(solution)/shard_map/all_to_all | solution.py:529
  134.4 6.8 %encode_rows.1 = (f32[128,16,128]{2,1,0:T(8,128)}, bf16[128,16,128]{2,1,0:T(8,128)(2,1)}) custom-call(bf16[128,32,1024]{2,1,0:T(8,128)(2,1)} %all-to-all-done.rows_hbm, bf16[2,1024,256]{2,1,0:T(8,128)(2,1)} %maximum_bitcast_fusion.weight_ref, f32[2,128]{1,0:T(2,128)} %select_bitcast_fusion.bias_ref), custom_call_target="tpu_custom_call" | custom-call | flops 2147483648 | bytes 11534336 | tf_op jit(solution)/shard_map/encode_rows/pallas_call | solution.py:142
  141.2 10.6 %all-to-all-start.1 = ((f32[128,16,128]{2,1,0:T(8,128)}), f32[128,16,128]{2,1,0:T(8,128)S(1)}, u32[]{:S(2)}, u32[]{:S(2)}) async-start(f32[128,16,128]{2,1,0:T(8,128)} %get-tuple-element.22), calls=%async_computation.1 | async-start | bytes 2097152 | tf_op jit(solution)/shard_map/all_to_all | solution.py:542
  151.8 0.0 all-gather.6.cloned.1.call-start
  151.9 0.7 all-gather.6.cloned.1.call-update
  152.6 18.6 %all-to-all-done.1 = f32[128,16,128]{2,1,0:T(8,128)S(1)} async-done(((f32[128,16,128]{2,1,0:T(8,128)}), f32[128,16,128]{2,1,0:T(8,128)S(1)}, u32[]{:S(2)}, u32[]{:S(2)}) %all-to-all-start.1) | async-done | bytes 1048608 | tf_op jit(solution)/shard_map/all_to_all | solution.py:542
  171.1 1.0 copy-done.2
  172.1 3.8 %activate_rows.1 = (bf16[528,128]{1,0:T(8,128)(2,1)}, bf16[4,32,48,128]{3,2,1,0:T(8,128)(2,1)}) custom-call(s32[2,256]{1,0:T(2,128)} %bitcast.23, f32[4,512,128]{2,1,0:T(8,128)} %bitcast.17), custom_call_target="tpu_custom_call" | custom-call | flops 134217728 | bytes 3145728 | tf_op jit(solution)/shard_map/activate_rows/pallas_call | solution.py:191
  175.9 0.5 collective-permute-start
  176.4 2.3 collective-permute-start.1
  178.8 0.8 collective-permute-start.2
  179.6 2.0 collective-permute-done.refs_1_
  181.6 1.8 collective-permute-done.1.refs_2_
  183.5 1.1 collective-permute-done.2.refs_3_
  184.6 9.2 %all-to-all-start.3 = ((bf16[128,48,128]{2,1,0:T(8,128)(2,1)}), bf16[128,48,128]{2,1,0:T(8,128)(2,1)}, u32[]{:S(2)}, u32[]{:S(2)}) async-start(bf16[128,48,128]{2,1,0:T(8,128)(2,1)} %bitcast.20), calls=%async_computation.3 | async-start | bytes 3145728 | tf_op jit(solution)/shard_map/all_to_all | solution.py:547
  193.8 0.6 reshape.47.refs_6_
  194.4 20.2 %home_rows.1 = (bf16[256,1024]{1,0:T(8,128)(2,1)}, bf16[256,1024]{1,0:T(8,128)(2,1)}, bf16[256,1024]{1,0:T(8,128)(2,1)}, bf16[256,1024]{1,0:T(8,128)(2,1)}, bf16...) custom-call(bf16[528,128]{1,0:T(8,128)(2,1)} %get-tuple-element.25.refs_0_, ...), custom_call_target="tpu_custom_call" | custom-call | flops 8589934592 | bytes 20971520 | tf_op jit(solution)/shard_map/home_rows/pallas_call | solution.py:303
  214.6 2.6 collective-permute-start.6
  217.3 0.6 collective-permute-start.7
  217.9 0.6 collective-permute-start.8
  218.5 2.1 collective-permute-start.3
  220.5 1.2 collective-permute-start.4
  221.7 3.6 %collective-permute-done.6.refs_1_ = bf16[512,128]{1,0:T(8,128)(2,1)S(1)} collective-permute-done((bf16[512,128]{1,0:T(8,128)(2,1)}, bf16[512,128]{1,0:T(8,128)(2,1)S(1)}, u32[]{:S(2)}, u32[]{:S(2)}) %collective-permute-start.6) | collective-permute-done | bytes 131104 | tf_op jit(solution)/shard_map/ppermute | solution.py:510
  225.3 0.1 collective-permute-start.5
  225.5 1.9 collective-permute-done.7.refs_2_
  227.4 2.9 %collective-permute-done.8.refs_3_ = bf16[512,128]{1,0:T(8,128)(2,1)S(1)} collective-permute-done((bf16[512,128]{1,0:T(8,128)(2,1)}, bf16[512,128]{1,0:T(8,128)(2,1)S(1)}, u32[]{:S(2)}, u32[]{:S(2)}) %collective-permute-start.8) | collective-permute-done | bytes 131104 | tf_op jit(solution)/shard_map/ppermute | solution.py:510
  230.3 0.6 copy-done.7
  231.0 2.0 sum_pieces.1
  232.9 12.9 %all-to-all-start.2 = ((bf16[128,16,128]{2,1,0:T(8,128)(2,1)}), bf16[128,16,128]{2,1,0:T(8,128)(2,1)}, u32[]{:S(2)}, u32[]{:S(2)}) async-start(bf16[128,16,128]{2,1,0:T(8,128)(2,1)} %bitcast.18), calls=%async_computation.2 | async-start | bytes 1048576 | tf_op jit(solution)/shard_map/all_to_all | solution.py:554
  245.9 15.2 %mix_decoder.1.mixed_hbm = f32[256,1024]{1,0:T(8,128)} custom-call(bf16[128,48,128]{2,1,0:T(8,128)(2,1)} %all-to-all-done.3.msg_ref.msg_hbm, bf16[8192,1024]{1,0:T(8,128)(2,1)} %all-gather.4.cloned.1.call-done.refs_5_.dec_hbm, bf16[256,1024]{1,0:T(8,128)(2,1)} %constant_dynamic-slice_fusion.start_ref), custom_call_target="tpu_custom_call" | custom-call | flops 8589934592 | bytes 20971520 | tf_op jit(solution)/shard_map/mix_decoder/pallas_call | solution.py:421
  261.1 0.8 copy-done.3
  261.8 0.2 copy-done.4
  262.0 2.9 %assemble_recon.1 = bf16[256,4096]{1,0:T(8,128)(2,1)} custom-call(s32[1]{0:T(128)} %bitcast.refs_4_.at_ref, bf16[256,1024]{1,0:T(8,128)(2,1)} %get-tuple-element.29.refs_0_, bf16[256,1024]{1,0:T(8,128)(2,1)} %copy-done.3, bf16[256,1024]{1,0:T(8,128)(2,1)} %copy-done.4, bf16[256,1024]{1,0:T(8,128)(2,1)} %collective-permute-done.5.refs_3_), custom_call_target="tpu_custom_call" | custom-call | bytes 4194304 | tf_op jit(solution)/shard_map/assemble_recon/pallas_call | solution.py:337
  264.9 0.0 all-gather.6.cloned.1.call-done
  264.9 4.1 %all-to-all-done.2.gate_hbm = bf16[128,16,128]{2,1,0:T(8,128)(2,1)} async-done(((bf16[128,16,128]{2,1,0:T(8,128)(2,1)}), bf16[128,16,128]{2,1,0:T(8,128)(2,1)}, u32[]{:S(2)}, u32[]{:S(2)}) %all-to-all-start.2) | async-done | bytes 524320 | tf_op jit(solution)/shard_map/all_to_all | solution.py:554
  269.0 9.6 %dictionary_grads.1 = (f32[256,1024]{1,0:T(8,128)}, f32[256,1024]{1,0:T(8,128)}) custom-call(bf16[128,16,128]{2,1,0:T(8,128)(2,1)} %all-to-all-done.2.gate_hbm, bf16[4,128,16,128]{3,2,1,0:T(8,128)(2,1)} %bitcast.24, bf16[128,48,128]{2,1,0:T(8,128)(2,1)} %all-to-all-done.3.msg_ref.msg_hbm, bf16[4096,1024]{1,0:T(8,128)(2,1)} %bitcast.12.rows_hbm, ...), custom_call_target="tpu_custom_call" | custom-call | flops 4294967296 | bytes 16777216 | tf_op jit(solution)/shard_map/dictionary_grads/pallas_call | solution.py:490
  (25 shorter events, 0.1 us)
Async XLA Ops:
  7.2 1.6 copy-start
  7.2 187.2 %all-gather.4.cloned.1.call-start = ((), (), s32[]{:S(2)}) async-start(), calls=%async_computation.4 | async-start | bytes 17301504 | tf_op jit(solution)/shard_map/all_gather | solution.py:535
  16.7 12.0 %copy-start.1 = (bf16[256,1024]{1,0:T(8,128)(2,1)S(1)}, bf16[256,1024]{1,0:T(8,128)(2,1)}, u32[]{:S(2)}) copy-start(bf16[256,1024]{1,0:T(8,128)(2,1)} %constant_dynamic-slice_fusion.start_ref) | copy-start | bytes 1572868
  16.7 117.7 %all-to-all-start = ((bf16[128,32,1024]{2,1,0:T(8,128)(2,1)}), bf16[128,32,1024]{2,1,0:T(8,128)(2,1)}, u32[]{:S(2)}, u32[]{:S(2)}) async-start(bf16[128,32,1024]{2,1,0:T(8,128)(2,1)} %bitcast.15), calls=%async_computation | async-start | bytes 16777216 | tf_op jit(solution)/shard_map/all_to_all | solution.py:529
  29.0 4.2 %copy-start.9 = (f32[256]{0:T(256)S(1)}, f32[256]{0:T(256)}, u32[]{:S(2)}) copy-start(f32[256]{0:T(256)} %param.9) | copy-start | bytes 3076
  141.2 29.9 %all-to-all-start.1 = ((f32[128,16,128]{2,1,0:T(8,128)}), f32[128,16,128]{2,1,0:T(8,128)S(1)}, u32[]{:S(2)}, u32[]{:S(2)}) async-start(f32[128,16,128]{2,1,0:T(8,128)} %get-tuple-element.22), calls=%async_computation.1 | async-start | bytes 2097152 | tf_op jit(solution)/shard_map/all_to_all | solution.py:542
  151.8 113.1 %all-gather.6.cloned.1.call-start = ((), (), s32[]{:S(2)}) async-start(), calls=%async_computation.5 | async-start | bytes 2621440 | tf_op jit(solution)/shard_map/all_gather | solution.py:543
  171.1 1.0 copy-start.2
  172.1 21.7 %copy-start.8 = (f32[4096]{0:T(1024)S(1)}, f32[4096]{0:T(1024)}, u32[]{:S(2)}) copy-start(f32[4096]{0:T(1024)} %param.11) | copy-start | bytes 49156
  175.9 5.7 %collective-permute-start = (bf16[528,128]{1,0:T(8,128)(2,1)}, bf16[528,128]{1,0:T(8,128)(2,1)S(1)}, u32[]{:S(2)}, u32[]{:S(2)}) collective-permute-start(bf16[528,128]{1,0:T(8,128)(2,1)} %get-tuple-element.25.refs_0_), channel_id=1, source_target_pairs={{0,32},{32,64},{64,96},{96,0},{1,33},{33,65},{65,97},{97,1},{2,34}... | collective-permute-start | bytes 405512 | tf_op jit(solution)/shard_map/ppermute | solution.py:510
  176.4 7.0 %collective-permute-start.1 = (bf16[528,128]{1,0:T(8,128)(2,1)}, bf16[528,128]{1,0:T(8,128)(2,1)S(1)}, u32[]{:S(2)}, u32[]{:S(2)}) collective-permute-start(bf16[528,128]{1,0:T(8,128)(2,1)} %get-tuple-element.25.refs_0_), channel_id=1, source_target_pairs={{0,64},{32,96},{64,0},{96,32},{1,65},{33,97},{65,1},{97,33},{2,66}... | collective-permute-start | bytes 405512 | tf_op jit(solution)/shard_map/ppermute | solution.py:510
  178.8 5.8 %collective-permute-start.2 = (bf16[528,128]{1,0:T(8,128)(2,1)}, bf16[528,128]{1,0:T(8,128)(2,1)S(1)}, u32[]{:S(2)}, u32[]{:S(2)}) collective-permute-start(bf16[528,128]{1,0:T(8,128)(2,1)} %get-tuple-element.25.refs_0_), channel_id=1, source_target_pairs={{0,96},{32,0},{64,32},{96,64},{1,97},{33,1},{65,33},{97,65},{2,98}... | collective-permute-start | bytes 405512 | tf_op jit(solution)/shard_map/ppermute | solution.py:510
  181.6 12.8 %copy-start.10 = (bf16[528,128]{1,0:T(8,128)(2,1)}, bf16[528,128]{1,0:T(8,128)(2,1)S(1)}, u32[]{:S(2)}) copy-start(bf16[528,128]{1,0:T(8,128)(2,1)S(1)} %collective-permute-done.refs_1_) | copy-start | bytes 405508
  183.5 11.0 %copy-start.11 = (bf16[528,128]{1,0:T(8,128)(2,1)}, bf16[528,128]{1,0:T(8,128)(2,1)S(1)}, u32[]{:S(2)}) copy-start(bf16[528,128]{1,0:T(8,128)(2,1)S(1)} %collective-permute-done.1.refs_2_) | copy-start | bytes 405508
  184.6 9.8 %copy-start.12 = (bf16[528,128]{1,0:T(8,128)(2,1)}, bf16[528,128]{1,0:T(8,128)(2,1)S(1)}, u32[]{:S(2)}) copy-start(bf16[528,128]{1,0:T(8,128)(2,1)S(1)} %collective-permute-done.2.refs_3_) | copy-start | bytes 405508
  184.6 48.3 %all-to-all-start.3 = ((bf16[128,48,128]{2,1,0:T(8,128)(2,1)}), bf16[128,48,128]{2,1,0:T(8,128)(2,1)}, u32[]{:S(2)}, u32[]{:S(2)}) async-start(bf16[128,48,128]{2,1,0:T(8,128)(2,1)} %bitcast.20), calls=%async_computation.3 | async-start | bytes 3145728 | tf_op jit(solution)/shard_map/all_to_all | solution.py:547
  214.6 10.7 %collective-permute-start.6 = (bf16[512,128]{1,0:T(8,128)(2,1)}, bf16[512,128]{1,0:T(8,128)(2,1)S(1)}, u32[]{:S(2)}, u32[]{:S(2)}) collective-permute-start(bf16[512,128]{1,0:T(8,128)(2,1)} %get-tuple-element.34), channel_id=1, source_target_pairs={{0,96},{32,0},{64,32},{96,64},{1,97},{33,1},{65,33},{97,65},{2,98}... | collective-permute-start | bytes 393224 | tf_op jit(solution)/shard_map/ppermute | solution.py:510
  217.3 10.1 %collective-permute-start.7 = (bf16[512,128]{1,0:T(8,128)(2,1)}, bf16[512,128]{1,0:T(8,128)(2,1)S(1)}, u32[]{:S(2)}, u32[]{:S(2)}) collective-permute-start(bf16[512,128]{1,0:T(8,128)(2,1)} %get-tuple-element.35), channel_id=1, source_target_pairs={{0,64},{32,96},{64,0},{96,32},{1,65},{33,97},{65,1},{97,33},{2,66}... | collective-permute-start | bytes 393224 | tf_op jit(solution)/shard_map/ppermute | solution.py:510
  217.9 12.4 %collective-permute-start.8 = (bf16[512,128]{1,0:T(8,128)(2,1)}, bf16[512,128]{1,0:T(8,128)(2,1)S(1)}, u32[]{:S(2)}, u32[]{:S(2)}) collective-permute-start(bf16[512,128]{1,0:T(8,128)(2,1)} %get-tuple-element.36), channel_id=1, source_target_pairs={{0,32},{32,64},{64,96},{96,0},{1,33},{33,65},{65,97},{97,1},{2,34}... | collective-permute-start | bytes 393224 | tf_op jit(solution)/shard_map/ppermute | solution.py:510
  218.5 42.6 %collective-permute-start.3 = (bf16[256,1024]{1,0:T(8,128)(2,1)}, bf16[256,1024]{1,0:T(8,128)(2,1)S(1)}, u32[]{:S(2)}, u32[]{:S(2)}) collective-permute-start(bf16[256,1024]{1,0:T(8,128)(2,1)} %get-tuple-element.30), channel_id=1, source_target_pairs={{0,96},{32,0},{64,32},{96,64},{1,97},{33,1},{65,33},{97,65},{2,98}... | collective-permute-start | bytes 1572872 | tf_op jit(solution)/shard_map/ppermute | solution.py:510
  220.5 40.5 %collective-permute-start.4 = (bf16[256,1024]{1,0:T(8,128)(2,1)}, bf16[256,1024]{1,0:T(8,128)(2,1)S(1)}, u32[]{:S(2)}, u32[]{:S(2)}) collective-permute-start(bf16[256,1024]{1,0:T(8,128)(2,1)} %get-tuple-element.31), channel_id=1, source_target_pairs={{0,64},{32,96},{64,0},{96,32},{1,65},{33,97},{65,1},{97,33},{2,66}... | collective-permute-start | bytes 1572872 | tf_op jit(solution)/shard_map/ppermute | solution.py:510
  225.3 5.0 %copy-start.5 = (bf16[512,128]{1,0:T(8,128)(2,1)}, bf16[512,128]{1,0:T(8,128)(2,1)S(1)}, u32[]{:S(2)}) copy-start(bf16[512,128]{1,0:T(8,128)(2,1)S(1)} %collective-permute-done.6.refs_1_) | copy-start | bytes 393220
  225.3 35.7 %collective-permute-start.5 = (bf16[256,1024]{1,0:T(8,128)(2,1)}, bf16[256,1024]{1,0:T(8,128)(2,1)}, u32[]{:S(2)}, u32[]{:S(2)}) collective-permute-start(bf16[256,1024]{1,0:T(8,128)(2,1)} %get-tuple-element.32), channel_id=1, source_target_pairs={{0,32},{32,64},{64,96},{96,0},{1,33},{33,65},{65,97},{97,1},{2,34}... | collective-permute-start | bytes 1572872 | tf_op jit(solution)/shard_map/ppermute | solution.py:510
  227.4 2.9 %copy-start.6 = (bf16[512,128]{1,0:T(8,128)(2,1)}, bf16[512,128]{1,0:T(8,128)(2,1)S(1)}, u32[]{:S(2)}) copy-start(bf16[512,128]{1,0:T(8,128)(2,1)S(1)} %collective-permute-done.7.refs_2_) | copy-start | bytes 393220
  230.3 0.6 copy-start.7
  232.9 36.0 %all-to-all-start.2 = ((bf16[128,16,128]{2,1,0:T(8,128)(2,1)}), bf16[128,16,128]{2,1,0:T(8,128)(2,1)}, u32[]{:S(2)}, u32[]{:S(2)}) async-start(bf16[128,16,128]{2,1,0:T(8,128)(2,1)} %bitcast.18), calls=%async_computation.2 | async-start | bytes 1048576 | tf_op jit(solution)/shard_map/all_to_all | solution.py:554
  261.0 0.8 copy-start.3
  261.1 0.9 copy-start.4
Sparse Core Ops, SparseCore 0:
  10.3 179.7 all-gather.3
  191.8 60.4 all-gather.5

commit v7 on v6

--- a/solution.py
+++ b/solution.py
@@ -72,38 +72,48 @@
     return dot(kept.reshape(sources * 32, 128), jnp.ones((128, 128), BF)).astype(BF)
 
 
-def route_kernel(ids_ref, resid_ref, bias_ref, out_ref, pick_ref):
-    slots, rows = pick_ref.shape
-
-    @pl.when(pl.program_id(0) == 0)
-    def _():
-        ids = ids_ref[...]
-        rank0, rank1 = ranks(ids, slots // CAP)
-        slot = iota((slots, rows), 0)
-        is0 = slot == ids[0:1, :] * CAP + rank0
-        is1 = slot == ids[1:2, :] * CAP + rank1
-        pick_ref[...] = jnp.where(is0 | is1, 1.0, 0.0).astype(BF)
-
-    centered = (resid_ref[...].astype(F32) - bias_ref[...]).astype(BF)
-    step = 256
-    for at in range(0, slots, step):
-        out_ref[0, at : at + step, :] = dot(pick_ref[at : at + step, :], centered).astype(BF)
+def route_kernel(ids_ref, resid_ref, bias_ref, out_hbm, pick_ref, out_ref, sems):
+    parts, slots, cols = out_ref.shape
+    rows = pick_ref.shape[1]
+    ids = ids_ref[...]
+    rank0, rank1 = ranks(ids, slots // CAP)
+    slot = iota((slots, rows), 0)
+    is0 = slot == ids[0:1, :] * CAP + rank0
+    is1 = slot == ids[1:2, :] * CAP + rank1
+    pick_ref[...] = jnp.where(is0 | is1, 1.0, 0.0).astype(BF)
+    pieces = sems.shape[1]
+    tall = slots // pieces
+
+    def send(part, piece):
+        at = pl.ds(piece * tall, tall)
+        return pltpu.make_async_copy(out_ref.at[part, at], out_hbm.at[part, at], sems.at[part, piece])
+
+    for part in range(parts):
+        here = slice(part * cols, (part + 1) * cols)
+        centered = (resid_ref[:, here].astype(F32) - bias_ref[:, here]).astype(BF)
+        for piece in range(pieces):
+            at = slice(piece * tall, (piece + 1) * tall)
+            out_ref[part, at, :] = dot(pick_ref[at, :], centered).astype(BF)
+            send(part, piece).start()
+    for part in range(parts):
+        for piece in range(pieces):
+            send(part, piece).wait()
 
 
 def route(ids, resid, dec_b, parts, slots):
     rows, width = resid.shape
     cols = width // parts
+    vmem = pl.BlockSpec(memory_space=pltpu.VMEM)
     return pl.pallas_call(
         route_kernel,
-        grid=(parts,),
-        in_specs=[
-            pl.BlockSpec(ids.shape, lambda i: (0, 0)),
-            pl.BlockSpec((rows, cols), lambda i: (0, i)),
-            pl.BlockSpec((1, cols), lambda i: (0, i)),
+        in_specs=[vmem] * 3,
+        out_specs=pl.BlockSpec(memory_space=pl.ANY),
+        out_shape=jax.ShapeDtypeStruct((parts, slots, cols), BF),
+        scratch_shapes=[
+            pltpu.VMEM((slots, rows), BF),
+            pltpu.VMEM((parts, slots, cols), BF),
+            pltpu.SemaphoreType.DMA((parts, 4)),
         ],
-        out_specs=pl.BlockSpec((1, slots, cols), lambda i: (i, 0, 0)),
-        out_shape=jax.ShapeDtypeStruct((parts, slots, cols), BF),
-        scratch_shapes=[pltpu.VMEM((slots, rows), BF)],
         compiler_params=params(),
         cost_estimate=cost(2 * slots * rows * width, 10 * 2**20),
         name="route_rows",
@@ -151,15 +161,34 @@
     )(arrived, weights, bias)
 
 
-def activate_kernel(ids_ref, pre_ref, group_ref, msg_ref):
+def activate_kernel(ids_ref, pre_ref, group_ref):
+    packed = pre_ref.shape[1]
+    ids = ids_ref[...]
+    total = pre_ref[0] + pre_ref[1] + pre_ref[2] + pre_ref[3]
+    group_ref[:packed, :] = jnp.maximum(total, 0.0).astype(BF)
+    halves = [ids[:, :128], ids[:, 128:], jnp.zeros((12, 128), jnp.int32)]
+    group_ref[packed:, :] = jnp.concatenate(halves, axis=0).astype(F32).astype(BF)
+
+
+def activate(ids, partial):
+    parts, packed, lanes = partial.shape
+    return pl.pallas_call(
+        activate_kernel,
+        out_shape=jax.ShapeDtypeStruct((packed + 16, lanes), BF),
+        compiler_params=params(),
+        cost_estimate=cost(4 * packed * lanes, 2**20),
+        name="activate_slots",
+    )(ids, partial)
+
+
+def message_kernel(ids_ref, acts_ref, msg_ref):
     shards = msg_ref.shape[1]
-    packed = pre_ref.shape[1]
+    packed = acts_ref.shape[0] - 16
     rows = ids_ref.shape[1]
     slots = 2 * packed
     ids = ids_ref[...]
     rank0, rank1 = ranks(ids, slots // CAP)
-    total = pre_ref[0] + pre_ref[1] + pre_ref[2] + pre_ref[3]
-    acts = jnp.maximum(total, 0.0).astype(BF)
+    acts = acts_ref[:packed, :]
     slot = iota((slots, rows), 0)
     found = []
     for k, rank in ((0, rank0), (1, rank1)):
@@ -171,9 +200,6 @@
     first, second = found
     straight = jnp.concatenate([first, second], axis=1).astype(BF)
     crossed = jnp.concatenate([second, first], axis=1).astype(BF)
-    group_ref[:packed, :] = acts
-    halves = [ids[:, :128], ids[:, 128:], jnp.zeros((12, 128), jnp.int32)]
-    group_ref[packed:, :] = jnp.concatenate(halves, axis=0).astype(F32).astype(BF)
     pick0 = jnp.where(slot == ids[0:1, :] * CAP + rank0, 1.0, 0.0).astype(BF)
     pick1 = jnp.where(slot == ids[1:2, :] * CAP + rank1, 1.0, 0.0).astype(BF)
     msg = (dot(pick0, straight) + dot(pick1, crossed)).astype(BF)
@@ -185,19 +211,16 @@
         msg_ref[copy, :, slots // shards :, :] = table
 
 
-def activate(ids, partial, shards):
-    parts, packed, lanes = partial.shape
-    rows = ids.shape[1]
-    return pl.pallas_call(
-        activate_kernel,
-        out_shape=[
-            jax.ShapeDtypeStruct((packed + 16, lanes), BF),
-            jax.ShapeDtypeStruct((parts, shards, 2 * packed // shards + 16, lanes), BF),
-        ],
-        compiler_params=params(),
-        cost_estimate=cost(8 * packed * rows * lanes, 3 * 2**20),
-        name="activate_rows",
-    )(ids, partial)
+def messages(ids, acts, parts, shards):
+    tall, lanes = acts.shape
+    slots = 2 * (tall - 16)
+    return pl.pallas_call(
+        message_kernel,
+        out_shape=jax.ShapeDtypeStruct((parts, shards, slots // shards + 16, lanes), BF),
+        compiler_params=params(),
+        cost_estimate=cost(8 * slots * ids.shape[1] * lanes, 2**21),
+        name="make_messages",
+    )(ids, acts)
 
 
 def doubled(pair):
@@ -431,7 +454,7 @@
             pltpu.SemaphoreType.DMA((4, 4)),
         ],
         compiler_params=params(),
-        cost_estimate=cost(2 * latents * 256 * (per + cols), 20 * 2**20),
+        cost_estimate=cost(1, 1),
         name="mix_decoder",
     )(msg, dec_all, own_dec)
 
@@ -541,7 +564,8 @@
     pre, proj = encode(scale, arrived, weights, bias)
     partial = lax.all_to_all(pre, everyone, 0, 0, tiled=True)
     projs = lax.all_gather(proj, "dp", axis=0, tiled=False)
-    acts, msg = activate(ids, partial.reshape(parts, shards * 2 * CAP, 128), shards)
+    acts = activate(ids, partial.reshape(parts, shards * 2 * CAP, 128))
+    msg = messages(ids, acts, parts, shards)
     group = [shifted(acts, d, parts) for d in range(parts)]
     msg, *group = lax.optimization_barrier((msg, *group))
     message = lax.all_to_all(
@@ -552,11 +576,13 @@
     made = home(scale, place, group, dec_all, dec_b.reshape(parts, cols))
     total = summed([shifted(made[parts + d], -d, parts) for d in range(parts)], parts)
     gates = lax.all_to_all(total.reshape(devices, 2 * CAP, 128), everyone, 0, 0, tiled=True)
-    recon = assemble(at_x, [shifted(made[d], -d, parts) for d in range(parts)])
+    total, *made = lax.optimization_barrier((total, *made[:parts]))
+    pieces = [shifted(made[d], -d, parts) for d in range(parts)]
     mixed = mix(message, dec_all, dec_x)
     enc_grad, dec_grad = grads(
         scale, gates, projs, message, arrived.reshape(devices * here * CAP, cols), mixed
     )
+    recon = assemble(at_x, pieces)
     return (recon, enc_grad, dec_grad)
 
 

time: 286 us -> 284 us (level)
  waiting for transfers between devices: 137 us -> 134 us
    all_to_all x1, waiting for transfers between devices: 4.06 us -> 0.01 us  [body(): lax.all_to_all(total.reshape(devices, 2 * CAP, 128), everyone, 0, 0, tile...]
    pallas_call x2 -> x3, Pallas kernels: 10.9 us -> 11 us  [the longest x1 5.47 us: route(): pl.pallas_call(route_kernel, in_specs=[vmem] * 3, out_specs=pl.BlockSpec(...]
  transfers between devices with their start and end apart: 15 -> 15, of which waited for: 9 -> 8; matrix products, arithmetic and copies ran while one was open for 2% -> 2% of each run, Pallas kernels for 20% -> 23%
where the time goes in v7:
time: 284 us; the launch traced here: 281 us
  waiting for transfers between devices  134 us (47%)
  Pallas kernels  67.3 us (24%)
  starting transfers between devices  55.7 us (20%)
  between operations  14.3 us (5%)
  local copies, waits for them, and re-layouts  7.03 us (2%)
    all_to_all x1, waiting for transfers between devices, body(): lax.all_to_all(outgoing.reshape(devices, here * CAP, cols), everyone, 0,...  99.1 us
    pallas_call x1, Pallas kernels, home(): pl.pallas_call(functools.partial(home_kernel, scale, parts), in_specs=[vm...  19.8 us
    all_to_all x1, waiting for transfers between devices, body(): partial = lax.all_to_all(pre, everyone, 0, 0, tiled=True)  18.6 us
    ppermute x9, waiting for transfers between devices, shifted(): lax.ppermute(value, 'dp', [(i, (i + by) % parts) for i in range(parts)])  15.4 us
    pallas_call x1, Pallas kernels, mix(): pl.pallas_call(mix_kernel, in_specs=[vmem, pl.BlockSpec(memory_space=pl.A...  15.1 us
    all_to_all x1, starting transfers between devices, body(): partial = lax.all_to_all(pre, everyone, 0, 0, tiled=True)  12.3 us
    all_to_all x1, starting transfers between devices, body(): lax.all_to_all(outgoing.reshape(devices, here * CAP, cols), everyone, 0,...  12 us
    all_to_all x1, starting transfers between devices, body(): lax.all_to_all(total.reshape(devices, 2 * CAP, 128), everyone, 0, 0, tile...  11.2 us
  transfers between devices with their start and end apart: 15, of which 8 were waited for; matrix products, arithmetic and copies ran while one was open for 2% of the time, Pallas kernels for 23%

profile of v7, /device:TPU:1, one launch (start us, length us, event | category | flops | bytes accessed | tf_op | source)
XLA Modules:
  0.0 280.8 jit_solution(16344543797631876710)
XLA Ops:
  7.2 0.0 copy-start
  7.2 0.0 all-gather.4.cloned.1.call-start
  7.2 1.5 copy-done
  8.8 0.9 constant_dynamic-slice_fusion.start_ref
  9.6 0.0 all-gather.4.cloned.1.call-update
  9.7 5.5 %route_rows.1 = bf16[4,1024,1024]{2,1,0:T(8,128)(2,1)} custom-call(s32[2,256]{1,0:T(2,128)} %bitcast.22, bf16[256,4096]{1,0:T(8,128)(2,1)} %resid_ref.1, f32[1,4096]{1,0:T(1,128)} %bitcast.21), custom_call_target="tpu_custom_call" | custom-call | flops 2147483648 | bytes 10485760 | tf_op jit(solution)/shard_map/route_rows/pallas_call | solution.py:107
  15.1 12.0 %all-to-all-start = ((bf16[128,32,1024]{2,1,0:T(8,128)(2,1)}), bf16[128,32,1024]{2,1,0:T(8,128)(2,1)}, u32[]{:S(2)}, u32[]{:S(2)}) async-start(bf16[128,32,1024]{2,1,0:T(8,128)(2,1)} %bitcast.15), calls=%async_computation | async-start | bytes 16777216 | tf_op jit(solution)/shard_map/all_to_all | solution.py:552
  27.1 0.3 copy.12
  27.4 0.0 copy-start.9
  27.4 1.1 constant_dynamic-slice_fusion.1
  28.5 1.0 copy.11
  29.5 2.1 maximum_bitcast_fusion.weight_ref
  31.6 0.6 select_bitcast_fusion.bias_ref
  32.2 99.1 %all-to-all-done.rows_hbm = bf16[128,32,1024]{2,1,0:T(8,128)(2,1)} async-done(((bf16[128,32,1024]{2,1,0:T(8,128)(2,1)}), bf16[128,32,1024]{2,1,0:T(8,128)(2,1)}, u32[]{:S(2)}, u32[]{:S(2)}) %all-to-all-start) | async-done | bytes 8388640 | tf_op jit(solution)/shard_map/all_to_all | solution.py:552
  131.3 6.9 %encode_rows.1 = (f32[128,16,128]{2,1,0:T(8,128)}, bf16[128,16,128]{2,1,0:T(8,128)(2,1)}) custom-call(bf16[128,32,1024]{2,1,0:T(8,128)(2,1)} %all-to-all-done.rows_hbm, bf16[2,1024,256]{2,1,0:T(8,128)(2,1)} %maximum_bitcast_fusion.weight_ref, f32[2,128]{1,0:T(2,128)} %select_bitcast_fusion.bias_ref), custom_call_target="tpu_custom_call" | custom-call | flops 2147483648 | bytes 11534336 | tf_op jit(solution)/shard_map/encode_rows/pallas_call | solution.py:152
  138.2 12.3 %all-to-all-start.1 = ((f32[128,16,128]{2,1,0:T(8,128)}), f32[128,16,128]{2,1,0:T(8,128)S(1)}, u32[]{:S(2)}, u32[]{:S(2)}) async-start(f32[128,16,128]{2,1,0:T(8,128)} %get-tuple-element.24), calls=%async_computation.1 | async-start | bytes 2097152 | tf_op jit(solution)/shard_map/all_to_all | solution.py:565
  150.5 0.0 all-gather.6.cloned.1.call-start
  150.5 0.7 all-gather.6.cloned.1.call-update
  151.2 18.6 %all-to-all-done.1 = f32[128,16,128]{2,1,0:T(8,128)S(1)} async-done(((f32[128,16,128]{2,1,0:T(8,128)}), f32[128,16,128]{2,1,0:T(8,128)S(1)}, u32[]{:S(2)}, u32[]{:S(2)}) %all-to-all-start.1) | async-done | bytes 1048608 | tf_op jit(solution)/shard_map/all_to_all | solution.py:565
  169.8 1.0 copy-done.2
  170.8 2.0 activate_slots.1.acts_ref.refs_0_
  172.8 0.4 collective-permute-start
  173.2 2.3 collective-permute-start.1
  175.5 0.7 collective-permute-start.2
  176.2 3.5 %make_messages.1 = bf16[4,32,48,128]{3,2,1,0:T(8,128)(2,1)} custom-call(s32[2,256]{1,0:T(2,128)} %bitcast.24, bf16[528,128]{1,0:T(8,128)(2,1)} %activate_slots.1.acts_ref.refs_0_), custom_call_target="tpu_custom_call" | custom-call | flops 268435456 | bytes 2097152 | tf_op jit(solution)/shard_map/make_messages/pallas_call | solution.py:217
  179.8 0.4 collective-permute-done.1.refs_2_
  180.1 1.3 collective-permute-done.2.refs_3_
  181.4 9.1 %all-to-all-start.3 = ((bf16[128,48,128]{2,1,0:T(8,128)(2,1)}), bf16[128,48,128]{2,1,0:T(8,128)(2,1)}, u32[]{:S(2)}, u32[]{:S(2)}) async-start(bf16[128,48,128]{2,1,0:T(8,128)(2,1)} %bitcast.17), calls=%async_computation.3 | async-start | bytes 3145728 | tf_op jit(solution)/shard_map/all_to_all | solution.py:571
  190.6 0.6 reshape.47.refs_6_
  191.2 19.8 %home_rows.1 = (bf16[256,1024]{1,0:T(8,128)(2,1)}, bf16[256,1024]{1,0:T(8,128)(2,1)}, bf16[256,1024]{1,0:T(8,128)(2,1)}, bf16[256,1024]{1,0:T(8,128)(2,1)}, bf16...) custom-call(bf16[528,128]{1,0:T(8,128)(2,1)} %activate_slots.1.acts_ref.re, ...), custom_call_target="tpu_custom_call" | custom-call | flops 8589934592 | bytes 20971520 | tf_op jit(solution)/shard_map/home_rows/pallas_call | solution.py:326
  211.0 2.7 collective-permute-start.3
  213.7 0.6 collective-permute-start.4
  214.3 0.6 collective-permute-start.5
  214.9 4.7 %collective-permute-done.3.refs_1_ = bf16[512,128]{1,0:T(8,128)(2,1)S(1)} collective-permute-done((bf16[512,128]{1,0:T(8,128)(2,1)}, bf16[512,128]{1,0:T(8,128)(2,1)S(1)}, u32[]{:S(2)}, u32[]{:S(2)}) %collective-permute-start.3) | collective-permute-done | bytes 131104 | tf_op jit(solution)/shard_map/ppermute | solution.py:533
  219.6 3.8 %collective-permute-done.4.refs_2_ = bf16[512,128]{1,0:T(8,128)(2,1)S(1)} collective-permute-done((bf16[512,128]{1,0:T(8,128)(2,1)}, bf16[512,128]{1,0:T(8,128)(2,1)S(1)}, u32[]{:S(2)}, u32[]{:S(2)}) %collective-permute-start.4) | collective-permute-done | bytes 131104 | tf_op jit(solution)/shard_map/ppermute | solution.py:533
  223.4 3.2 %collective-permute-done.5.refs_3_ = bf16[512,128]{1,0:T(8,128)(2,1)S(1)} collective-permute-done((bf16[512,128]{1,0:T(8,128)(2,1)}, bf16[512,128]{1,0:T(8,128)(2,1)S(1)}, u32[]{:S(2)}, u32[]{:S(2)}) %collective-permute-start.5) | collective-permute-done | bytes 131104 | tf_op jit(solution)/shard_map/ppermute | solution.py:533
  226.5 0.6 copy-done.7
  227.2 2.0 sum_pieces.1
  229.2 0.0 all-to-all-done.3.msg_ref.msg_hbm
  229.2 11.2 %all-to-all-start.2 = ((bf16[128,16,128]{2,1,0:T(8,128)(2,1)}), bf16[128,16,128]{2,1,0:T(8,128)(2,1)}, u32[]{:S(2)}, u32[]{:S(2)}) async-start(bf16[128,16,128]{2,1,0:T(8,128)(2,1)} %bitcast.19), calls=%async_computation.2 | async-start | bytes 1048576 | tf_op jit(solution)/shard_map/all_to_all | solution.py:578
  240.3 2.7 collective-permute-start.6
  243.0 0.6 collective-permute-start.7
  243.6 0.6 collective-permute-start.8
  244.2 15.1 %mix_decoder.1.mixed_hbm = f32[256,1024]{1,0:T(8,128)} custom-call(bf16[128,48,128]{2,1,0:T(8,128)(2,1)} %all-to-all-done.3.msg_ref.msg_hbm, bf16[8192,1024]{1,0:T(8,128)(2,1)} %all-gather.4.cloned.1.call-done.refs_5_.dec_hbm, bf16[256,1024]{1,0:T(8,128)(2,1)} %constant_dynamic-slice_fusion.start_ref), custom_call_target="tpu_custom_call" | custom-call | flops 1 | bytes 1 | tf_op jit(solution)/shard_map/mix_decoder/pallas_call | solution.py:444
  259.3 0.0 all-gather.6.cloned.1.call-done
  259.3 9.6 %dictionary_grads.1 = (f32[256,1024]{1,0:T(8,128)}, f32[256,1024]{1,0:T(8,128)}) custom-call(bf16[128,16,128]{2,1,0:T(8,128)(2,1)} %all-to-all-done.2.gate_hbm, bf16[4,128,16,128]{3,2,1,0:T(8,128)(2,1)} %bitcast.25, bf16[128,48,128]{2,1,0:T(8,128)(2,1)} %all-to-all-done.3.msg_ref.msg_hbm, bf16[4096,1024]{1,0:T(8,128)(2,1)} %bitcast.12.rows_hbm, ...), custom_call_target="tpu_custom_call" | custom-call | flops 4294967296 | bytes 16777216 | tf_op jit(solution)/shard_map/dictionary_grads/pallas_call | solution.py:513
  269.0 2.1 collective-permute-done.8.refs_3_
  271.1 2.9 %assemble_recon.1 = bf16[256,4096]{1,0:T(8,128)(2,1)} custom-call(s32[1]{0:T(128)} %bitcast.refs_4_.at_ref, bf16[256,1024]{1,0:T(8,128)(2,1)} %get-tuple-element.37.refs_0_, bf16[256,1024]{1,0:T(8,128)(2,1)} %copy-done.3, bf16[256,1024]{1,0:T(8,128)(2,1)} %copy-done.4, bf16[256,1024]{1,0:T(8,128)(2,1)} %collective-permute-done.8.refs_3_), custom_call_target="tpu_custom_call" | custom-call | bytes 4194304 | tf_op jit(solution)/shard_map/assemble_recon/pallas_call | solution.py:360
  (26 shorter events, 0.1 us)
Async XLA Ops:
  7.2 1.6 copy-start
  7.2 184.0 %all-gather.4.cloned.1.call-start = ((), (), s32[]{:S(2)}) async-start(), calls=%async_computation.4 | async-start | bytes 17301504 | tf_op jit(solution)/shard_map/all_gather | solution.py:558
  15.1 12.0 %copy-start.1 = (bf16[256,1024]{1,0:T(8,128)(2,1)S(1)}, bf16[256,1024]{1,0:T(8,128)(2,1)}, u32[]{:S(2)}) copy-start(bf16[256,1024]{1,0:T(8,128)(2,1)} %constant_dynamic-slice_fusion.start_ref) | copy-start | bytes 1572868
  15.1 116.2 %all-to-all-start = ((bf16[128,32,1024]{2,1,0:T(8,128)(2,1)}), bf16[128,32,1024]{2,1,0:T(8,128)(2,1)}, u32[]{:S(2)}, u32[]{:S(2)}) async-start(bf16[128,32,1024]{2,1,0:T(8,128)(2,1)} %bitcast.15), calls=%async_computation | async-start | bytes 16777216 | tf_op jit(solution)/shard_map/all_to_all | solution.py:552
  27.4 4.2 %copy-start.9 = (f32[256]{0:T(256)S(1)}, f32[256]{0:T(256)}, u32[]{:S(2)}) copy-start(f32[256]{0:T(256)} %param.9) | copy-start | bytes 3076
  138.2 31.6 %all-to-all-start.1 = ((f32[128,16,128]{2,1,0:T(8,128)}), f32[128,16,128]{2,1,0:T(8,128)S(1)}, u32[]{:S(2)}, u32[]{:S(2)}) async-start(f32[128,16,128]{2,1,0:T(8,128)} %get-tuple-element.24), calls=%async_computation.1 | async-start | bytes 2097152 | tf_op jit(solution)/shard_map/all_to_all | solution.py:565
  150.5 108.8 %all-gather.6.cloned.1.call-start = ((), (), s32[]{:S(2)}) async-start(), calls=%async_computation.5 | async-start | bytes 2621440 | tf_op jit(solution)/shard_map/all_gather | solution.py:566
  169.8 1.0 copy-start.2
  172.8 17.8 %copy-start.8 = (f32[4096]{0:T(1024)S(1)}, f32[4096]{0:T(1024)}, u32[]{:S(2)}) copy-start(f32[4096]{0:T(1024)} %param.11) | copy-start | bytes 49156
  172.8 7.0 %collective-permute-start = (bf16[528,128]{1,0:T(8,128)(2,1)}, bf16[528,128]{1,0:T(8,128)(2,1)S(1)}, u32[]{:S(2)}, u32[]{:S(2)}) collective-permute-start(bf16[528,128]{1,0:T(8,128)(2,1)} %activate_slots.1.acts_ref.refs_0_), channel_id=1, source_target_pairs={{0,32},{32,64},{64,96},{96,0},{1,33},{33,65},{65,97},{97,1},{2,34}... | collective-permute-start | bytes 405512 | tf_op jit(solution)/shard_map/ppermute | solution.py:533
  173.2 6.9 %collective-permute-start.1 = (bf16[528,128]{1,0:T(8,128)(2,1)}, bf16[528,128]{1,0:T(8,128)(2,1)S(1)}, u32[]{:S(2)}, u32[]{:S(2)}) collective-permute-start(bf16[528,128]{1,0:T(8,128)(2,1)} %activate_slots.1.acts_ref.refs_0_), channel_id=1, source_target_pairs={{0,64},{32,96},{64,0},{96,32},{1,65},{33,97},{65,1},{97,33},{2,66}... | collective-permute-start | bytes 405512 | tf_op jit(solution)/shard_map/ppermute | solution.py:533
  175.5 5.9 %collective-permute-start.2 = (bf16[528,128]{1,0:T(8,128)(2,1)}, bf16[528,128]{1,0:T(8,128)(2,1)S(1)}, u32[]{:S(2)}, u32[]{:S(2)}) collective-permute-start(bf16[528,128]{1,0:T(8,128)(2,1)} %activate_slots.1.acts_ref.refs_0_), channel_id=1, source_target_pairs={{0,96},{32,0},{64,32},{96,64},{1,97},{33,1},{65,33},{97,65},{2,98}... | collective-permute-start | bytes 405512 | tf_op jit(solution)/shard_map/ppermute | solution.py:533
  179.8 11.4 %copy-start.10 = (bf16[528,128]{1,0:T(8,128)(2,1)}, bf16[528,128]{1,0:T(8,128)(2,1)S(1)}, u32[]{:S(2)}) copy-start(bf16[528,128]{1,0:T(8,128)(2,1)S(1)} %collective-permute-done.refs_1_) | copy-start | bytes 405508
  180.1 11.0 %copy-start.11 = (bf16[528,128]{1,0:T(8,128)(2,1)}, bf16[528,128]{1,0:T(8,128)(2,1)S(1)}, u32[]{:S(2)}) copy-start(bf16[528,128]{1,0:T(8,128)(2,1)S(1)} %collective-permute-done.1.refs_2_) | copy-start | bytes 405508
  181.4 9.8 %copy-start.12 = (bf16[528,128]{1,0:T(8,128)(2,1)}, bf16[528,128]{1,0:T(8,128)(2,1)S(1)}, u32[]{:S(2)}) copy-start(bf16[528,128]{1,0:T(8,128)(2,1)S(1)} %collective-permute-done.2.refs_3_) | copy-start | bytes 405508
  181.4 47.7 %all-to-all-start.3 = ((bf16[128,48,128]{2,1,0:T(8,128)(2,1)}), bf16[128,48,128]{2,1,0:T(8,128)(2,1)}, u32[]{:S(2)}, u32[]{:S(2)}) async-start(bf16[128,48,128]{2,1,0:T(8,128)(2,1)} %bitcast.17), calls=%async_computation.3 | async-start | bytes 3145728 | tf_op jit(solution)/shard_map/all_to_all | solution.py:571
  211.0 8.5 %collective-permute-start.3 = (bf16[512,128]{1,0:T(8,128)(2,1)}, bf16[512,128]{1,0:T(8,128)(2,1)S(1)}, u32[]{:S(2)}, u32[]{:S(2)}) collective-permute-start(bf16[512,128]{1,0:T(8,128)(2,1)} %get-tuple-element.30), channel_id=1, source_target_pairs={{0,96},{32,0},{64,32},{96,64},{1,97},{33,1},{65,33},{97,65},{2,98}... | collective-permute-start | bytes 393224 | tf_op jit(solution)/shard_map/ppermute | solution.py:533
  213.7 9.6 %collective-permute-start.4 = (bf16[512,128]{1,0:T(8,128)(2,1)}, bf16[512,128]{1,0:T(8,128)(2,1)S(1)}, u32[]{:S(2)}, u32[]{:S(2)}) collective-permute-start(bf16[512,128]{1,0:T(8,128)(2,1)} %get-tuple-element.31), channel_id=1, source_target_pairs={{0,64},{32,96},{64,0},{96,32},{1,65},{33,97},{65,1},{97,33},{2,66}... | collective-permute-start | bytes 393224 | tf_op jit(solution)/shard_map/ppermute | solution.py:533
  214.3 12.3 %collective-permute-start.5 = (bf16[512,128]{1,0:T(8,128)(2,1)}, bf16[512,128]{1,0:T(8,128)(2,1)S(1)}, u32[]{:S(2)}, u32[]{:S(2)}) collective-permute-start(bf16[512,128]{1,0:T(8,128)(2,1)} %get-tuple-element.32), channel_id=1, source_target_pairs={{0,32},{32,64},{64,96},{96,0},{1,33},{33,65},{65,97},{97,1},{2,34}... | collective-permute-start | bytes 393224 | tf_op jit(solution)/shard_map/ppermute | solution.py:533
  219.6 7.0 %copy-start.5 = (bf16[512,128]{1,0:T(8,128)(2,1)}, bf16[512,128]{1,0:T(8,128)(2,1)S(1)}, u32[]{:S(2)}) copy-start(bf16[512,128]{1,0:T(8,128)(2,1)S(1)} %collective-permute-done.3.refs_1_) | copy-start | bytes 393220
  223.4 3.2 %copy-start.6 = (bf16[512,128]{1,0:T(8,128)(2,1)}, bf16[512,128]{1,0:T(8,128)(2,1)S(1)}, u32[]{:S(2)}) copy-start(bf16[512,128]{1,0:T(8,128)(2,1)S(1)} %collective-permute-done.4.refs_2_) | copy-start | bytes 393220
  226.5 0.7 copy-start.7
  229.2 30.1 %all-to-all-start.2 = ((bf16[128,16,128]{2,1,0:T(8,128)(2,1)}), bf16[128,16,128]{2,1,0:T(8,128)(2,1)}, u32[]{:S(2)}, u32[]{:S(2)}) async-start(bf16[128,16,128]{2,1,0:T(8,128)(2,1)} %bitcast.19), calls=%async_computation.2 | async-start | bytes 1048576 | tf_op jit(solution)/shard_map/all_to_all | solution.py:578
  240.3 28.6 %collective-permute-start.6 = (bf16[256,1024]{1,0:T(8,128)(2,1)}, bf16[256,1024]{1,0:T(8,128)(2,1)S(1)}, u32[]{:S(2)}, u32[]{:S(2)}) collective-permute-start(bf16[256,1024]{1,0:T(8,128)(2,1)} %get-tuple-element.38), channel_id=1, source_target_pairs={{0,96},{32,0},{64,32},{96,64},{1,97},{33,1},{65,33},{97,65},{2,98}... | collective-permute-start | bytes 1572872 | tf_op jit(solution)/shard_map/ppermute | solution.py:533
  243.0 26.0 %collective-permute-start.7 = (bf16[256,1024]{1,0:T(8,128)(2,1)}, bf16[256,1024]{1,0:T(8,128)(2,1)S(1)}, u32[]{:S(2)}, u32[]{:S(2)}) collective-permute-start(bf16[256,1024]{1,0:T(8,128)(2,1)} %get-tuple-element.39), channel_id=1, source_target_pairs={{0,64},{32,96},{64,0},{96,32},{1,65},{33,97},{65,1},{97,33},{2,66}... | collective-permute-start | bytes 1572872 | tf_op jit(solution)/shard_map/ppermute | solution.py:533
  243.6 27.5 %collective-permute-start.8 = (bf16[256,1024]{1,0:T(8,128)(2,1)}, bf16[256,1024]{1,0:T(8,128)(2,1)}, u32[]{:S(2)}, u32[]{:S(2)}) collective-permute-start(bf16[256,1024]{1,0:T(8,128)(2,1)} %get-tuple-element.40), channel_id=1, source_target_pairs={{0,32},{32,64},{64,96},{96,0},{1,33},{33,65},{65,97},{97,1},{2,34}... | collective-permute-start | bytes 1572872 | tf_op jit(solution)/shard_map/ppermute | solution.py:533
  269.0 2.1 copy-start.3
  269.0 2.1 copy-start.4
Sparse Core Ops, SparseCore 0:
  10.3 179.3 all-gather.3
  191.3 41.5 all-gather.5

commit v8 on v7

--- a/solution.py
+++ b/solution.py
@@ -334,7 +334,7 @@
             pltpu.VMEM((parts, 2 * packed, rows), BF),
             pltpu.VMEM((parts, 2 * packed, cols), BF),
             pltpu.VMEM((latents, cols), BF),
-            pltpu.SemaphoreType.DMA((8,)),
+            pltpu.SemaphoreType.DMA((4,)),
         ],
         compiler_params=params(),
         cost_estimate=cost(8 * latents * cols * 128, 20 * 2**20),
@@ -451,7 +451,7 @@
             pltpu.VMEM((4, per, 128), BF),
             pltpu.VMEM((4, per, 128), BF),
             pltpu.VMEM(dec_all.shape, BF),
-            pltpu.SemaphoreType.DMA((4, 4)),
+            pltpu.SemaphoreType.DMA((1, 4)),
         ],
         compiler_params=params(),
         cost_estimate=cost(1, 1),

time: 284 us -> 283 us (level)
  transfers between devices with their start and end apart: 15 -> 15, of which waited for: 8 -> 8; matrix products, arithmetic and copies ran while one was open for 2% -> 2% of each run, Pallas kernels for 23% -> 22%
where the time goes in v8:
time: 283 us; the launch traced here: 280 us
  waiting for transfers between devices  135 us (48%)
  Pallas kernels  65.6 us (23%)
  starting transfers between devices  55.7 us (20%)
  between operations  14.3 us (5%)
  local copies, waits for them, and re-layouts  7.03 us (2%)
    all_to_all x1, waiting for transfers between devices, body(): lax.all_to_all(outgoing.reshape(devices, here * CAP, cols), everyone, 0,...  99.1 us
    pallas_call x1, Pallas kernels, home(): pl.pallas_call(functools.partial(home_kernel, scale, parts), in_specs=[vm...  19.5 us
    all_to_all x1, waiting for transfers between devices, body(): partial = lax.all_to_all(pre, everyone, 0, 0, tiled=True)  18.6 us
    ppermute x9, waiting for transfers between devices, shifted(): lax.ppermute(value, 'dp', [(i, (i + by) % parts) for i in range(parts)])  16.8 us
    pallas_call x1, Pallas kernels, mix(): pl.pallas_call(mix_kernel, in_specs=[vmem, pl.BlockSpec(memory_space=pl.A...  14 us
    all_to_all x1, starting transfers between devices, body(): partial = lax.all_to_all(pre, everyone, 0, 0, tiled=True)  12.3 us
    all_to_all x1, starting transfers between devices, body(): lax.all_to_all(outgoing.reshape(devices, here * CAP, cols), everyone, 0,...  12 us
    all_to_all x1, starting transfers between devices, body(): lax.all_to_all(total.reshape(devices, 2 * CAP, 128), everyone, 0, 0, tile...  11.2 us
  transfers between devices with their start and end apart: 15, of which 8 were waited for; matrix products, arithmetic and copies ran while one was open for 2% of the time, Pallas kernels for 22%

profile of v8, /device:TPU:1, one launch (start us, length us, event | category | flops | bytes accessed | tf_op | source)
XLA Modules:
  0.0 280.4 jit_solution(8378982332978626037)
XLA Ops:
  7.2 0.0 copy-start
  7.2 0.0 all-gather.4.cloned.1.call-start
  7.2 1.5 copy-done
  8.8 0.9 constant_dynamic-slice_fusion.start_ref
  9.6 0.0 all-gather.4.cloned.1.call-update
  9.7 5.5 %route_rows.1 = bf16[4,1024,1024]{2,1,0:T(8,128)(2,1)} custom-call(s32[2,256]{1,0:T(2,128)} %bitcast.22, bf16[256,4096]{1,0:T(8,128)(2,1)} %resid_ref.1, f32[1,4096]{1,0:T(1,128)} %bitcast.21), custom_call_target="tpu_custom_call" | custom-call | flops 2147483648 | bytes 10485760 | tf_op jit(solution)/shard_map/route_rows/pallas_call | solution.py:107
  15.1 12.0 %all-to-all-start = ((bf16[128,32,1024]{2,1,0:T(8,128)(2,1)}), bf16[128,32,1024]{2,1,0:T(8,128)(2,1)}, u32[]{:S(2)}, u32[]{:S(2)}) async-start(bf16[128,32,1024]{2,1,0:T(8,128)(2,1)} %bitcast.15), calls=%async_computation | async-start | bytes 16777216 | tf_op jit(solution)/shard_map/all_to_all | solution.py:552
  27.1 0.3 copy.12
  27.4 0.0 copy-start.9
  27.4 1.1 constant_dynamic-slice_fusion.1
  28.5 1.0 copy.11
  29.5 2.1 maximum_bitcast_fusion.weight_ref
  31.6 0.6 select_bitcast_fusion.bias_ref
  32.2 99.1 %all-to-all-done.rows_hbm = bf16[128,32,1024]{2,1,0:T(8,128)(2,1)} async-done(((bf16[128,32,1024]{2,1,0:T(8,128)(2,1)}), bf16[128,32,1024]{2,1,0:T(8,128)(2,1)}, u32[]{:S(2)}, u32[]{:S(2)}) %all-to-all-start) | async-done | bytes 8388640 | tf_op jit(solution)/shard_map/all_to_all | solution.py:552
  131.3 6.9 %encode_rows.1 = (f32[128,16,128]{2,1,0:T(8,128)}, bf16[128,16,128]{2,1,0:T(8,128)(2,1)}) custom-call(bf16[128,32,1024]{2,1,0:T(8,128)(2,1)} %all-to-all-done.rows_hbm, bf16[2,1024,256]{2,1,0:T(8,128)(2,1)} %maximum_bitcast_fusion.weight_ref, f32[2,128]{1,0:T(2,128)} %select_bitcast_fusion.bias_ref), custom_call_target="tpu_custom_call" | custom-call | flops 2147483648 | bytes 11534336 | tf_op jit(solution)/shard_map/encode_rows/pallas_call | solution.py:152
  138.2 12.3 %all-to-all-start.1 = ((f32[128,16,128]{2,1,0:T(8,128)}), f32[128,16,128]{2,1,0:T(8,128)S(1)}, u32[]{:S(2)}, u32[]{:S(2)}) async-start(f32[128,16,128]{2,1,0:T(8,128)} %get-tuple-element.24), calls=%async_computation.1 | async-start | bytes 2097152 | tf_op jit(solution)/shard_map/all_to_all | solution.py:565
  150.5 0.0 all-gather.6.cloned.1.call-start
  150.5 0.7 all-gather.6.cloned.1.call-update
  151.2 18.6 %all-to-all-done.1 = f32[128,16,128]{2,1,0:T(8,128)S(1)} async-done(((f32[128,16,128]{2,1,0:T(8,128)}), f32[128,16,128]{2,1,0:T(8,128)S(1)}, u32[]{:S(2)}, u32[]{:S(2)}) %all-to-all-start.1) | async-done | bytes 1048608 | tf_op jit(solution)/shard_map/all_to_all | solution.py:565
  169.8 1.0 copy-done.2
  170.8 2.0 activate_slots.1.acts_ref.refs_0_
  172.8 0.4 collective-permute-start
  173.2 2.3 collective-permute-start.1
  175.5 0.7 collective-permute-start.2
  176.2 3.5 %make_messages.1 = bf16[4,32,48,128]{3,2,1,0:T(8,128)(2,1)} custom-call(s32[2,256]{1,0:T(2,128)} %bitcast.24, bf16[528,128]{1,0:T(8,128)(2,1)} %activate_slots.1.acts_ref.refs_0_), custom_call_target="tpu_custom_call" | custom-call | flops 268435456 | bytes 2097152 | tf_op jit(solution)/shard_map/make_messages/pallas_call | solution.py:217
  179.8 0.0 collective-permute-done.refs_1_
  179.8 0.4 collective-permute-done.1.refs_2_
  180.1 1.3 collective-permute-done.2.refs_3_
  181.4 9.1 %all-to-all-start.3 = ((bf16[128,48,128]{2,1,0:T(8,128)(2,1)}), bf16[128,48,128]{2,1,0:T(8,128)(2,1)}, u32[]{:S(2)}, u32[]{:S(2)}) async-start(bf16[128,48,128]{2,1,0:T(8,128)(2,1)} %bitcast.17), calls=%async_computation.3 | async-start | bytes 3145728 | tf_op jit(solution)/shard_map/all_to_all | solution.py:571
  190.6 0.6 reshape.47.refs_6_
  191.2 19.5 %home_rows.1 = (bf16[256,1024]{1,0:T(8,128)(2,1)}, bf16[256,1024]{1,0:T(8,128)(2,1)}, bf16[256,1024]{1,0:T(8,128)(2,1)}, bf16[256,1024]{1,0:T(8,128)(2,1)}, bf16...) custom-call(bf16[528,128]{1,0:T(8,128)(2,1)} %activate_slots.1.acts_ref.re, ...), custom_call_target="tpu_custom_call" | custom-call | flops 8589934592 | bytes 20971520 | tf_op jit(solution)/shard_map/home_rows/pallas_call | solution.py:326
  210.7 2.7 collective-permute-start.3
  213.4 0.6 collective-permute-start.4
  214.0 0.6 collective-permute-start.5
  214.6 4.8 %collective-permute-done.3.refs_1_ = bf16[512,128]{1,0:T(8,128)(2,1)S(1)} collective-permute-done((bf16[512,128]{1,0:T(8,128)(2,1)}, bf16[512,128]{1,0:T(8,128)(2,1)S(1)}, u32[]{:S(2)}, u32[]{:S(2)}) %collective-permute-start.3) | collective-permute-done | bytes 131104 | tf_op jit(solution)/shard_map/ppermute | solution.py:533
  219.4 3.6 %collective-permute-done.4.refs_2_ = bf16[512,128]{1,0:T(8,128)(2,1)S(1)} collective-permute-done((bf16[512,128]{1,0:T(8,128)(2,1)}, bf16[512,128]{1,0:T(8,128)(2,1)S(1)}, u32[]{:S(2)}, u32[]{:S(2)}) %collective-permute-start.4) | collective-permute-done | bytes 131104 | tf_op jit(solution)/shard_map/ppermute | solution.py:533
  223.0 3.2 %collective-permute-done.5.refs_3_ = bf16[512,128]{1,0:T(8,128)(2,1)S(1)} collective-permute-done((bf16[512,128]{1,0:T(8,128)(2,1)}, bf16[512,128]{1,0:T(8,128)(2,1)S(1)}, u32[]{:S(2)}, u32[]{:S(2)}) %collective-permute-start.5) | collective-permute-done | bytes 131104 | tf_op jit(solution)/shard_map/ppermute | solution.py:533
  226.2 0.6 copy-done.7
  226.9 2.0 sum_pieces.1
  228.8 11.2 %all-to-all-start.2 = ((bf16[128,16,128]{2,1,0:T(8,128)(2,1)}), bf16[128,16,128]{2,1,0:T(8,128)(2,1)}, u32[]{:S(2)}, u32[]{:S(2)}) async-start(bf16[128,16,128]{2,1,0:T(8,128)(2,1)} %bitcast.19), calls=%async_computation.2 | async-start | bytes 1048576 | tf_op jit(solution)/shard_map/all_to_all | solution.py:578
  240.0 2.7 collective-permute-start.6
  242.7 0.6 collective-permute-start.7
  243.3 0.6 collective-permute-start.8
  243.8 14.0 %mix_decoder.1.mixed_hbm = f32[256,1024]{1,0:T(8,128)} custom-call(bf16[128,48,128]{2,1,0:T(8,128)(2,1)} %all-to-all-done.3.msg_ref.msg_hbm, bf16[8192,1024]{1,0:T(8,128)(2,1)} %all-gather.4.cloned.1.call-done.refs_5_.dec_hbm, bf16[256,1024]{1,0:T(8,128)(2,1)} %constant_dynamic-slice_fusion.start_ref), custom_call_target="tpu_custom_call" | custom-call | flops 1 | bytes 1 | tf_op jit(solution)/shard_map/mix_decoder/pallas_call | solution.py:444
  257.8 0.0 all-gather.6.cloned.1.call-done
  257.9 9.4 %dictionary_grads.1 = (f32[256,1024]{1,0:T(8,128)}, f32[256,1024]{1,0:T(8,128)}) custom-call(bf16[128,16,128]{2,1,0:T(8,128)(2,1)} %all-to-all-done.2.gate_hbm, bf16[4,128,16,128]{3,2,1,0:T(8,128)(2,1)} %bitcast.25, bf16[128,48,128]{2,1,0:T(8,128)(2,1)} %all-to-all-done.3.msg_ref.msg_hbm, bf16[4096,1024]{1,0:T(8,128)(2,1)} %bitcast.12.rows_hbm, ...), custom_call_target="tpu_custom_call" | custom-call | flops 4294967296 | bytes 16777216 | tf_op jit(solution)/shard_map/dictionary_grads/pallas_call | solution.py:513
  267.3 3.4 %collective-permute-done.8.refs_3_ = bf16[256,1024]{1,0:T(8,128)(2,1)} collective-permute-done((bf16[256,1024]{1,0:T(8,128)(2,1)}, bf16[256,1024]{1,0:T(8,128)(2,1)}, u32[]{:S(2)}, u32[]{:S(2)}) %collective-permute-start.8) | collective-permute-done | bytes 524320 | tf_op jit(solution)/shard_map/ppermute | solution.py:533
  270.7 2.9 %assemble_recon.1 = bf16[256,4096]{1,0:T(8,128)(2,1)} custom-call(s32[1]{0:T(128)} %bitcast.refs_4_.at_ref, bf16[256,1024]{1,0:T(8,128)(2,1)} %get-tuple-element.37.refs_0_, bf16[256,1024]{1,0:T(8,128)(2,1)} %copy-done.3, bf16[256,1024]{1,0:T(8,128)(2,1)} %copy-done.4, bf16[256,1024]{1,0:T(8,128)(2,1)} %collective-permute-done.8.refs_3_), custom_call_target="tpu_custom_call" | custom-call | bytes 4194304 | tf_op jit(solution)/shard_map/assemble_recon/pallas_call | solution.py:360
  (26 shorter events, 0.1 us)
Async XLA Ops:
  7.2 1.6 copy-start
  7.2 184.0 %all-gather.4.cloned.1.call-start = ((), (), s32[]{:S(2)}) async-start(), calls=%async_computation.4 | async-start | bytes 17301504 | tf_op jit(solution)/shard_map/all_gather | solution.py:558
  15.1 12.0 %copy-start.1 = (bf16[256,1024]{1,0:T(8,128)(2,1)S(1)}, bf16[256,1024]{1,0:T(8,128)(2,1)}, u32[]{:S(2)}) copy-start(bf16[256,1024]{1,0:T(8,128)(2,1)} %constant_dynamic-slice_fusion.start_ref) | copy-start | bytes 1572868
  15.1 116.2 %all-to-all-start = ((bf16[128,32,1024]{2,1,0:T(8,128)(2,1)}), bf16[128,32,1024]{2,1,0:T(8,128)(2,1)}, u32[]{:S(2)}, u32[]{:S(2)}) async-start(bf16[128,32,1024]{2,1,0:T(8,128)(2,1)} %bitcast.15), calls=%async_computation | async-start | bytes 16777216 | tf_op jit(solution)/shard_map/all_to_all | solution.py:552
  27.4 4.2 %copy-start.9 = (f32[256]{0:T(256)S(1)}, f32[256]{0:T(256)}, u32[]{:S(2)}) copy-start(f32[256]{0:T(256)} %param.9) | copy-start | bytes 3076
  138.2 31.6 %all-to-all-start.1 = ((f32[128,16,128]{2,1,0:T(8,128)}), f32[128,16,128]{2,1,0:T(8,128)S(1)}, u32[]{:S(2)}, u32[]{:S(2)}) async-start(f32[128,16,128]{2,1,0:T(8,128)} %get-tuple-element.24), calls=%async_computation.1 | async-start | bytes 2097152 | tf_op jit(solution)/shard_map/all_to_all | solution.py:565
  150.5 107.3 %all-gather.6.cloned.1.call-start = ((), (), s32[]{:S(2)}) async-start(), calls=%async_computation.5 | async-start | bytes 2621440 | tf_op jit(solution)/shard_map/all_gather | solution.py:566
  169.8 1.0 copy-start.2
  172.8 17.8 %copy-start.8 = (f32[4096]{0:T(1024)S(1)}, f32[4096]{0:T(1024)}, u32[]{:S(2)}) copy-start(f32[4096]{0:T(1024)} %param.11) | copy-start | bytes 49156
  172.8 7.0 %collective-permute-start = (bf16[528,128]{1,0:T(8,128)(2,1)}, bf16[528,128]{1,0:T(8,128)(2,1)S(1)}, u32[]{:S(2)}, u32[]{:S(2)}) collective-permute-start(bf16[528,128]{1,0:T(8,128)(2,1)} %activate_slots.1.acts_ref.refs_0_), channel_id=1, source_target_pairs={{0,32},{32,64},{64,96},{96,0},{1,33},{33,65},{65,97},{97,1},{2,34}... | collective-permute-start | bytes 405512 | tf_op jit(solution)/shard_map/ppermute | solution.py:533
  173.2 6.9 %collective-permute-start.1 = (bf16[528,128]{1,0:T(8,128)(2,1)}, bf16[528,128]{1,0:T(8,128)(2,1)S(1)}, u32[]{:S(2)}, u32[]{:S(2)}) collective-permute-start(bf16[528,128]{1,0:T(8,128)(2,1)} %activate_slots.1.acts_ref.refs_0_), channel_id=1, source_target_pairs={{0,64},{32,96},{64,0},{96,32},{1,65},{33,97},{65,1},{97,33},{2,66}... | collective-permute-start | bytes 405512 | tf_op jit(solution)/shard_map/ppermute | solution.py:533
  175.5 5.9 %collective-permute-start.2 = (bf16[528,128]{1,0:T(8,128)(2,1)}, bf16[528,128]{1,0:T(8,128)(2,1)S(1)}, u32[]{:S(2)}, u32[]{:S(2)}) collective-permute-start(bf16[528,128]{1,0:T(8,128)(2,1)} %activate_slots.1.acts_ref.refs_0_), channel_id=1, source_target_pairs={{0,96},{32,0},{64,32},{96,64},{1,97},{33,1},{65,33},{97,65},{2,98}... | collective-permute-start | bytes 405512 | tf_op jit(solution)/shard_map/ppermute | solution.py:533
  179.8 11.4 %copy-start.10 = (bf16[528,128]{1,0:T(8,128)(2,1)}, bf16[528,128]{1,0:T(8,128)(2,1)S(1)}, u32[]{:S(2)}) copy-start(bf16[528,128]{1,0:T(8,128)(2,1)S(1)} %collective-permute-done.refs_1_) | copy-start | bytes 405508
  180.1 11.0 %copy-start.11 = (bf16[528,128]{1,0:T(8,128)(2,1)}, bf16[528,128]{1,0:T(8,128)(2,1)S(1)}, u32[]{:S(2)}) copy-start(bf16[528,128]{1,0:T(8,128)(2,1)S(1)} %collective-permute-done.1.refs_2_) | copy-start | bytes 405508
  181.4 9.8 %copy-start.12 = (bf16[528,128]{1,0:T(8,128)(2,1)}, bf16[528,128]{1,0:T(8,128)(2,1)S(1)}, u32[]{:S(2)}) copy-start(bf16[528,128]{1,0:T(8,128)(2,1)S(1)} %collective-permute-done.2.refs_3_) | copy-start | bytes 405508
  181.4 47.4 %all-to-all-start.3 = ((bf16[128,48,128]{2,1,0:T(8,128)(2,1)}), bf16[128,48,128]{2,1,0:T(8,128)(2,1)}, u32[]{:S(2)}, u32[]{:S(2)}) async-start(bf16[128,48,128]{2,1,0:T(8,128)(2,1)} %bitcast.17), calls=%async_computation.3 | async-start | bytes 3145728 | tf_op jit(solution)/shard_map/all_to_all | solution.py:571
  210.7 8.7 %collective-permute-start.3 = (bf16[512,128]{1,0:T(8,128)(2,1)}, bf16[512,128]{1,0:T(8,128)(2,1)S(1)}, u32[]{:S(2)}, u32[]{:S(2)}) collective-permute-start(bf16[512,128]{1,0:T(8,128)(2,1)} %get-tuple-element.30), channel_id=1, source_target_pairs={{0,96},{32,0},{64,32},{96,64},{1,97},{33,1},{65,33},{97,65},{2,98}... | collective-permute-start | bytes 393224 | tf_op jit(solution)/shard_map/ppermute | solution.py:533
  213.4 9.6 %collective-permute-start.4 = (bf16[512,128]{1,0:T(8,128)(2,1)}, bf16[512,128]{1,0:T(8,128)(2,1)S(1)}, u32[]{:S(2)}, u32[]{:S(2)}) collective-permute-start(bf16[512,128]{1,0:T(8,128)(2,1)} %get-tuple-element.31), channel_id=1, source_target_pairs={{0,64},{32,96},{64,0},{96,32},{1,65},{33,97},{65,1},{97,33},{2,66}... | collective-permute-start | bytes 393224 | tf_op jit(solution)/shard_map/ppermute | solution.py:533
  214.0 12.2 %collective-permute-start.5 = (bf16[512,128]{1,0:T(8,128)(2,1)}, bf16[512,128]{1,0:T(8,128)(2,1)S(1)}, u32[]{:S(2)}, u32[]{:S(2)}) collective-permute-start(bf16[512,128]{1,0:T(8,128)(2,1)} %get-tuple-element.32), channel_id=1, source_target_pairs={{0,32},{32,64},{64,96},{96,0},{1,33},{33,65},{65,97},{97,1},{2,34}... | collective-permute-start | bytes 393224 | tf_op jit(solution)/shard_map/ppermute | solution.py:533
  219.4 6.8 %copy-start.5 = (bf16[512,128]{1,0:T(8,128)(2,1)}, bf16[512,128]{1,0:T(8,128)(2,1)S(1)}, u32[]{:S(2)}) copy-start(bf16[512,128]{1,0:T(8,128)(2,1)S(1)} %collective-permute-done.3.refs_1_) | copy-start | bytes 393220
  223.0 3.2 %copy-start.6 = (bf16[512,128]{1,0:T(8,128)(2,1)}, bf16[512,128]{1,0:T(8,128)(2,1)S(1)}, u32[]{:S(2)}) copy-start(bf16[512,128]{1,0:T(8,128)(2,1)S(1)} %collective-permute-done.4.refs_2_) | copy-start | bytes 393220
  226.2 0.7 copy-start.7
  228.8 29.0 %all-to-all-start.2 = ((bf16[128,16,128]{2,1,0:T(8,128)(2,1)}), bf16[128,16,128]{2,1,0:T(8,128)(2,1)}, u32[]{:S(2)}, u32[]{:S(2)}) async-start(bf16[128,16,128]{2,1,0:T(8,128)(2,1)} %bitcast.19), calls=%async_computation.2 | async-start | bytes 1048576 | tf_op jit(solution)/shard_map/all_to_all | solution.py:578
  240.0 27.2 %collective-permute-start.6 = (bf16[256,1024]{1,0:T(8,128)(2,1)}, bf16[256,1024]{1,0:T(8,128)(2,1)S(1)}, u32[]{:S(2)}, u32[]{:S(2)}) collective-permute-start(bf16[256,1024]{1,0:T(8,128)(2,1)} %get-tuple-element.38), channel_id=1, source_target_pairs={{0,96},{32,0},{64,32},{96,64},{1,97},{33,1},{65,33},{97,65},{2,98}... | collective-permute-start | bytes 1572872 | tf_op jit(solution)/shard_map/ppermute | solution.py:533
  242.7 24.6 %collective-permute-start.7 = (bf16[256,1024]{1,0:T(8,128)(2,1)}, bf16[256,1024]{1,0:T(8,128)(2,1)S(1)}, u32[]{:S(2)}, u32[]{:S(2)}) collective-permute-start(bf16[256,1024]{1,0:T(8,128)(2,1)} %get-tuple-element.39), channel_id=1, source_target_pairs={{0,64},{32,96},{64,0},{96,32},{1,65},{33,97},{65,1},{97,33},{2,66}... | collective-permute-start | bytes 1572872 | tf_op jit(solution)/shard_map/ppermute | solution.py:533
  243.3 27.5 %collective-permute-start.8 = (bf16[256,1024]{1,0:T(8,128)(2,1)}, bf16[256,1024]{1,0:T(8,128)(2,1)}, u32[]{:S(2)}, u32[]{:S(2)}) collective-permute-start(bf16[256,1024]{1,0:T(8,128)(2,1)} %get-tuple-element.40), channel_id=1, source_target_pairs={{0,32},{32,64},{64,96},{96,0},{1,33},{33,65},{65,97},{97,1},{2,34}... | collective-permute-start | bytes 1572872 | tf_op jit(solution)/shard_map/ppermute | solution.py:533
  267.2 3.5 %copy-start.3 = (bf16[256,1024]{1,0:T(8,128)(2,1)}, bf16[256,1024]{1,0:T(8,128)(2,1)S(1)}, u32[]{:S(2)}) copy-start(bf16[256,1024]{1,0:T(8,128)(2,1)S(1)} %collective-permute-done.6.refs_1_) | copy-start | bytes 1572868
  267.3 3.5 %copy-start.4 = (bf16[256,1024]{1,0:T(8,128)(2,1)}, bf16[256,1024]{1,0:T(8,128)(2,1)S(1)}, u32[]{:S(2)}) copy-start(bf16[256,1024]{1,0:T(8,128)(2,1)S(1)} %collective-permute-done.7.refs_2_) | copy-start | bytes 1572868
Sparse Core Ops, SparseCore 0:
  10.3 179.3 all-gather.3
  191.3 41.5 all-gather.5

commit v9 on v8

--- a/solution.py
+++ b/solution.py
@@ -161,16 +161,37 @@
     )(arrived, weights, bias)
 
 
-def activate_kernel(ids_ref, pre_ref, group_ref):
+def info_kernel(blocks, ids_ref, info_ref):
+    ids = ids_ref[...]
+    rank = jnp.concatenate(ranks(ids, blocks), axis=0)
+    rows = [ids[:, :128], ids[:, 128:], rank[:, :128], rank[:, 128:], jnp.zeros((8, 128), jnp.int32)]
+    info_ref[...] = jnp.concatenate(rows, axis=0).astype(F32).astype(BF)
+
+
+def pair_info(ids, blocks):
+    return pl.pallas_call(
+        functools.partial(info_kernel, blocks),
+        out_shape=jax.ShapeDtypeStruct((16, 128), BF),
+        compiler_params=params(),
+        cost_estimate=cost(2e7, 2**16),
+        name="pair_info",
+    )(ids)
+
+
+def read_info(info):
+    rows = info.astype(F32).astype(jnp.int32)
+    ids = jnp.concatenate([rows[0:2], rows[2:4]], axis=1)
+    return ids, jnp.concatenate([rows[4:6], rows[6:8]], axis=1)
+
+
+def activate_kernel(info_ref, pre_ref, group_ref):
     packed = pre_ref.shape[1]
-    ids = ids_ref[...]
     total = pre_ref[0] + pre_ref[1] + pre_ref[2] + pre_ref[3]
     group_ref[:packed, :] = jnp.maximum(total, 0.0).astype(BF)
-    halves = [ids[:, :128], ids[:, 128:], jnp.zeros((12, 128), jnp.int32)]
-    group_ref[packed:, :] = jnp.concatenate(halves, axis=0).astype(F32).astype(BF)
-
-
-def activate(ids, partial):
+    group_ref[packed:, :] = info_ref[...]
+
+
+def activate(info, partial):
     parts, packed, lanes = partial.shape
     return pl.pallas_call(
         activate_kernel,
@@ -178,7 +199,7 @@
         compiler_params=params(),
         cost_estimate=cost(4 * packed * lanes, 2**20),
         name="activate_slots",
-    )(ids, partial)
+    )(info, partial)
 
 
 def message_kernel(ids_ref, acts_ref, msg_ref):
@@ -280,10 +301,9 @@
 
     slot = iota((slots, rows), 0)
     for d in range(parts):
-        halves = group[d][packed:, :].astype(F32).astype(jnp.int32)
-        ids = jnp.concatenate([halves[0:2], halves[2:4]], axis=1)
-        rank0, rank1 = ranks(ids, slots // CAP)
-        here = (slot == ids[0:1, :] * CAP + rank0) | (slot == ids[1:2, :] * CAP + rank1)
+        ids, rank = read_info(group[d][packed:, :])
+        place = ids * CAP + rank
+        here = (slot == place[0:1, :]) | (slot == place[1:2, :])
         pick_ref[d] = jnp.where(here, 1.0, 0.0).astype(BF)
 
     def aligned(start, size):
@@ -564,7 +584,7 @@
     pre, proj = encode(scale, arrived, weights, bias)
     partial = lax.all_to_all(pre, everyone, 0, 0, tiled=True)
     projs = lax.all_gather(proj, "dp", axis=0, tiled=False)
-    acts = activate(ids, partial.reshape(parts, shards * 2 * CAP, 128))
+    acts = activate(pair_info(ids, here * shards), partial.reshape(parts, shards * 2 * CAP, 128))
     msg = messages(ids, acts, parts, shards)
     group = [shifted(acts, d, parts) for d in range(parts)]
     msg, *group = lax.optimization_barrier((msg, *group))

time: 283 us -> 283 us (level)
  transfers between devices with their start and end apart: 15 -> 15, of which waited for: 8 -> 8; matrix products, arithmetic and copies ran while one was open for 2% -> 2% of each run, Pallas kernels for 22% -> 23%
where the time goes in v9:
time: 283 us; the launch traced here: 280 us
  waiting for transfers between devices  134 us (47%)
  Pallas kernels  67 us (24%)
  starting transfers between devices  55.7 us (20%)
  between operations  14.3 us (5%)
  local copies, waits for them, and re-layouts  7.03 us (2%)
    all_to_all x1, waiting for transfers between devices, body(): lax.all_to_all(outgoing.reshape(devices, here * CAP, cols), everyone, 0,...  99.1 us
    pallas_call x1, Pallas kernels, home(): pl.pallas_call(functools.partial(home_kernel, scale, parts), in_specs=[vm...  19.5 us
    all_to_all x1, waiting for transfers between devices, body(): partial = lax.all_to_all(pre, everyone, 0, 0, tiled=True)  17.1 us
    ppermute x9, waiting for transfers between devices, shifted(): lax.ppermute(value, 'dp', [(i, (i + by) % parts) for i in range(parts)])  16.8 us
    pallas_call x1, Pallas kernels, mix(): pl.pallas_call(mix_kernel, in_specs=[vmem, pl.BlockSpec(memory_space=pl.A...  14 us
    all_to_all x1, starting transfers between devices, body(): partial = lax.all_to_all(pre, everyone, 0, 0, tiled=True)  12.3 us
    all_to_all x1, starting transfers between devices, body(): lax.all_to_all(outgoing.reshape(devices, here * CAP, cols), everyone, 0,...  12 us
    all_to_all x1, starting transfers between devices, body(): lax.all_to_all(total.reshape(devices, 2 * CAP, 128), everyone, 0, 0, tile...  11.2 us
  transfers between devices with their start and end apart: 15, of which 8 were waited for; matrix products, arithmetic and copies ran while one was open for 2% of the time, Pallas kernels for 23%

profile of v9, /device:TPU:1, one launch (start us, length us, event | category | flops | bytes accessed | tf_op | source)
XLA Modules:
  0.0 280.5 jit_solution(9104592333450024894)
XLA Ops:
  7.2 0.0 copy-start
  7.2 0.0 all-gather.4.cloned.1.call-start
  7.2 1.5 copy-done
  8.8 0.9 constant_dynamic-slice_fusion.start_ref
  9.6 0.0 all-gather.4.cloned.1.call-update
  9.7 5.5 %route_rows.1 = bf16[4,1024,1024]{2,1,0:T(8,128)(2,1)} custom-call(s32[2,256]{1,0:T(2,128)} %bitcast.22, bf16[256,4096]{1,0:T(8,128)(2,1)} %resid_ref.1, f32[1,4096]{1,0:T(1,128)} %bitcast.21), custom_call_target="tpu_custom_call" | custom-call | flops 2147483648 | bytes 10485760 | tf_op jit(solution)/shard_map/route_rows/pallas_call | solution.py:107
  15.1 12.0 %all-to-all-start = ((bf16[128,32,1024]{2,1,0:T(8,128)(2,1)}), bf16[128,32,1024]{2,1,0:T(8,128)(2,1)}, u32[]{:S(2)}, u32[]{:S(2)}) async-start(bf16[128,32,1024]{2,1,0:T(8,128)(2,1)} %bitcast.15), calls=%async_computation | async-start | bytes 16777216 | tf_op jit(solution)/shard_map/all_to_all | solution.py:572
  27.1 0.3 copy.12
  27.4 0.0 copy-start.9
  27.4 1.1 constant_dynamic-slice_fusion.1
  28.5 1.0 copy.11
  29.5 2.1 maximum_bitcast_fusion.weight_ref
  31.6 0.6 select_bitcast_fusion.bias_ref
  32.2 99.1 %all-to-all-done.rows_hbm = bf16[128,32,1024]{2,1,0:T(8,128)(2,1)} async-done(((bf16[128,32,1024]{2,1,0:T(8,128)(2,1)}), bf16[128,32,1024]{2,1,0:T(8,128)(2,1)}, u32[]{:S(2)}, u32[]{:S(2)}) %all-to-all-start) | async-done | bytes 8388640 | tf_op jit(solution)/shard_map/all_to_all | solution.py:572
  131.3 6.9 %encode_rows.1 = (f32[128,16,128]{2,1,0:T(8,128)}, bf16[128,16,128]{2,1,0:T(8,128)(2,1)}) custom-call(bf16[128,32,1024]{2,1,0:T(8,128)(2,1)} %all-to-all-done.rows_hbm, bf16[2,1024,256]{2,1,0:T(8,128)(2,1)} %maximum_bitcast_fusion.weight_ref, f32[2,128]{1,0:T(2,128)} %select_bitcast_fusion.bias_ref), custom_call_target="tpu_custom_call" | custom-call | flops 2147483648 | bytes 11534336 | tf_op jit(solution)/shard_map/encode_rows/pallas_call | solution.py:152
  138.2 12.3 %all-to-all-start.1 = ((f32[128,16,128]{2,1,0:T(8,128)}), f32[128,16,128]{2,1,0:T(8,128)S(1)}, u32[]{:S(2)}, u32[]{:S(2)}) async-start(f32[128,16,128]{2,1,0:T(8,128)} %get-tuple-element.24), calls=%async_computation.1 | async-start | bytes 2097152 | tf_op jit(solution)/shard_map/all_to_all | solution.py:585
  150.5 0.0 all-gather.6.cloned.1.call-start
  150.5 0.7 all-gather.6.cloned.1.call-update
  151.2 1.5 pair_info.1.info_ref
  152.7 17.1 %all-to-all-done.1 = f32[128,16,128]{2,1,0:T(8,128)S(1)} async-done(((f32[128,16,128]{2,1,0:T(8,128)}), f32[128,16,128]{2,1,0:T(8,128)S(1)}, u32[]{:S(2)}, u32[]{:S(2)}) %all-to-all-start.1) | async-done | bytes 1048608 | tf_op jit(solution)/shard_map/all_to_all | solution.py:585
  169.8 1.0 copy-done.2
  170.8 2.0 activate_slots.1.acts_ref.refs_0_
  172.8 0.4 collective-permute-start
  173.2 2.3 collective-permute-start.1
  175.5 0.7 collective-permute-start.2
  176.2 3.5 %make_messages.1 = bf16[4,32,48,128]{3,2,1,0:T(8,128)(2,1)} custom-call(s32[2,256]{1,0:T(2,128)} %bitcast.24, bf16[528,128]{1,0:T(8,128)(2,1)} %activate_slots.1.acts_ref.refs_0_), custom_call_target="tpu_custom_call" | custom-call | flops 268435456 | bytes 2097152 | tf_op jit(solution)/shard_map/make_messages/pallas_call | solution.py:238
  179.7 0.4 collective-permute-done.1.refs_2_
  180.1 1.3 collective-permute-done.2.refs_3_
  181.4 9.1 %all-to-all-start.3 = ((bf16[128,48,128]{2,1,0:T(8,128)(2,1)}), bf16[128,48,128]{2,1,0:T(8,128)(2,1)}, u32[]{:S(2)}, u32[]{:S(2)}) async-start(bf16[128,48,128]{2,1,0:T(8,128)(2,1)} %bitcast.17), calls=%async_computation.3 | async-start | bytes 3145728 | tf_op jit(solution)/shard_map/all_to_all | solution.py:591
  190.6 0.6 reshape.47.refs_6_
  191.2 19.5 %home_rows.1 = (bf16[256,1024]{1,0:T(8,128)(2,1)}, bf16[256,1024]{1,0:T(8,128)(2,1)}, bf16[256,1024]{1,0:T(8,128)(2,1)}, bf16[256,1024]{1,0:T(8,128)(2,1)}, bf16...) custom-call(bf16[528,128]{1,0:T(8,128)(2,1)} %activate_slots.1.acts_ref.re, ...), custom_call_target="tpu_custom_call" | custom-call | flops 8589934592 | bytes 20971520 | tf_op jit(solution)/shard_map/home_rows/pallas_call | solution.py:346
  210.7 2.7 collective-permute-start.3
  213.4 0.6 collective-permute-start.4
  214.0 0.6 collective-permute-start.5
  214.5 4.8 %collective-permute-done.3.refs_1_ = bf16[512,128]{1,0:T(8,128)(2,1)S(1)} collective-permute-done((bf16[512,128]{1,0:T(8,128)(2,1)}, bf16[512,128]{1,0:T(8,128)(2,1)S(1)}, u32[]{:S(2)}, u32[]{:S(2)}) %collective-permute-start.3) | collective-permute-done | bytes 131104 | tf_op jit(solution)/shard_map/ppermute | solution.py:553
  219.4 3.6 %collective-permute-done.4.refs_2_ = bf16[512,128]{1,0:T(8,128)(2,1)S(1)} collective-permute-done((bf16[512,128]{1,0:T(8,128)(2,1)}, bf16[512,128]{1,0:T(8,128)(2,1)S(1)}, u32[]{:S(2)}, u32[]{:S(2)}) %collective-permute-start.4) | collective-permute-done | bytes 131104 | tf_op jit(solution)/shard_map/ppermute | solution.py:553
  223.0 3.2 %collective-permute-done.5.refs_3_ = bf16[512,128]{1,0:T(8,128)(2,1)S(1)} collective-permute-done((bf16[512,128]{1,0:T(8,128)(2,1)}, bf16[512,128]{1,0:T(8,128)(2,1)S(1)}, u32[]{:S(2)}, u32[]{:S(2)}) %collective-permute-start.5) | collective-permute-done | bytes 131104 | tf_op jit(solution)/shard_map/ppermute | solution.py:553
  226.2 0.6 copy-done.7
  226.9 2.0 sum_pieces.1
  228.8 11.2 %all-to-all-start.2 = ((bf16[128,16,128]{2,1,0:T(8,128)(2,1)}), bf16[128,16,128]{2,1,0:T(8,128)(2,1)}, u32[]{:S(2)}, u32[]{:S(2)}) async-start(bf16[128,16,128]{2,1,0:T(8,128)(2,1)} %bitcast.19), calls=%async_computation.2 | async-start | bytes 1048576 | tf_op jit(solution)/shard_map/all_to_all | solution.py:598
  240.0 2.7 collective-permute-start.6
  242.7 0.6 collective-permute-start.7
  243.3 0.6 collective-permute-start.8
  243.8 14.0 %mix_decoder.1.mixed_hbm = f32[256,1024]{1,0:T(8,128)} custom-call(bf16[128,48,128]{2,1,0:T(8,128)(2,1)} %all-to-all-done.3.msg_ref.msg_hbm, bf16[8192,1024]{1,0:T(8,128)(2,1)} %all-gather.4.cloned.1.call-done.refs_5_.dec_hbm, bf16[256,1024]{1,0:T(8,128)(2,1)} %constant_dynamic-slice_fusion.start_ref), custom_call_target="tpu_custom_call" | custom-call | flops 1 | bytes 1 | tf_op jit(solution)/shard_map/mix_decoder/pallas_call | solution.py:464
  257.8 0.0 all-gather.6.cloned.1.call-done
  257.9 9.4 %dictionary_grads.1 = (f32[256,1024]{1,0:T(8,128)}, f32[256,1024]{1,0:T(8,128)}) custom-call(bf16[128,16,128]{2,1,0:T(8,128)(2,1)} %all-to-all-done.2.gate_hbm, bf16[4,128,16,128]{3,2,1,0:T(8,128)(2,1)} %bitcast.25, bf16[128,48,128]{2,1,0:T(8,128)(2,1)} %all-to-all-done.3.msg_ref.msg_hbm, bf16[4096,1024]{1,0:T(8,128)(2,1)} %bitcast.12.rows_hbm, ...), custom_call_target="tpu_custom_call" | custom-call | flops 4294967296 | bytes 16777216 | tf_op jit(solution)/shard_map/dictionary_grads/pallas_call | solution.py:533
  267.3 3.4 %collective-permute-done.8.refs_3_ = bf16[256,1024]{1,0:T(8,128)(2,1)} collective-permute-done((bf16[256,1024]{1,0:T(8,128)(2,1)}, bf16[256,1024]{1,0:T(8,128)(2,1)}, u32[]{:S(2)}, u32[]{:S(2)}) %collective-permute-start.8) | collective-permute-done | bytes 524320 | tf_op jit(solution)/shard_map/ppermute | solution.py:553
  270.7 2.9 %assemble_recon.1 = bf16[256,4096]{1,0:T(8,128)(2,1)} custom-call(s32[1]{0:T(128)} %bitcast.refs_4_.at_ref, bf16[256,1024]{1,0:T(8,128)(2,1)} %get-tuple-element.37.refs_0_, bf16[256,1024]{1,0:T(8,128)(2,1)} %copy-done.3, bf16[256,1024]{1,0:T(8,128)(2,1)} %copy-done.4, bf16[256,1024]{1,0:T(8,128)(2,1)} %collective-permute-done.8.refs_3_), custom_call_target="tpu_custom_call" | custom-call | bytes 4194304 | tf_op jit(solution)/shard_map/assemble_recon/pallas_call | solution.py:380
  (27 shorter events, 0.1 us)
Async XLA Ops:
  7.2 1.6 copy-start
  7.2 184.0 %all-gather.4.cloned.1.call-start = ((), (), s32[]{:S(2)}) async-start(), calls=%async_computation.4 | async-start | bytes 17301504 | tf_op jit(solution)/shard_map/all_gather | solution.py:578
  15.1 12.0 %copy-start.1 = (bf16[256,1024]{1,0:T(8,128)(2,1)S(1)}, bf16[256,1024]{1,0:T(8,128)(2,1)}, u32[]{:S(2)}) copy-start(bf16[256,1024]{1,0:T(8,128)(2,1)} %constant_dynamic-slice_fusion.start_ref) | copy-start | bytes 1572868
  15.1 116.2 %all-to-all-start = ((bf16[128,32,1024]{2,1,0:T(8,128)(2,1)}), bf16[128,32,1024]{2,1,0:T(8,128)(2,1)}, u32[]{:S(2)}, u32[]{:S(2)}) async-start(bf16[128,32,1024]{2,1,0:T(8,128)(2,1)} %bitcast.15), calls=%async_computation | async-start | bytes 16777216 | tf_op jit(solution)/shard_map/all_to_all | solution.py:572
  27.4 4.2 %copy-start.9 = (f32[256]{0:T(256)S(1)}, f32[256]{0:T(256)}, u32[]{:S(2)}) copy-start(f32[256]{0:T(256)} %param.9) | copy-start | bytes 3076
  138.2 31.6 %all-to-all-start.1 = ((f32[128,16,128]{2,1,0:T(8,128)}), f32[128,16,128]{2,1,0:T(8,128)S(1)}, u32[]{:S(2)}, u32[]{:S(2)}) async-start(f32[128,16,128]{2,1,0:T(8,128)} %get-tuple-element.24), calls=%async_computation.1 | async-start | bytes 2097152 | tf_op jit(solution)/shard_map/all_to_all | solution.py:585
  150.5 107.4 %all-gather.6.cloned.1.call-start = ((), (), s32[]{:S(2)}) async-start(), calls=%async_computation.5 | async-start | bytes 2621440 | tf_op jit(solution)/shard_map/all_gather | solution.py:586
  169.8 1.0 copy-start.2
  172.8 17.8 %copy-start.8 = (f32[4096]{0:T(1024)S(1)}, f32[4096]{0:T(1024)}, u32[]{:S(2)}) copy-start(f32[4096]{0:T(1024)} %param.11) | copy-start | bytes 49156
  172.8 7.0 %collective-permute-start = (bf16[528,128]{1,0:T(8,128)(2,1)}, bf16[528,128]{1,0:T(8,128)(2,1)S(1)}, u32[]{:S(2)}, u32[]{:S(2)}) collective-permute-start(bf16[528,128]{1,0:T(8,128)(2,1)} %activate_slots.1.acts_ref.refs_0_), channel_id=1, source_target_pairs={{0,32},{32,64},{64,96},{96,0},{1,33},{33,65},{65,97},{97,1},{2,34}... | collective-permute-start | bytes 405512 | tf_op jit(solution)/shard_map/ppermute | solution.py:553
  173.2 6.9 %collective-permute-start.1 = (bf16[528,128]{1,0:T(8,128)(2,1)}, bf16[528,128]{1,0:T(8,128)(2,1)S(1)}, u32[]{:S(2)}, u32[]{:S(2)}) collective-permute-start(bf16[528,128]{1,0:T(8,128)(2,1)} %activate_slots.1.acts_ref.refs_0_), channel_id=1, source_target_pairs={{0,64},{32,96},{64,0},{96,32},{1,65},{33,97},{65,1},{97,33},{2,66}... | collective-permute-start | bytes 405512 | tf_op jit(solution)/shard_map/ppermute | solution.py:553
  175.5 5.9 %collective-permute-start.2 = (bf16[528,128]{1,0:T(8,128)(2,1)}, bf16[528,128]{1,0:T(8,128)(2,1)S(1)}, u32[]{:S(2)}, u32[]{:S(2)}) collective-permute-start(bf16[528,128]{1,0:T(8,128)(2,1)} %activate_slots.1.acts_ref.refs_0_), channel_id=1, source_target_pairs={{0,96},{32,0},{64,32},{96,64},{1,97},{33,1},{65,33},{97,65},{2,98}... | collective-permute-start | bytes 405512 | tf_op jit(solution)/shard_map/ppermute | solution.py:553
  179.7 11.4 %copy-start.10 = (bf16[528,128]{1,0:T(8,128)(2,1)}, bf16[528,128]{1,0:T(8,128)(2,1)S(1)}, u32[]{:S(2)}) copy-start(bf16[528,128]{1,0:T(8,128)(2,1)S(1)} %collective-permute-done.refs_1_) | copy-start | bytes 405508
  180.1 11.0 %copy-start.11 = (bf16[528,128]{1,0:T(8,128)(2,1)}, bf16[528,128]{1,0:T(8,128)(2,1)S(1)}, u32[]{:S(2)}) copy-start(bf16[528,128]{1,0:T(8,128)(2,1)S(1)} %collective-permute-done.1.refs_2_) | copy-start | bytes 405508
  181.4 9.8 %copy-start.12 = (bf16[528,128]{1,0:T(8,128)(2,1)}, bf16[528,128]{1,0:T(8,128)(2,1)S(1)}, u32[]{:S(2)}) copy-start(bf16[528,128]{1,0:T(8,128)(2,1)S(1)} %collective-permute-done.2.refs_3_) | copy-start | bytes 405508
  181.4 47.4 %all-to-all-start.3 = ((bf16[128,48,128]{2,1,0:T(8,128)(2,1)}), bf16[128,48,128]{2,1,0:T(8,128)(2,1)}, u32[]{:S(2)}, u32[]{:S(2)}) async-start(bf16[128,48,128]{2,1,0:T(8,128)(2,1)} %bitcast.17), calls=%async_computation.3 | async-start | bytes 3145728 | tf_op jit(solution)/shard_map/all_to_all | solution.py:591
  210.7 8.7 %collective-permute-start.3 = (bf16[512,128]{1,0:T(8,128)(2,1)}, bf16[512,128]{1,0:T(8,128)(2,1)S(1)}, u32[]{:S(2)}, u32[]{:S(2)}) collective-permute-start(bf16[512,128]{1,0:T(8,128)(2,1)} %get-tuple-element.30), channel_id=1, source_target_pairs={{0,96},{32,0},{64,32},{96,64},{1,97},{33,1},{65,33},{97,65},{2,98}... | collective-permute-start | bytes 393224 | tf_op jit(solution)/shard_map/ppermute | solution.py:553
  213.4 9.6 %collective-permute-start.4 = (bf16[512,128]{1,0:T(8,128)(2,1)}, bf16[512,128]{1,0:T(8,128)(2,1)S(1)}, u32[]{:S(2)}, u32[]{:S(2)}) collective-permute-start(bf16[512,128]{1,0:T(8,128)(2,1)} %get-tuple-element.31), channel_id=1, source_target_pairs={{0,64},{32,96},{64,0},{96,32},{1,65},{33,97},{65,1},{97,33},{2,66}... | collective-permute-start | bytes 393224 | tf_op jit(solution)/shard_map/ppermute | solution.py:553
  214.0 12.3 %collective-permute-start.5 = (bf16[512,128]{1,0:T(8,128)(2,1)}, bf16[512,128]{1,0:T(8,128)(2,1)S(1)}, u32[]{:S(2)}, u32[]{:S(2)}) collective-permute-start(bf16[512,128]{1,0:T(8,128)(2,1)} %get-tuple-element.32), channel_id=1, source_target_pairs={{0,32},{32,64},{64,96},{96,0},{1,33},{33,65},{65,97},{97,1},{2,34}... | collective-permute-start | bytes 393224 | tf_op jit(solution)/shard_map/ppermute | solution.py:553
  219.4 6.8 %copy-start.5 = (bf16[512,128]{1,0:T(8,128)(2,1)}, bf16[512,128]{1,0:T(8,128)(2,1)S(1)}, u32[]{:S(2)}) copy-start(bf16[512,128]{1,0:T(8,128)(2,1)S(1)} %collective-permute-done.3.refs_1_) | copy-start | bytes 393220
  223.0 3.2 %copy-start.6 = (bf16[512,128]{1,0:T(8,128)(2,1)}, bf16[512,128]{1,0:T(8,128)(2,1)S(1)}, u32[]{:S(2)}) copy-start(bf16[512,128]{1,0:T(8,128)(2,1)S(1)} %collective-permute-done.4.refs_2_) | copy-start | bytes 393220
  226.2 0.7 copy-start.7
  228.8 29.0 %all-to-all-start.2 = ((bf16[128,16,128]{2,1,0:T(8,128)(2,1)}), bf16[128,16,128]{2,1,0:T(8,128)(2,1)}, u32[]{:S(2)}, u32[]{:S(2)}) async-start(bf16[128,16,128]{2,1,0:T(8,128)(2,1)} %bitcast.19), calls=%async_computation.2 | async-start | bytes 1048576 | tf_op jit(solution)/shard_map/all_to_all | solution.py:598
  240.0 27.2 %collective-permute-start.6 = (bf16[256,1024]{1,0:T(8,128)(2,1)}, bf16[256,1024]{1,0:T(8,128)(2,1)S(1)}, u32[]{:S(2)}, u32[]{:S(2)}) collective-permute-start(bf16[256,1024]{1,0:T(8,128)(2,1)} %get-tuple-element.38), channel_id=1, source_target_pairs={{0,96},{32,0},{64,32},{96,64},{1,97},{33,1},{65,33},{97,65},{2,98}... | collective-permute-start | bytes 1572872 | tf_op jit(solution)/shard_map/ppermute | solution.py:553
  242.7 24.6 %collective-permute-start.7 = (bf16[256,1024]{1,0:T(8,128)(2,1)}, bf16[256,1024]{1,0:T(8,128)(2,1)S(1)}, u32[]{:S(2)}, u32[]{:S(2)}) collective-permute-start(bf16[256,1024]{1,0:T(8,128)(2,1)} %get-tuple-element.39), channel_id=1, source_target_pairs={{0,64},{32,96},{64,0},{96,32},{1,65},{33,97},{65,1},{97,33},{2,66}... | collective-permute-start | bytes 1572872 | tf_op jit(solution)/shard_map/ppermute | solution.py:553
  243.3 27.5 %collective-permute-start.8 = (bf16[256,1024]{1,0:T(8,128)(2,1)}, bf16[256,1024]{1,0:T(8,128)(2,1)}, u32[]{:S(2)}, u32[]{:S(2)}) collective-permute-start(bf16[256,1024]{1,0:T(8,128)(2,1)} %get-tuple-element.40), channel_id=1, source_target_pairs={{0,32},{32,64},{64,96},{96,0},{1,33},{33,65},{65,97},{97,1},{2,34}... | collective-permute-start | bytes 1572872 | tf_op jit(solution)/shard_map/ppermute | solution.py:553
  267.3 3.5 %copy-start.3 = (bf16[256,1024]{1,0:T(8,128)(2,1)}, bf16[256,1024]{1,0:T(8,128)(2,1)S(1)}, u32[]{:S(2)}) copy-start(bf16[256,1024]{1,0:T(8,128)(2,1)S(1)} %collective-permute-done.6.refs_1_) | copy-start | bytes 1572868
  267.3 3.5 %copy-start.4 = (bf16[256,1024]{1,0:T(8,128)(2,1)}, bf16[256,1024]{1,0:T(8,128)(2,1)S(1)}, u32[]{:S(2)}) copy-start(bf16[256,1024]{1,0:T(8,128)(2,1)S(1)} %collective-permute-done.7.refs_2_) | copy-start | bytes 1572868
Sparse Core Ops, SparseCore 0:
  10.3 179.3 all-gather.3
  191.3 41.5 all-gather.5
